TPU v7x, 32 devices: a whole 2x2x4 slice. The times are simulated.
32 devices in a mesh: dp: 4 (over z), row: 2 (over core), col: 4 (over y, x).
Axes of the slice: x: 2, y: 2, z: 4, core: 2. Of those that a mesh axis runs over, the one named last changes fastest.
Arguments:
- tokens: bfloat16 [12608, 768], P(('dp', 'row'), 'col'), may hold values from -6 to 6
- cotangent: bfloat16 [12608, 768], P(('dp', 'row'), 'col'), may hold values from -6 to 6
- routes: int32 [12608, 2], P('dp'), may hold values from 0 to 31, all different within a row; in each aligned block of 3152 rows (0 to 3151, 3152 to 6303, ...) at most 400 rows name the same one
- adapter_pick: int32 [64], replicated, may hold values from 0 to 7
- gain_attn: float32 [768], P('col'), may hold values from 0.5 to 1.5
- gain_moe: float32 [768], P('col'), may hold values from 0.5 to 1.5
- w_qkv: bfloat16 [3, 768, 768], P(None, 'col', 'row'), may hold values from -0.21875 to 0.21875
- w_out: bfloat16 [768, 768], P('row', 'col'), may hold values from -0.875 to 0.875
- w_router: bfloat16 [768, 32], replicated, may hold values from -0.15625 to 0.15625
- w_up: bfloat16 [32, 768, 3072], P(None, None, ('row', 'col')), may hold values from -0.21875 to 0.21875
- w_down: bfloat16 [32, 3072, 768], P(None, ('row', 'col')), may hold values from -1.75 to 1.75
- a_qkv: bfloat16 [3, 768, 128], P(None, 'col'), may hold values from -0.21875 to 0.21875
- b_qkv: bfloat16 [3, 128, 768], P(None, None, 'row'), may hold values from -0.75 to 0.75
- a_out: bfloat16 [768, 128], P('row'), may hold values from -0.875 to 0.875
- b_out: bfloat16 [128, 768], P(None, 'col'), may hold values from -0.75 to 0.75
- a_router: bfloat16 [768, 128], replicated, may hold values from -0.21875 to 0.21875
- b_router: bfloat16 [128, 32], replicated, may hold values from -0.5 to 0.5
- a_up: bfloat16 [768, 128], replicated, may hold values from -0.21875 to 0.21875
- b_up: bfloat16 [128, 3072], P(None, ('row', 'col')), may hold values from -0.75 to 0.75
- a_down: bfloat16 [3072, 128], P(('row', 'col')), may hold values from -0.109375 to 0.109375
- b_down: bfloat16 [128, 768], replicated, may hold values from -1.5 to 1.5
Outputs:
- block_out: bfloat16 [12608, 768], P(('dp', 'row'), 'col')
- grad_tokens: float32 [12608, 768], P(('dp', 'row'), 'col')
- grad_a_qkv: float32 [3, 768, 128], P(None, 'col')
- grad_b_qkv: float32 [3, 128, 768], P(None, None, 'row')
- grad_a_out: float32 [768, 128], P('row')
- grad_b_out: float32 [128, 768], P(None, 'col')
- grad_a_router: float32 [768, 128], replicated
- grad_b_router: float32 [128, 32], replicated
- grad_a_up: float32 [768, 128], replicated
- grad_b_up: float32 [128, 3072], P(None, ('row', 'col'))
- grad_a_down: float32 [3072, 128], P(('row', 'col'))
- grad_b_down: float32 [128, 768], replicated
Inputs may be any that keep to these rules, and one draw needn't show every extreme that they name: `routes`: each token names two different experts. In each aligned block of 3152 rows (the tokens of one index of dp) no expert is named by more than 400 rows, and in some block one expert is named by exactly 400 rows.
All inputs are finite; a program needn't handle non-finite values.
Results may differ from a plain program's by a relative error of at most 0.035.
Values may be sent and summed in bfloat16 or wider, within the bound.
No kernel may reach another device: no remote copies, remote signals or barrier semaphores. Data moves between devices by JAX's collectives and lax.ppermute only.
A program may use at most 448 MiB of HBM per device.

v0:
```python
import jax
import jax.numpy as jnp
from jax import lax
from jax.experimental import pallas as pl
from jax.experimental.pallas import tpu as pltpu
from jax.sharding import PartitionSpec as P

D = 768
EXPERTS = 32
SEQ = 197
SEQP = 208
RANK = 16
ADAPT = 128
IMG_GRP = 16
TOK = IMG_GRP * SEQP
BLK = 2 * SEQP
DUMMY = SEQ
TILE = 160
f32 = jnp.float32
bf16 = jnp.bfloat16


def max_tiles():
    return (2 * IMG_GRP * SEQ) // TILE + EXPERTS + 1


def dot(left, right):
    return jnp.dot(left, right, preferred_element_type=f32)


def dot_nt(left, right):
    return lax.dot_general(left, right, (((1,), (1,)), ((), ())), preferred_element_type=f32)


def dot_tn(left, right):
    return lax.dot_general(left, right, (((0,), (0,)), ((), ())), preferred_element_type=f32)


def lane_iota(shape):
    return lax.broadcasted_iota(jnp.int32, shape, len(shape) - 1)


def repeat_lanes(value):
    for shift in (16, 32, 64):
        value = value + pltpu.roll(value, shift, 1)
    return value


def table_kernel(n_blocks, picks_ref, *refs):
    x_blocks = refs[:n_blocks]
    c_blocks = refs[n_blocks : 2 * n_blocks]
    a_up, b_down, w_router, a_router, b_router, table_out, xin, cin, rows_x, rows_c, sem = refs[2 * n_blocks :]
    image = pl.program_id(0)
    lane = lane_iota((1, 128))

    @pl.when(image == 0)
    def start():
        copies = []
        for blocks, place in ((x_blocks, xin), (c_blocks, cin)):
            for b, block in enumerate(blocks):
                copies.append(pltpu.make_async_copy(block, place.at[pl.ds(b * BLK, BLK)], sem.at[len(copies)]))
        for copy in copies:
            copy.start()
        for copy in copies:
            copy.wait()

    row = pl.multiple_of(image * SEQP, 16)
    mask = (lane // RANK) == picks_ref[image]
    x = xin[pl.ds(row, SEQP), :]
    c = cin[pl.ds(row, SEQP), :]
    flat_x = rows_x.reshape(SEQP * 8, 128)
    flat_c = rows_c.reshape(SEQP * 8, 128)
    low_x = jnp.where(mask, dot(x, a_up[...]), 0.0)
    low_c = jnp.where(mask, dot_nt(c, b_down[...]), 0.0)
    low_r = jnp.where(mask, dot(x, a_router[...]), 0.0).astype(bf16)
    logits = dot(x, w_router[...]) + dot(low_r, b_router[...])
    logits = jnp.where(lane < 2 * EXPERTS, logits, -1e30)
    power = jnp.exp(logits - jnp.max(logits, axis=1, keepdims=True))
    total = jnp.sum(jnp.where(lane < EXPERTS, power, 0.0), axis=1, keepdims=True)
    probs = power / total
    lead = probs.astype(bf16).astype(f32)
    probs = jnp.where(lane < EXPERTS, lead, probs - lead)
    for j in range(6):
        flat_x[pl.ds(j, SEQP, 8), :] = x[:, 128 * j : 128 * j + 128].astype(f32)
        flat_c[pl.ds(j, SEQP, 8), :] = c[:, 128 * j : 128 * j + 128].astype(f32)
    flat_x[pl.ds(6, SEQP, 8), :] = low_x
    flat_x[pl.ds(7, SEQP, 8), :] = probs
    flat_c[pl.ds(6, SEQP, 8), :] = low_c
    flat_c[pl.ds(7, SEQP, 8), :] = jnp.zeros((SEQP, 128), f32)
    table_out[...] = jnp.concatenate([rows_x[...], rows_c[...]], axis=1).astype(bf16)


def table_call(picks, x_blocks, c_blocks, a_up, b_down, w_router, a_router, b_router):
    n = len(x_blocks)

    def whole(*shape):
        return pl.BlockSpec(shape, lambda e, *_: (0,) * len(shape))

    anywhere = pl.BlockSpec(memory_space=pl.ANY)
    return pl.pallas_call(
        lambda *refs: table_kernel(n, *refs),
        grid_spec=pltpu.PrefetchScalarGridSpec(
            num_scalar_prefetch=1,
            grid=(2 * n,),
            in_specs=[anywhere] * (2 * n)
            + [whole(D, ADAPT), whole(ADAPT, D), whole(D, 128), whole(D, ADAPT), whole(ADAPT, 128)],
            out_specs=pl.BlockSpec((SEQP, 16, 128), lambda i, *_: (i, 0, 0)),
            scratch_shapes=[
                pltpu.VMEM((n * BLK, D), bf16),
                pltpu.VMEM((n * BLK, D), bf16),
                pltpu.VMEM((SEQP, 8, 128), f32),
                pltpu.VMEM((SEQP, 8, 128), f32),
                pltpu.SemaphoreType.DMA((2 * n,)),
            ],
        ),
        out_shape=jax.ShapeDtypeStruct((n * BLK, 16, 128), bf16),
        compiler_params=pltpu.CompilerParams(vmem_limit_bytes=32 * 1024 * 1024),
        cost_estimate=pl.CostEstimate(flops=n * 3_000_000_000, bytes_accessed=n * 3_000_000, transcendentals=n * 60_000),
    )(picks, *x_blocks, *c_blocks, a_up, b_down, w_router, a_router, b_router)


def moe_kernel(places, list_ref, expert_ref, picks_ref, place_ref, *refs):
    n = len(places)
    tables = refs[:n]
    ep_outs, tg_outs = refs[n + 4 : n + 8], refs[n + 8 : n + 12]
    refs = refs[: n + 4] + refs[n + 12 :]
    (
        w_up_hbm, w_down_hbm, b_up, a_down,
        gbu_out, gad_out,
        table, acc_e, acc_t, in_x, in_c, out_e, out_t, xb, cb, w_up, w_down, stage_ep, stage_tg,
        in_sem, up_sem, down_sem, ep_sem, tg_sem,
    ) = refs[n:]
    acc_e_flat = acc_e.reshape(TOK * 8, 128)
    acc_t_flat = acc_t.reshape(TOK * 8, 128)
    in_x_flat = in_x.reshape(TILE * 8, 128)
    in_c_flat = in_c.reshape(TILE * 8, 128)
    out_e_flat = out_e.reshape(TILE * 8, 128)
    out_t_flat = out_t.reshape(TILE * 8, 128)
    lane = lane_iota((1, 128))
    n_tiles = expert_ref[max_tiles()]

    copies = []
    for piece, spots in zip(tables, places):
        for b, (t, s) in enumerate(spots):
            spot = 4 * t + jnp.where(place_ref[0] == t, swapped(s), s)
            copies.append(
                pltpu.make_async_copy(
                    piece.at[pl.ds(b * BLK, BLK)], table.at[pl.ds(pl.multiple_of(spot * BLK, 32), BLK)], in_sem.at[len(copies)]
                )
            )
    for copy in copies:
        copy.start()

    def weights(expert):
        slot = expert % 2
        return (
            pltpu.make_async_copy(w_up_hbm.at[expert], w_up.at[slot], up_sem.at[slot]),
            pltpu.make_async_copy(w_down_hbm.at[expert], w_down.at[slot], down_sem.at[slot]),
        )

    for copy in weights(0):
        copy.start()
    out_e[...] = jnp.zeros_like(out_e)
    out_t[...] = jnp.zeros_like(out_t)
    gbu_out[...] = jnp.zeros_like(gbu_out)
    gad_out[...] = jnp.zeros_like(gad_out)

    def clear(i, carry):
        acc_e[pl.ds(i * 64, 64)] = jnp.zeros((64, 8, 128), f32)
        acc_t[pl.ds(i * 64, 64)] = jnp.zeros((64, 8, 128), f32)
        return carry

    lax.fori_loop(0, TOK // 64, clear, 0)
    for copy in copies:
        copy.wait()

    def fetch(t):
        for i in range(TILE):
            both = table[list_ref[t * TILE + i]].astype(f32)
            in_x[i] = both[:8]
            in_c[i] = both[8:]

    def give(t):
        for b in range(TILE // 8):
            tokens = [list_ref[t * TILE + 8 * b + k] for k in range(8)]
            sums_e = [acc_e[tokens[k]] + out_e[8 * b + k] for k in range(8)]
            sums_t = [acc_t[tokens[k]] + out_t[8 * b + k] for k in range(8)]
            for k in range(8):
                acc_e[tokens[k]] = sums_e[k]
                acc_t[tokens[k]] = sums_t[k]

    fetch(0)

    def tile(t, carry):
        expert = expert_ref[t]
        slot = expert % 2

        @pl.when((t == 0) | (expert_ref[jnp.maximum(t - 1, 0)] != expert))
        def arrive():
            for copy in weights(expert):
                copy.wait()

            @pl.when(expert + 1 < EXPERTS)
            def ahead():
                for copy in weights(expert + 1):
                    copy.start()

        for j in range(7):
            xb[:, 128 * j : 128 * j + 128] = in_x_flat[pl.ds(j, TILE, 8), :].astype(bf16)
            cb[:, 128 * j : 128 * j + 128] = in_c_flat[pl.ds(j, TILE, 8), :].astype(bf16)
        spread = in_x_flat[pl.ds(7, TILE, 8), :]
        mine = (lane == expert) | (lane == expert + EXPERTS)
        gate = jnp.sum(jnp.where(mine, spread, 0.0), axis=1, keepdims=True)
        fetch(t + 1)
        give(jnp.maximum(t - 1, 0))
        hidden = dot(xb[:, :D], w_up[slot]) + dot(xb[:, D:], b_up[...])
        back = dot_nt(cb[:, :D], w_down[slot]) + dot_nt(cb[:, D:], a_down[...])
        cdf = 0.5 + 0.5 * lax.erf(hidden * 0.7071067811865476)
        slope = cdf + hidden * jnp.exp(hidden * hidden * -0.5) * 0.3989422804014327
        act = (hidden * cdf).astype(bf16)
        act_f = act.astype(f32)
        gate_grad = jnp.sum(act_f * back, axis=1, keepdims=True)
        grad_hidden = (gate * back * slope).astype(bf16)
        act_gate = (gate * act_f).astype(bf16)
        out_main = dot(act_gate, w_down[slot])
        out_low = dot(act_gate, a_down[...])
        in_main = dot_nt(grad_hidden, w_up[slot])
        in_low = dot_nt(grad_hidden, b_up[...])
        gbu_out[...] += dot_tn(grad_hidden, xb[:, D:])
        gad_out[...] += dot_tn(act_gate, cb[:, D:])
        for j in range(6):
            out_e_flat[pl.ds(j, TILE, 8), :] = out_main[:, 128 * j : 128 * j + 128]
            out_t_flat[pl.ds(j, TILE, 8), :] = in_main[:, 128 * j : 128 * j + 128]
        out_e_flat[pl.ds(6, TILE, 8), :] = out_low
        out_t_flat[pl.ds(6, TILE, 8), :] = in_low
        out_t_flat[pl.ds(7, TILE, 8), :] = jnp.where(lane == expert, gate_grad, 0.0)
        return carry

    lax.fori_loop(0, n_tiles, tile, 0)
    give(n_tiles - 1)

    some = IMG_GRP // 4
    for side, (ep_out, tg_out) in enumerate(zip(ep_outs, tg_outs)):

        def image(i, carry):
            slot = i % 2
            base = pl.multiple_of((i + side * some) * SEQP, 16) * 8
            mask = (lane // RANK) == picks_ref[i + side * some]
            rows = pl.ds(pl.multiple_of(i * SEQP, 16), SEQP)
            put_tg = pltpu.make_async_copy(stage_tg.at[slot], tg_out.at[rows], tg_sem.at[slot])
            put_ep = pltpu.make_async_copy(stage_ep.at[slot], ep_out.at[rows], ep_sem.at[slot])

            @pl.when(i >= 2)
            def drain():
                put_tg.wait()
                put_ep.wait()

            def chunk(j):
                flat = acc_e_flat if j < 8 else acc_t_flat
                return flat[pl.ds(base + j % 8, SEQP, 8), :]

            for j in range(6):
                at = slice(128 * j, 128 * j + 128)
                stage_tg[slot, :, at] = chunk(8 + j).astype(bf16)
                stage_ep[slot, :, at] = chunk(j).astype(bf16)
            low_in = repeat_lanes(jnp.where(mask, chunk(14), 0.0))
            low_out = repeat_lanes(jnp.where(mask, chunk(6), 0.0))
            last = jnp.where(lane < 48, low_in, jnp.where(lane < 64, low_out, 0.0))
            stage_tg[slot, :, D:] = jnp.where(lane < 32, chunk(15), last).astype(bf16)
            put_tg.start()
            put_ep.start()
            return carry

        lax.fori_loop(0, some, image, 0)
        for i in range(some - 2, some):
            rows = pl.ds(i * SEQP, SEQP)
            pltpu.make_async_copy(stage_tg.at[i % 2], tg_out.at[rows], tg_sem.at[i % 2]).wait()
            pltpu.make_async_copy(stage_ep.at[i % 2], ep_out.at[rows], ep_sem.at[i % 2]).wait()


def moe_call(token_list, tile_experts, picks, place, tables, places, w_up, w_down, b_up, a_down):
    half = w_up.shape[2]
    n = len(tables)
    n_copies = sum(len(spots) for spots in places)
    anywhere = pl.BlockSpec(memory_space=pl.ANY)
    inside = pl.BlockSpec(memory_space=pltpu.VMEM)
    return pl.pallas_call(
        lambda *refs: moe_kernel(places, *refs),
        grid_spec=pltpu.PrefetchScalarGridSpec(
            num_scalar_prefetch=4,
            grid=(1,),
            in_specs=[anywhere] * (n + 2) + [inside, inside],
            out_specs=[anywhere] * 8 + [inside, inside],
            scratch_shapes=[
                pltpu.VMEM((TOK, 16, 128), bf16),
                pltpu.VMEM((TOK, 8, 128), f32),
                pltpu.VMEM((TOK, 8, 128), f32),
                pltpu.VMEM((TILE, 8, 128), f32),
                pltpu.VMEM((TILE, 8, 128), f32),
                pltpu.VMEM((TILE, 8, 128), f32),
                pltpu.VMEM((TILE, 8, 128), f32),
                pltpu.VMEM((TILE, D + 128), bf16),
                pltpu.VMEM((TILE, D + 128), bf16),
                pltpu.VMEM((2, D, half), bf16),
                pltpu.VMEM((2, half, D), bf16),
                pltpu.VMEM((2, SEQP, D), bf16),
                pltpu.VMEM((2, SEQP, D + 128), bf16),
                pltpu.SemaphoreType.DMA((n_copies,)),
                pltpu.SemaphoreType.DMA((2,)),
                pltpu.SemaphoreType.DMA((2,)),
                pltpu.SemaphoreType.DMA((2,)),
                pltpu.SemaphoreType.DMA((2,)),
            ],
        ),
        out_shape=[
            *[jax.ShapeDtypeStruct((TOK // 4, D), bf16)] * 4,
            *[jax.ShapeDtypeStruct((TOK // 4, D + 128), bf16)] * 4,
            jax.ShapeDtypeStruct((half, ADAPT), f32),
            jax.ShapeDtypeStruct((half, ADAPT), f32),
        ],
        compiler_params=pltpu.CompilerParams(vmem_limit_bytes=58 * 1024 * 1024),
        cost_estimate=pl.CostEstimate(flops=20_000_000_000, bytes_accessed=60_000_000, transcendentals=10_000_000),
    )(token_list, tile_experts, picks, place, *tables, w_up, w_down, b_up, a_down)


def swapped(s):
    return ((s & 1) << 1) | (s >> 1)


def block_spot(block, row, col):
    from_row = block // 4
    s = (block % 4) ^ col
    return 4 * (from_row ^ row) + jnp.where(from_row == 0, swapped(s), s)


def routing(routes, row, col):
    token = jnp.arange(25 * 128, dtype=jnp.int32)[None, :]
    image = token // SEQ
    spot = block_spot(image // 2, row, col) * BLK + (image % 2) * SEQP + token % SEQ
    real = token < IMG_GRP * SEQ
    picked = jnp.pad(routes.T, ((0, 0), (0, 25 * 128 - IMG_GRP * SEQ)), constant_values=EXPERTS)
    beyond = EXPERTS * 4096 + DUMMY
    keys = jnp.where(real, picked * 4096 + spot, beyond).reshape(-1)
    experts = jnp.arange(EXPERTS, dtype=jnp.int32)
    count = jnp.sum((picked[None] == experts[:, None, None]).astype(jnp.int32), axis=(1, 2))
    tiles = (jnp.maximum(count, 1) + TILE - 1) // TILE
    extra = tiles * TILE - count
    filler = jnp.where(
        jnp.arange(256, dtype=jnp.int32)[None, :] < extra[:, None], (experts * 4096)[:, None] + DUMMY, beyond
    ).reshape(-1)
    ordered = lax.sort(jnp.concatenate([keys, filler])) & 4095
    ends = jnp.sum(jnp.where(experts[None, :] <= experts[:, None], tiles[None, :], 0), axis=1)
    steps = jnp.arange(max_tiles(), dtype=jnp.int32)
    owner = jnp.minimum(jnp.sum((ends[None, :] <= steps[:, None]).astype(jnp.int32), axis=1), EXPERTS - 1)
    return ordered, jnp.concatenate([owner, jnp.sum(tiles)[None]])


HEADS = 12
HEAD_DIM = 64


def pick_mask(pick):
    return (lane_iota((1, ADAPT)) // RANK) == pick


def norm_stats(values):
    centre = jnp.sum(values, axis=1, keepdims=True) * (1.0 / D)
    shifted = values - centre
    spread = jnp.sum(shifted * shifted, axis=1, keepdims=True) * (1.0 / D)
    inverse = lax.rsqrt(spread + 1e-06)
    return shifted * inverse, inverse


def norm_back(grad, gain, unit, inverse):
    scaled = grad * gain
    total = jnp.sum(scaled, axis=1, keepdims=True) * (1.0 / D)
    along = jnp.sum(scaled * unit, axis=1, keepdims=True) * (1.0 / D)
    return inverse * (scaled - total - unit * along)


def qkv_copies(place_ref, blocks, own_b, scratch, sem):
    w_qkv, a_qkv, b_qkv = scratch
    row, col = place_ref[0], place_ref[1]
    copies = []

    def copy(source, target):
        copies.append(pltpu.make_async_copy(source, target, sem.at[len(copies)]))

    for t in range(2):
        half_at = pl.multiple_of((row ^ t) * 384, 128)
        for s in range(4):
            block = blocks[4 * t + s]
            at = pl.multiple_of((col ^ s) * 192, 64)
            low_at = pl.multiple_of((col ^ s) * 192 + (row ^ t) * 96, 32)
            for p in range(3):
                copy(block.at[pl.ds(192 * p, 192)], w_qkv.at[p, pl.ds(at, 192), pl.ds(half_at, 384)])
                copy(block.at[pl.ds(576, 96), pl.ds(128 * p, 128)], a_qkv.at[p, pl.ds(low_at, 96), :])
        for p in range(3):
            source = own_b.at[p] if t == 0 else blocks[4].at[pl.ds(W_ROWS + 128 * p, 128)]
            copy(source, b_qkv.at[p, :, pl.ds(half_at, 384)])
    return copies


def out_copies(place_ref, far_block, own_a, out_w, scratch, sem):
    w_out, a_out = scratch
    row = place_ref[0]
    copies = []

    def copy(source, target):
        copies.append(pltpu.make_async_copy(source, target, sem.at[len(copies)]))

    for t in range(2):
        half_at = pl.multiple_of((row ^ t) * 384, 128)
        copy(out_w[t].at[pl.ds(0, 384)], w_out.at[pl.ds(half_at, 384), :])
        for j in range(3):
            if t == 0:
                source = own_a.at[pl.ds(128 * j, 128)]
            else:
                source = far_block.at[pl.ds(W_ROWS + 384, 128), pl.ds(128 * j, 128)]
            copy(source, a_out.at[pl.ds(half_at + 128 * j, 128), :])
    return copies


W_ROWS = 944
QKV_SCRATCH = [
    pltpu.VMEM((3, D, D), bf16),
    pltpu.VMEM((3, D, ADAPT), bf16),
    pltpu.VMEM((3, ADAPT, D), bf16),
    pltpu.SemaphoreType.DMA((54,)),
]
OUT_SCRATCH = [
    pltpu.VMEM((D, D), bf16),
    pltpu.VMEM((D, ADAPT), bf16),
    pltpu.SemaphoreType.DMA((8,)),
]


def split_kernel(place_ref, tokens_ref, cot_ref, own_out, one_out, two_out, three_out, left, right, stage, sem):
    rows = tokens_ref.shape[0]
    width = D // 4
    left[0:rows, 0:width] = tokens_ref[...].astype(f32)
    right[0:rows, 0:width] = cot_ref[...].astype(f32)
    lane = lane_iota((1, 128))
    real = lax.broadcasted_iota(jnp.int32, (SEQP, 1), 0) < SEQ
    for i in range(8):
        at = slice(SEQ * i, SEQ * i + SEQP)
        spot = slice(SEQP * (i % 2), SEQP * (i % 2) + SEQP)
        moved = pltpu.roll(right[at, :], 64, 1)
        middle = jnp.where(lane < 64, left[at, 128:256], moved[:, 0:128])
        stage[i // 2, spot, 0:128] = jnp.where(real, left[at, 0:128], 0.0).astype(bf16)
        stage[i // 2, spot, 128:256] = jnp.where(real, middle, 0.0).astype(bf16)
        stage[i // 2, spot, 256:384] = jnp.where(real, moved[:, 128:256], 0.0).astype(bf16)
    copies = [
        pltpu.make_async_copy(stage.at[place_ref[1] ^ s], out, sem.at[s])
        for s, out in enumerate((own_out, one_out, two_out, three_out))
    ]
    for copy in copies:
        copy.start()
    for copy in copies:
        copy.wait()


def split_call(place, tokens, cotangent):
    rows = tokens.shape[0]
    tall = -(-(SEQ * 7 + SEQP) // 8) * 8
    inside = pl.BlockSpec(memory_space=pltpu.VMEM)
    return pl.pallas_call(
        split_kernel,
        grid_spec=pltpu.PrefetchScalarGridSpec(
            num_scalar_prefetch=1,
            grid=(1,),
            in_specs=[inside, inside],
            out_specs=[ANYWHERE] * 4,
            scratch_shapes=[
                pltpu.VMEM((tall, 256), f32),
                pltpu.VMEM((tall, 256), f32),
                pltpu.VMEM((4, BLK, 384), bf16),
                pltpu.SemaphoreType.DMA((4,)),
            ],
        ),
        out_shape=[jax.ShapeDtypeStruct((BLK, 384), bf16)] * 4,
        compiler_params=pltpu.CompilerParams(vmem_limit_bytes=32 * 1024 * 1024),
        cost_estimate=pl.CostEstimate(flops=1_000_000_000, bytes_accessed=3_000_000, transcendentals=0),
    )(place, tokens, cotangent)


def merge_kernel(place_ref, *refs):
    blocks, refs = refs[:4], refs[4:]
    block_out, tokens_out, stage, tall, sem = refs
    copies = [
        pltpu.make_async_copy(block, stage.at[place_ref[1] ^ s], sem.at[s]) for s, block in enumerate(blocks)
    ]
    for copy in copies:
        copy.start()
    for copy in copies:
        copy.wait()
    width = D // 4
    rows = tokens_out.shape[0]
    for i in range(8):
        at = slice(SEQ * i, SEQ * i + SEQ)
        both = stage[i // 2, SEQP * (i % 2) : SEQP * (i % 2) + SEQP, :].astype(f32)[:SEQ]
        tokens_out[at, :] = both[:, :width]
        tall[at, :] = both[:, width:]
    block_out[...] = tall[0:rows, :].astype(bf16)


def merge_call(place, blocks, rows):
    width = D // 4
    inside = pl.BlockSpec(memory_space=pltpu.VMEM)
    return pl.pallas_call(
        merge_kernel,
        grid_spec=pltpu.PrefetchScalarGridSpec(
            num_scalar_prefetch=1,
            grid=(1,),
            in_specs=[ANYWHERE] * 4,
            out_specs=[inside, inside],
            scratch_shapes=[
                pltpu.VMEM((4, BLK, 2 * width), bf16),
                pltpu.VMEM((rows, width), f32),
                pltpu.SemaphoreType.DMA((4,)),
            ],
        ),
        out_shape=[jax.ShapeDtypeStruct((rows, width), bf16), jax.ShapeDtypeStruct((rows, width), f32)],
        compiler_params=pltpu.CompilerParams(vmem_limit_bytes=32 * 1024 * 1024),
        cost_estimate=pl.CostEstimate(flops=1_000_000_000, bytes_accessed=3_000_000, transcendentals=0),
    )(place, *blocks)


def place_weights(place_ref, blocks, own_b, own_a, out_w, w_qkv, a_qkv, b_qkv, w_out, a_out):
    row, col = place_ref[0], place_ref[1]
    for t in range(2):
        half_at = pl.multiple_of((row ^ t) * 384, 128)
        across = pl.ds(half_at, 384)
        for s in range(4):
            block = blocks[4 * t + s]
            at = pl.multiple_of((col ^ s) * 192, 64)
            low_at = pl.multiple_of((col ^ s) * 192 + (row ^ t) * 96, 32)
            for p in range(3):
                w_qkv[p, pl.ds(at, 192), across] = block[192 * p : 192 * p + 192, :]
                a_qkv[p, pl.ds(low_at, 96), :] = block[576:672, 128 * p : 128 * p + 128]
        w_out[across, :] = out_w[t][0:384, :]
        for p in range(3):
            down = pl.ds(pl.multiple_of(half_at + 128 * p, 128), 128)
            if t == 0:
                b_qkv[p, :, across] = own_b[p]
                a_out[down, :] = own_a[128 * p : 128 * p + 128, :]
            else:
                b_qkv[p, :, across] = blocks[4][W_ROWS + 128 * p : W_ROWS + 128 * p + 128, :]
                a_out[down, :] = blocks[4][W_ROWS + 384 : W_ROWS + 512, 128 * p : 128 * p + 128]


def attend_kernel(picks_ref, place_ref, *refs):
    blocks, refs = refs[:8], refs[8:]
    (
        own_b, own_a, out_near, out_far, x_ref, gain_one, gain_two, b_out,
        two_out, resid_out, normed_out, qkv_out, mixed_out, probs_out, lows_out,
        w_qkv, a_qkv, b_qkv, w_out, a_out,
    ) = refs
    image = pl.program_id(0)

    @pl.when(image == 0)
    def start():
        place_weights(place_ref, blocks, own_b, own_a, (out_near, out_far), w_qkv, a_qkv, b_qkv, w_out, a_out)

    mask = pick_mask(picks_ref[image])
    x = x_ref[...].astype(f32)
    unit, unused = norm_stats(x)
    normed = (unit * gain_one[...]).astype(bf16)
    normed_out[...] = normed
    for p in range(3):
        low = jnp.where(mask, dot(normed, a_qkv[p]), 0.0).astype(bf16)
        lows_out[:, 128 * p : 128 * p + 128] = low
        qkv_out[p] = (dot(normed, w_qkv[p]) + dot(low, b_qkv[p])).astype(bf16)
    lane = lane_iota((1, 128))
    key_lane = lane_iota((1, SEQP))
    for pair in range(HEADS // 2):
        at = slice(128 * pair, 128 * pair + 128)
        q = qkv_out[0, :, at]
        k = qkv_out[1, :, at]
        v = qkv_out[2, :, at]
        parts = []
        for side in range(2):
            own = (lane // HEAD_DIM) == side
            scores = dot_nt(jnp.where(own, q, jnp.zeros_like(q)), k) * (HEAD_DIM**-0.5)
            scores = jnp.where(key_lane < SEQ, scores, -1e30)
            power = jnp.exp(scores - jnp.max(scores, axis=1, keepdims=True))
            probs = (power / jnp.sum(power, axis=1, keepdims=True)).astype(bf16)
            probs_out[0, 2 * pair + side] = probs
            parts.append(dot(probs, v))
        mixed_out[:, at] = jnp.where(lane < HEAD_DIM, parts[0], parts[1]).astype(bf16)
    mixed = mixed_out[...]
    low = jnp.where(mask, dot(mixed, a_out[...]), 0.0).astype(bf16)
    lows_out[:, 384:512] = low
    resid = x + dot(mixed, w_out[...]) + dot(low, b_out[...])
    resid_out[...] = resid
    unit, unused = norm_stats(resid)
    real = lax.broadcasted_iota(jnp.int32, (SEQP, 1), 0) < SEQ
    two_out[...] = jnp.where(real, unit * gain_two[...], 0.0).astype(bf16)


def image_rows(lanes):
    return pl.BlockSpec((SEQP, lanes), lambda i, *_: (i, 0))


def kept(*shape):
    return pl.BlockSpec(shape, lambda i, *_: (0,) * len(shape))


QKV_SPEC = pl.BlockSpec((3, SEQP, D), lambda i, *_: (0, i, 0))
PROBS_SPEC = pl.BlockSpec((1, HEADS, SEQP, SEQP), lambda i, *_: (i, 0, 0, 0))
ANYWHERE = pl.BlockSpec(memory_space=pl.ANY)


def attend_call(picks, place, blocks, own_b, own_a, out_w, x, gain_one, gain_two, b_out):
    rows = x.shape[0]
    return pl.pallas_call(
        attend_kernel,
        grid_spec=pltpu.PrefetchScalarGridSpec(
            num_scalar_prefetch=2,
            grid=(2,),
            in_specs=[kept(*block.shape) for block in (*blocks, own_b, own_a, *out_w)]
            + [image_rows(D), kept(1, D), kept(1, D), kept(ADAPT, D)],
            out_specs=[
                image_rows(D), image_rows(D), image_rows(D), QKV_SPEC,
                image_rows(D), PROBS_SPEC, image_rows(512),
            ],
            scratch_shapes=QKV_SCRATCH[:-1] + OUT_SCRATCH[:-1],
        ),
        out_shape=[
            jax.ShapeDtypeStruct((rows, D), bf16),
            jax.ShapeDtypeStruct((rows, D), f32),
            jax.ShapeDtypeStruct((rows, D), bf16),
            jax.ShapeDtypeStruct((3, rows, D), bf16),
            jax.ShapeDtypeStruct((rows, D), bf16),
            jax.ShapeDtypeStruct((2, HEADS, SEQP, SEQP), bf16),
            jax.ShapeDtypeStruct((rows, 512), bf16),
        ],
        compiler_params=pltpu.CompilerParams(vmem_limit_bytes=60 * 1024 * 1024),
        cost_estimate=pl.CostEstimate(flops=4_000_000_000, bytes_accessed=15_000_000, transcendentals=2_000_000),
    )(picks, place, *blocks, own_b, own_a, *out_w, x, gain_one, gain_two, b_out)


def out_back_kernel(picks_ref, place_ref, *refs):
    (
        far_block, own_a, out_near, out_far, gain_two, b_out, two_ref, resid_ref, mixed_ref, lows_ref,
        cot_ref, grad_a, grad_b, w_router, a_router, b_router, a_up, b_down,
        resid_grad_out, mixed_grad_out, base_out, both_out, a_part_out, b_part_out,
        w_out, a_out, sem, both, a_part, b_part,
    ) = refs
    image = pl.program_id(0)

    @pl.when(image == 0)
    def start():
        copies = out_copies(place_ref, far_block, own_a, (out_near, out_far), (w_out, a_out), sem)
        for copy in copies:
            copy.start()
        for part in (both, a_part, b_part):
            part[...] = jnp.zeros_like(part)
        for copy in copies:
            copy.wait()

    mask = pick_mask(picks_ref[image])
    lane = lane_iota((1, 128))

    def add_part(row, value):
        at = slice(row, row + value.shape[0])
        both[at, :] += value

    two = two_ref[...]
    received = grad_a[...].astype(f32) + grad_b[...].astype(f32)
    low_r = jnp.where(mask, dot(two, a_router[...]), 0.0).astype(bf16)
    logits = dot(two, w_router[...]) + dot(low_r, b_router[...])
    logits = jnp.where(lane < EXPERTS, logits, -1e30)
    power = jnp.exp(logits - jnp.max(logits, axis=1, keepdims=True))
    probs = power / jnp.sum(power, axis=1, keepdims=True)
    last = received[:, D:]
    grad_probs = jnp.where(lane < EXPERTS, last, 0.0)
    low_in = jnp.where(mask, repeat_lanes(jnp.where((lane >= 32) & (lane < 48), last, 0.0)), 0.0).astype(bf16)
    low_out = jnp.where(mask, repeat_lanes(jnp.where((lane >= 48) & (lane < 64), last, 0.0)), 0.0).astype(bf16)
    cot = cot_ref[...]
    resid = resid_ref[...]
    base_out[...] = resid + dot(low_out, b_down[...])
    add_part(768, dot_tn(two, low_in))
    add_part(1536, dot_tn(cot, low_out))
    grad_logits = probs * (grad_probs - jnp.sum(probs * grad_probs, axis=1, keepdims=True))
    grad_logits = grad_logits.astype(bf16)
    grad_low = jnp.where(mask, dot_nt(grad_logits, b_router[...]), 0.0).astype(bf16)
    grad_two = received[:, :D] + dot_nt(low_in, a_up[...])
    grad_two = grad_two + dot_nt(grad_logits, w_router[...]) + dot_nt(grad_low, a_router[...])
    add_part(0, dot_tn(two, grad_low))
    add_part(2304, dot_tn(grad_logits, low_r))
    unit, inverse = norm_stats(resid)
    grad_resid = cot.astype(f32) + norm_back(grad_two, gain_two[...], unit, inverse)
    resid_grad_out[...] = grad_resid
    grad_attn = grad_resid.astype(bf16)
    grad_low = jnp.where(mask, dot_nt(grad_attn, b_out[...]), 0.0).astype(bf16)
    mixed_grad_out[...] = (dot_nt(grad_attn, w_out[...]) + dot_nt(grad_low, a_out[...])).astype(bf16)
    a_part[...] += dot_tn(mixed_ref[...], grad_low)
    b_part[...] += dot_tn(grad_attn, lows_ref[:, 384:512])

    @pl.when(image == 1)
    def finish():
        both_out[...] = both[...].astype(bf16)
        a_part_out[...] = a_part[...].astype(bf16)
        b_part_out[...] = b_part[...].astype(bf16)


BOTH_ROWS = 2560


def out_back_call(picks, place, far_block, own_a, out_w, gain_two, b_out, two, resid, mixed, lows, cot, grad_a, grad_b,
                  w_router, a_router, b_router, a_up, b_down):
    rows = two.shape[0]
    return pl.pallas_call(
        out_back_kernel,
        grid_spec=pltpu.PrefetchScalarGridSpec(
            num_scalar_prefetch=2,
            grid=(2,),
            in_specs=[ANYWHERE] * 4
            + [kept(1, D), kept(ADAPT, D), image_rows(D), image_rows(D), image_rows(D), image_rows(512)]
            + [image_rows(D), image_rows(D + 128), image_rows(D + 128)]
            + [kept(D, 128), kept(D, ADAPT), kept(ADAPT, 128), kept(D, ADAPT), kept(ADAPT, D)],
            out_specs=[image_rows(D), image_rows(D), image_rows(D), kept(BOTH_ROWS, 128), kept(D, 128), kept(D, 128)],
            scratch_shapes=OUT_SCRATCH
            + [pltpu.VMEM((BOTH_ROWS, 128), f32), pltpu.VMEM((D, 128), f32), pltpu.VMEM((D, 128), f32)],
        ),
        out_shape=[
            jax.ShapeDtypeStruct((rows, D), f32),
            jax.ShapeDtypeStruct((rows, D), bf16),
            jax.ShapeDtypeStruct((rows, D), f32),
            jax.ShapeDtypeStruct((BOTH_ROWS, 128), bf16),
            jax.ShapeDtypeStruct((D, 128), bf16),
            jax.ShapeDtypeStruct((D, 128), bf16),
        ],
        compiler_params=pltpu.CompilerParams(vmem_limit_bytes=60 * 1024 * 1024),
        cost_estimate=pl.CostEstimate(flops=6_000_000_000, bytes_accessed=15_000_000, transcendentals=100_000),
    )(picks, place, far_block, own_a, *out_w, gain_two, b_out, two, resid, mixed, lows, cot, grad_a, grad_b,
      w_router, a_router, b_router, a_up, b_down)


def qkv_back_kernel(picks_ref, place_ref, *refs):
    blocks, refs = refs[:8], refs[8:]
    (
        own_b, x_ref, gain_one, normed_ref, qkv_ref, probs_ref, lows_ref, resid_grad, grad_mixed,
        tokens_out, a_part_out, b_part_out,
        w_qkv, a_qkv, b_qkv, sem, a_part, b_part, grads,
    ) = refs
    image = pl.program_id(0)
    copies = qkv_copies(place_ref, blocks, own_b, (w_qkv, a_qkv, b_qkv), sem)

    @pl.when(image == 0)
    def start():
        for copy in copies:
            copy.start()
        a_part[...] = jnp.zeros_like(a_part)
        b_part[...] = jnp.zeros_like(b_part)

    mask = pick_mask(picks_ref[image])
    lane = lane_iota((1, 128))
    for pair in range(HEADS // 2):
        at = slice(128 * pair, 128 * pair + 128)
        q = qkv_ref[0, :, at]
        k = qkv_ref[1, :, at]
        v = qkv_ref[2, :, at]
        gm = grad_mixed[:, at]
        found = []
        for side in range(2):
            own = (lane // HEAD_DIM) == side
            weights = probs_ref[0, 2 * pair + side]
            weights_f = weights.astype(f32)
            grad_w = dot_nt(jnp.where(own, gm, jnp.zeros_like(gm)), v)
            inner = jnp.sum(weights_f * grad_w, axis=1, keepdims=True)
            grad_s = (weights_f * (grad_w - inner)).astype(bf16)
            found.append(
                (
                    dot(grad_s, k) * (HEAD_DIM**-0.5),
                    dot_tn(grad_s, q) * (HEAD_DIM**-0.5),
                    dot_tn(weights, gm),
                )
            )
        for p in range(3):
            grads[p, :, at] = jnp.where(lane < HEAD_DIM, found[0][p], found[1][p]).astype(bf16)

    @pl.when(image == 0)
    def arrived():
        for copy in copies:
            copy.wait()

    normed = normed_ref[...]
    grad_normed = jnp.zeros((SEQP, D), f32)
    for p in range(3):
        piece = grads[p]
        grad_low = jnp.where(mask, dot_nt(piece, b_qkv[p]), 0.0).astype(bf16)
        grad_normed = grad_normed + dot_nt(piece, w_qkv[p]) + dot_nt(grad_low, a_qkv[p])
        a_part[D * p : D * p + D, :] += dot_tn(normed, grad_low)
        b_part[D * p : D * p + D, :] += dot_tn(piece, lows_ref[:, 128 * p : 128 * p + 128])
    unit, inverse = norm_stats(x_ref[...].astype(f32))
    tokens_out[...] = (resid_grad[...] + norm_back(grad_normed, gain_one[...], unit, inverse)).astype(bf16)

    @pl.when(image == 1)
    def finish():
        a_part_out[...] = a_part[...].astype(bf16)
        b_part_out[...] = b_part[...].astype(bf16)


def qkv_back_call(picks, place, blocks, own_b, x, gain_one, normed, qkv, probs, lows, resid_grad, grad_mixed):
    rows = x.shape[0]
    return pl.pallas_call(
        qkv_back_kernel,
        grid_spec=pltpu.PrefetchScalarGridSpec(
            num_scalar_prefetch=2,
            grid=(2,),
            in_specs=[ANYWHERE] * (len(blocks) + 1)
            + [image_rows(D), kept(1, D), image_rows(D), QKV_SPEC, PROBS_SPEC, image_rows(512)]
            + [image_rows(D), image_rows(D)],
            out_specs=[image_rows(D), kept(3 * D, 128), kept(3 * D, 128)],
            scratch_shapes=QKV_SCRATCH
            + [
                pltpu.VMEM((3 * D, 128), f32),
                pltpu.VMEM((3 * D, 128), f32),
                pltpu.VMEM((3, SEQP, D), bf16),
            ],
        ),
        out_shape=[
            jax.ShapeDtypeStruct((rows, D), bf16),
            jax.ShapeDtypeStruct((3 * D, 128), bf16),
            jax.ShapeDtypeStruct((3 * D, 128), bf16),
        ],
        compiler_params=pltpu.CompilerParams(vmem_limit_bytes=60 * 1024 * 1024),
        cost_estimate=pl.CostEstimate(flops=9_000_000_000, bytes_accessed=15_000_000, transcendentals=1000),
    )(picks, place, *blocks, own_b, x, gain_one, normed, qkv, probs, lows, resid_grad, grad_mixed)


TABLES = (((0, 0), (1, 0)), ((0, 1), (0, 2), (1, 1), (1, 2)), ((0, 3), (1, 3)))


def across_row(value):
    return lax.ppermute(value, "row", [(0, 1), (1, 0)])


def across_col(value, step):
    return lax.ppermute(value, "col", [(i, i ^ step) for i in range(4)])


def by_place(blocks, col):
    found = []
    for place in range(4):
        value = blocks[place]
        for other in range(1, 4):
            value = jnp.where(col == other, blocks[place ^ other], value)
        found.append(value)
    return found


def across_chip(value, first, second):
    pairs = [(i, i ^ first) for i in range(4)] + [(4 + i, 4 + (i ^ second)) for i in range(4)]
    return lax.ppermute(value, ("row", "col"), pairs)


def gather_col(value, row):
    from_x = across_col(value, 1)
    from_y = across_col(value, 2)
    return [value, from_x, from_y, across_chip(jnp.where(row == 0, from_x, from_y), 2, 1)]


def added(*values):
    total = values[0].astype(f32)
    for value in values[1:]:
        total = total + value.astype(f32)
    return total


def last_exchange(kept_rows, got):
    sent = added(kept_rows[BLK:], got[BLK:]).astype(bf16)
    return added(kept_rows[:BLK], got[:BLK]).astype(bf16), across_chip(sent, 2, 1)


def at_place(value, axis, place):
    return lax.dynamic_index_in_dim(value, place, axis, keepdims=False)


def scatter_dp(value):
    place = lax.axis_index("dp")
    view = value.reshape(4, -1, 128)
    found = [at_place(view, 0, place)]
    for s in range(1, 4):
        found.append(across_dp(at_place(view, 0, place ^ s), s))
    return added(*found).astype(bf16)


def across_dp(value, step):
    return lax.ppermute(value, "dp", [(i, i ^ step) for i in range(4)])


def spread_dp(value):
    return jnp.concatenate(by_place([value] + [across_dp(value, s) for s in range(1, 4)], lax.axis_index("dp")))


def part_share(col_parts, row_parts, both_parts, place):
    col_parts = at_place(col_parts.reshape(4, 4, 2, 96, 128), 2, place)
    row_parts = at_place(row_parts.reshape(4, 2, 4, 96, 128), 1, place)
    both_parts = at_place(both_parts.reshape(2, 4, BOTH_ROWS // 8, 128), 0, place)
    col_parts = col_parts.swapaxes(0, 1).reshape(4, 384, 128)
    row_parts = row_parts.swapaxes(0, 1).reshape(4, 384, 128)
    return jnp.concatenate([col_parts, row_parts, both_parts], axis=1)


def reduce_col(value, col):
    found = [at_place(value, 0, col)]
    for s in range(1, 4):
        found.append(across_col(at_place(value, 0, col ^ s), s))
    return added(*found).astype(bf16)


def spread_parts(mine, row, col):
    spread = by_place([mine[384:]] + [across_col(mine[384:], s) for s in range(1, 4)], col)
    row_sums = jnp.stack([one[:384].reshape(4, 96, 128) for one in spread], axis=1).reshape(4, 384, 128)
    near = jnp.concatenate([mine[:384]] + [one[384:] for one in spread])
    far = across_row(near)
    first = jnp.where(row == 0, near, far)
    second = jnp.where(row == 0, far, near)
    col_sums = jnp.stack([first[:384].reshape(4, 96, 128), second[:384].reshape(4, 96, 128)], axis=1).reshape(4, 192, 128)
    both_sums = jnp.concatenate([first[384:], second[384:]])
    return col_sums, row_sums, both_sums


def to_features(first, second, col):
    width = D // 4
    pieces = []
    for p in range(4):
        at = slice(width * p, width * p + width)
        pieces.append(jnp.concatenate([first[:, at], second[:, at]], axis=1))
    sent = by_place(pieces, col)
    return [sent[0]] + [across_col(sent[s], s) for s in range(1, 4)]


def on_device(
    tokens, cotangent, routes, adapter_pick, gain_attn, gain_moe, w_qkv, w_out, w_router, w_up, w_down,
    a_qkv, b_qkv, a_out, b_out, a_router, b_router, a_up, b_up, a_down, b_down,
):
    row = lax.axis_index("row")
    col = lax.axis_index("col")
    me = row * 4 + col
    place = jnp.stack([row, col]).astype(jnp.int32)

    width = D // 4
    half = D // 2
    gains = []
    for gain in (gain_attn, gain_moe):
        left = gain
        for unused in range(3):
            lead = lax.reduce_precision(left, 8, 7)
            gains.append(lead.astype(bf16))
            left = left - lead
    small = jnp.concatenate([w_out, b_out, jnp.stack(gains), jnp.zeros((26, width), bf16)], axis=0)
    low = at_place(a_qkv.reshape(3, 2, 96, ADAPT), 1, row)
    packed = jnp.concatenate(
        [w_qkv.reshape(576, half), jnp.concatenate([low[0], low[1], low[2]], axis=1),
         jnp.concatenate([small[:272], small[272:]], axis=1)]
    )
    for_row = jnp.concatenate(
        [packed, b_qkv.reshape(half, half), jnp.concatenate([a_out[:128], a_out[128:256], a_out[256:]], axis=1)]
    )
    pairs = split_call(place, tokens, cotangent)
    from_x, from_y = across_col(packed, 1), across_col(packed, 2)
    from_x, from_y, *pairs = lax.optimization_barrier((from_x, from_y, *pairs))
    near = [packed, from_x, from_y, across_chip(jnp.where(row == 0, from_x, from_y), 2, 1)]
    pairs = by_place([pairs[0]] + [across_col(pairs[s], s) for s in range(1, 4)], col)
    x = jnp.concatenate([pair[:, :width] for pair in pairs], axis=1)
    cot = jnp.concatenate([pair[:, width:] for pair in pairs], axis=1)
    far = [across_row(for_row)] + [across_row(block) for block in near[1:]]
    blocks = near + far

    def assembled(group):
        parts = by_place([block[672:944] for block in group], col)
        return jnp.concatenate(
            [jnp.concatenate([part[:, :width] for part in parts], axis=1),
             jnp.concatenate([part[:, width:] for part in parts], axis=1)], axis=0
        )

    out_w = [assembled(near), assembled(far)]
    full_b_out = out_w[0][384:512]
    gain_rows = out_w[0][512:518].astype(f32)
    gain_one = jnp.sum(gain_rows[:3], axis=0, keepdims=True)
    gain_two = jnp.sum(gain_rows[3:], axis=0, keepdims=True)

    picks_group = lax.dynamic_slice_in_dim(adapter_pick, lax.axis_index("dp") * IMG_GRP, IMG_GRP)
    order = jnp.arange(IMG_GRP, dtype=jnp.int32)
    picks = jnp.take(picks_group, ((order // 2) ^ me) * 2 + order % 2)
    spot_picks = jnp.sum(
        jnp.where(block_spot(order // 2, row, col)[None, :] * 2 + order[None, :] % 2 == order[:, None], picks_group[None, :], 0), axis=1
    )
    token_list, tile_experts = routing(routes, row, col)
    wide_router = jnp.concatenate([w_router, w_router, jnp.zeros((D, 64), bf16)], axis=1)
    wide_b_router = jnp.concatenate([b_router, b_router, jnp.zeros((ADAPT, 64), bf16)], axis=1)
    slim_router = jnp.concatenate([w_router, jnp.zeros((D, 96), bf16)], axis=1)
    slim_b_router = jnp.concatenate([b_router, jnp.zeros((ADAPT, 96), bf16)], axis=1)

    x, token_list, tile_experts = lax.optimization_barrier((x, token_list, tile_experts))
    cot, unused = lax.optimization_barrier((cot, far[3]))
    two, resid, normed, qkv, mixed, probs, lows = attend_call(
        picks, place, blocks, b_qkv, a_out, out_w, x, gain_one, gain_two, full_b_out
    )
    cot_near = gather_col(cot, row)
    two_x, two_y = across_col(two, 1), across_col(two, 2)

    def table(spots, twos, cots):
        return table_call(
            jnp.stack([picks[8 * t + 2 * s + side] for t, s in spots for side in range(2)]),
            twos, cots, a_up, b_down, wide_router, a_router, wide_b_router,
        )

    cot_far = [across_row(block) for block in cot_near]
    tables = [table(TABLES[0], [two, across_row(two)], [cot, cot_far[0]])]
    two_x, two_y, tables[0] = lax.optimization_barrier((two_x, two_y, tables[0]))
    diag = across_chip(jnp.where(row == 0, two_x, two_y), 2, 1)
    tables.append(
        table(TABLES[1], [two_x, two_y, across_row(two_x), across_row(two_y)], [cot_near[1], cot_near[2], cot_far[1], cot_far[2]])
    )
    diag, *tables = lax.optimization_barrier((diag, *tables))
    tables.append(table(TABLES[2], [diag, across_row(diag)], [cot_near[3], cot_far[3]]))
    *moved, part_b_up, part_a_down = moe_call(
        token_list, tile_experts, spot_picks, place, tables, TABLES, w_up, w_down, b_up, a_down
    )
    sums, grads = moved[:4], moved[4:]
    dp_parts = jnp.concatenate([part_b_up.astype(bf16), part_a_down.astype(bf16)])
    grad_sent = added(grads[1], across_row(grads[3])).astype(bf16)
    grad_kept = added(grads[0], across_row(grads[2])).astype(bf16)
    grad_sent, dp_parts, *sums = lax.optimization_barrier((grad_sent, dp_parts, *sums))
    grad_got = across_chip(grad_sent, 1, 2)
    sum_kept, sum_sent = across_row(sums[2]), across_row(sums[3])
    sums = [
        added(near[at : at + BLK], far[at : at + BLK]).astype(bf16)
        for near, far in ((sums[0], sum_kept), (sums[1], sum_sent)) for at in (0, BLK)
    ]
    four_dp = lax.axis_size("dp") == 4
    dp_sums = scatter_dp(dp_parts) if four_dp else lax.psum(dp_parts, "dp")
    grad_got, dp_sums, *sums = lax.optimization_barrier((grad_got, dp_sums, *sums))
    grad_a, grad_b = last_exchange(grad_kept, grad_got)
    if four_dp:
        dp_sums = spread_dp(dp_sums)
    grad_a, grad_b, dp_sums, *sums = lax.optimization_barrier((grad_a, grad_b, dp_sums, *sums))
    sums = [sums[0], across_chip(sums[1], 2, 1), across_chip(sums[2], 1, 2), across_chip(sums[3], 3, 3)]
    resid_grad, mixed_grad, base, both_parts, part_a_out, part_b_out = out_back_call(
        picks, place, blocks[4], a_out, out_w, gain_two, full_b_out, two, resid, mixed, lows, cot, grad_a, grad_b,
        slim_router, a_router, slim_b_router, a_up, b_down,
    )
    grad_tokens, part_a_qkv, part_b_qkv = qkv_back_call(
        picks, place, blocks, b_qkv, x, gain_one, normed, qkv, probs, lows, resid_grad, mixed_grad
    )
    part_a_qkv, part_b_qkv, *sums = lax.optimization_barrier((part_a_qkv, part_b_qkv, *sums))
    col_parts = jnp.concatenate([part_a_qkv, part_b_out])
    row_parts = jnp.concatenate([part_b_qkv, part_a_out])
    theirs = across_row(part_share(col_parts, row_parts, both_parts, 1 - row))
    shared = added(part_share(col_parts, row_parts, both_parts, row), theirs).astype(bf16)
    mine = reduce_col(shared, col)
    mine, grad_tokens, base = lax.optimization_barrier((mine, grad_tokens, base))
    moves = to_features(grad_tokens, (base + added(*sums)).astype(bf16), col)
    mine = spread_dp(scatter_dp(mine)) if four_dp else lax.psum(mine, "dp")
    block_out, grad_tokens = merge_call(place, moves, tokens.shape[0])
    col_sums, row_sums, both_sums = spread_parts(mine, row, col)
    col_sums = col_sums.astype(f32)
    row_sums = row_sums.astype(f32)
    both_sums = both_sums.astype(f32)
    dp_sums = dp_sums.astype(f32)
    return (
        block_out,
        grad_tokens,
        col_sums[:3],
        jnp.swapaxes(row_sums[:3], 1, 2),
        row_sums[3],
        col_sums[3].T,
        both_sums[:768],
        both_sums[2304:2336].T,
        both_sums[768:1536],
        dp_sums[:384].T,
        dp_sums[384:],
        both_sums[1536:2304].T,
    )


def solution(mesh):
    return jax.shard_map(
        on_device,
        mesh=mesh,
        in_specs=(
            P(("dp", "row"), "col"),
            P(("dp", "row"), "col"),
            P("dp", None),
            P(),
            P("col"),
            P("col"),
            P(None, "col", "row"),
            P("row", "col"),
            P(),
            P(None, None, ("row", "col")),
            P(None, ("row", "col"), None),
            P(None, "col", None),
            P(None, None, "row"),
            P("row", None),
            P(None, "col"),
            P(),
            P(),
            P(),
            P(None, ("row", "col")),
            P(("row", "col"), None),
            P(),
        ),
        out_specs=(
            P(("dp", "row"), "col"),
            P(("dp", "row"), "col"),
            P(None, "col", None),
            P(None, None, "row"),
            P("row", None),
            P(None, "col"),
            P(),
            P(),
            P(),
            P(None, ("row", "col")),
            P(("row", "col"), None),
            P(),
        ),
        check_vma=False,
    )
```

profile of v0, /device:TPU:0, one launch (start us, length us, event | category | flops | bytes accessed | tf_op | source)
XLA Modules:
  0.0 395.8 jit_solution(16721328428799715830)
XLA Ops:
  5.5 2.9 collective-permute-start
  17.6 7.8 %sort.14 = (s32[14592]{0:T(1024)S(1)}, s32[14592]{0:T(1024)}) sort(s32[14592]{0:T(1024)S(1)} %pad_add_fusion, s32[14592]{0:T(1024)S(1)} %iota.71), dimensions={0}, to_apply=%region_1.2 | sort | flops 204288 | bytes 233472 | tf_op jit(solution)/shard_map/sort | solution.py:351
  33.0 4.9 %collective-permute-done.7 = bf16[416,384]{1,0:T(8,128)(2,1)S(1)} collective-permute-done((bf16[416,384]{1,0:T(8,128)(2,1)S(1)}, bf16[416,384]{1,0:T(8,128)(2,1)S(1)}, u32[]{:S(2)}, u32[]{:S(2)}) %collective-permute-start.7) | collective-permute-done | bytes 319520 | tf_op jit(solution)/shard_map/ppermute | solution.py:842
  39.4 3.1 collective-permute-done.8
  46.8 3.5 collective-permute-done.2.refs_3_
  62.1 15.7 %shard_map.293 = (bf16[416,768]{1,0:T(8,128)(2,1)}, f32[416,768]{1,0:T(8,128)}, bf16[416,768]{1,0:T(8,128)(2,1)}, bf16[3,416,768]{2,1,0:T(8,128)(2,1)}, bf16[416...) custom-call(s32[16]{0:T(128)} %and_select_fusion.5.picks_ref, s32[2]{0:T(128)} %copy-done.7, ...), custom_call_target="tpu_custom_call" | custom-call | flops 4000000000 | bytes 15000000 | tf_op jit(solution)/shard_map/pallas_call | solution.py:616
  84.8 5.6 %shard_map.294.refs_4_ = bf16[832,16,128]{2,1,0:T(8,128)(2,1)S(1)} custom-call(s32[4]{0:T(128)S(1)} %pad_add_fusion.3.refs_0_, bf16[416,768]{1,0:T(8,128)(2,1)S(1)} %copy-done.1, bf16[416,768]{1,0:T(8,128)(2,1)} %collective-permute-done.12.refs_2_, bf16[416,768]{1,0:T(8,128)(2,1)S(1)} %pad_maximum_fusion.4.refs_3_.refs_10_, ...), custom_call_target="tpu_custom_call" | custom-call | flops 6000000000 | bytes 6000000 | tf_op jit(solution)/shard_map/pallas_call | solution.py:100
  92.2 6.4 %collective-permute-done.10.refs_1_ = bf16[416,768]{1,0:T(8,128)(2,1)S(1)} collective-permute-done((bf16[416,768]{1,0:T(8,128)(2,1)}, bf16[416,768]{1,0:T(8,128)(2,1)S(1)}, u32[]{:S(2)}, u32[]{:S(2)}) %collective-permute-start.10) | collective-permute-done | bytes 639008 | tf_op jit(solution)/shard_map/ppermute | solution.py:842
  99.3 6.1 %collective-permute-done.22.refs_3_ = bf16[416,768]{1,0:T(8,128)(2,1)S(1)} collective-permute-done((bf16[416,768]{1,0:T(8,128)(2,1)S(1)}, bf16[416,768]{1,0:T(8,128)(2,1)S(1)}, u32[]{:S(2)}, u32[]{:S(2)}) %collective-permute-start.22) | collective-permute-done | bytes 639008 | tf_op jit(solution)/shard_map/ppermute | solution.py:857
  106.6 9.7 %shard_map.295.refs_5_ = bf16[1664,16,128]{2,1,0:T(8,128)(2,1)S(1)} custom-call(s32[8]{0:T(128)S(1)} %pad_add_fusion.4.refs_0_, bf16[416,768]{1,0:T(8,128)(2,1)S(1)} %collective-permute-done.10.refs_1_, bf16[416,768]{1,0:T(8,128)(2,1)S(1)} %collective-permute-done.11.refs_2_, bf16[416,768]{1,0:T(8,128)(2,1)S(1)} %collective-permute-done.15.refs_3_, ...), custom_call_target="tpu_custom_call" | custom-call | flops 12000000000 | bytes 12000000 | tf_op jit(solution)/shard_map/pallas_call | solution.py:100
  116.3 2.8 copy-done.11
  121.3 5.1 %shard_map.296.refs_6_ = bf16[832,16,128]{2,1,0:T(8,128)(2,1)S(1)} custom-call(s32[4]{0:T(128)S(1)} %pad_add_fusion.5.refs_0_, bf16[416,768]{1,0:T(8,128)(2,1)S(1)} %collective-permute-done.14.refs_1_, bf16[416,768]{1,0:T(8,128)(2,1)S(1)} %collective-permute-done.21.refs_2_, bf16[416,768]{1,0:T(8,128)(2,1)S(1)} %collective-permute-done.22.refs_3_, ...), custom_call_target="tpu_custom_call" | custom-call | flops 6000000000 | bytes 6000000 | tf_op jit(solution)/shard_map/pallas_call | solution.py:100
  128.2 105.6 %shard_map.297 = (bf16[832,768]{1,0:T(8,128)(2,1)}, bf16[832,768]{1,0:T(8,128)(2,1)}, bf16[832,768]{1,0:T(8,128)(2,1)}, bf16[832,768]{1,0:T(8,128)(2,1)}, bf16[8...) custom-call(s32[14592]{0:T(1024)} %broadcast_and_fusion.refs_0_, ...), custom_call_target="tpu_custom_call" | custom-call | flops 20000000000 | bytes 60000000 | tf_op jit(solution)/shard_map/pallas_call | solution.py:287
  241.3 6.0 %collective-permute-start.28 = (bf16[192,128]{1,0:T(8,128)(2,1)S(1)}, bf16[192,128]{1,0:T(8,128)(2,1)S(1)}, u32[]{:S(2)}, u32[]{:S(2)}) collective-permute-start(bf16[192,128]{1,0:T(8,128)(2,1)S(1)} %get-tuple-element.306), channel_id=1, source_target_pairs={{0,16},{8,24},{16,0},{24,8},{1,17},{9,25},{17,1},{25,9},{2,18},{10... | collective-permute-start | bytes 147464 | tf_op jit(solution)/shard_map/ppermute | solution.py:892
  247.3 3.6 collective-permute-start.29
  253.3 2.8 add_convert_fusion.6
  256.1 2.5 add_convert_fusion.8
  260.5 2.7 add_convert_fusion.3
  264.1 2.4 collective-permute-start.33
  266.4 3.0 collective-permute-start.34
  276.0 2.2 collective-permute-start.38
  278.2 11.1 %shard_map.298 = (f32[416,768]{1,0:T(8,128)}, bf16[416,768]{1,0:T(8,128)(2,1)}, f32[416,768]{1,0:T(8,128)}, bf16[2560,128]{1,0:T(8,128)(2,1)}, bf16[768,128]{1,0:T(8,128)(2,1)}, /*index=5*/bf16[768,128]{1,0:T(8,128)(2,1)}) custom-call(s32[16]{0:T(128)} %and_select_fusion.5.picks_ref, s32[2]{0:T(128)} %copy-done.7, bf16[1456,384]{1,0:T(8,128)(2,1)} %copy-done.41, ...), custom_call_target="tpu_custom_call" | custom-call | flops 6000000000 | bytes 15000000 | tf_op jit(solution)/shard_map/pallas_call | solution.py:714
  290.4 19.6 %shard_map.299 = (bf16[416,768]{1,0:T(8,128)(2,1)}, bf16[2304,128]{1,0:T(8,128)(2,1)}, bf16[2304,128]{1,0:T(8,128)(2,1)}) custom-call(s32[16]{0:T(128)} %and_select_fusion.5.picks_ref, s32[2]{0:T(128)} %copy-done.7, bf16[944,384]{1,0:T(8,128)(2,1)} %maximum_maximum_fusion.2.refs_0_, bf16[944,384]{1,0:T(8,128)(2,1)} %collective-permute-done.refs_1_, ...), custom_call_target="tpu_custom_call" | custom-call | flops 8999999488 | bytes 15000000 | tf_op jit(solution)/shard_map/pallas_call | solution.py:808
  313.5 2.8 collective-permute-done.39
  320.0 2.2 collective-permute-start.42
  322.3 6.2 %collective-permute-done.40 = bf16[1088,128]{1,0:T(8,128)(2,1)S(1)} collective-permute-done((bf16[1088,128]{1,0:T(8,128)(2,1)}, bf16[1088,128]{1,0:T(8,128)(2,1)S(1)}, u32[]{:S(2)}, u32[]{:S(2)}) %collective-permute-start.40) | collective-permute-done | bytes 278560 | tf_op jit(solution)/shard_map/ppermute | solution.py:842
  328.5 5.7 %collective-permute-done.42 = bf16[1088,128]{1,0:T(8,128)(2,1)} collective-permute-done((bf16[1088,128]{1,0:T(8,128)(2,1)}, bf16[1088,128]{1,0:T(8,128)(2,1)}, u32[]{:S(2)}, u32[]{:S(2)}) %collective-permute-start.42) | collective-permute-done | bytes 278560 | tf_op jit(solution)/shard_map/ppermute | solution.py:842
  336.9 4.8 %collective-permute-start.47 = (bf16[272,128]{1,0:T(8,128)(2,1)S(1)}, bf16[272,128]{1,0:T(8,128)(2,1)S(1)}, u32[]{:S(2)}, u32[]{:S(2)}) collective-permute-start(bf16[272,128]{1,0:T(8,128)(2,1)S(1)} %get-tuple-element.279), channel_id=1, source_target_pairs={{0,16},{8,24},{16,0},{24,8},{1,17},{9,25},{17,1},{25,9},{2,18},{10... | collective-permute-start | bytes 208904 | tf_op jit(solution)/shard_map/ppermute | solution.py:892
  347.9 2.5 collective-permute-start.49
  362.4 4.8 %collective-permute-done.52 = bf16[704,128]{1,0:T(8,128)(2,1)S(1)} collective-permute-done((bf16[704,128]{1,0:T(8,128)(2,1)S(1)}, bf16[704,128]{1,0:T(8,128)(2,1)S(1)}, u32[]{:S(2)}, u32[]{:S(2)}) %collective-permute-start.52) | collective-permute-done | bytes 180256 | tf_op jit(solution)/shard_map/ppermute | solution.py:842
  367.2 2.6 collective-permute-start.45
  369.8 7.1 %collective-permute-done.53 = bf16[704,128]{1,0:T(8,128)(2,1)S(1)} collective-permute-done((bf16[704,128]{1,0:T(8,128)(2,1)S(1)}, bf16[704,128]{1,0:T(8,128)(2,1)S(1)}, u32[]{:S(2)}, u32[]{:S(2)}) %collective-permute-start.53) | collective-permute-done | bytes 180256 | tf_op jit(solution)/shard_map/ppermute | solution.py:842
  (336 shorter events, 120.2 us)
Async XLA Ops:
  5.5 20.5 %collective-permute-start = (bf16[944,384]{1,0:T(8,128)(2,1)}, bf16[944,384]{1,0:T(8,128)(2,1)}, u32[]{:S(2)}, u32[]{:S(2)}) collective-permute-start(bf16[944,384]{1,0:T(8,128)(2,1)} %maximum_maximum_fusion.2.refs_0_), channel_id=1, source_target_pairs={{0,1},{1,0},{2,3},{3,2},{4,5},{5,4},{6,7},{7,6},{8,9},{9,8},{10,11... | collective-permute-start | bytes 2174984 | tf_op jit(solution)/shard_map/ppermute | solution.py:842
  8.5 18.0 %collective-permute-start.1 = (bf16[944,384]{1,0:T(8,128)(2,1)}, bf16[944,384]{1,0:T(8,128)(2,1)}, u32[]{:S(2)}, u32[]{:S(2)}) collective-permute-start(bf16[944,384]{1,0:T(8,128)(2,1)} %maximum_maximum_fusion.2.refs_0_), channel_id=1, source_target_pairs={{0,2},{1,3},{2,0},{3,1},{4,6},{5,7},{6,4},{7,5},{8,10},{9,11},{10,... | collective-permute-start | bytes 2174984 | tf_op jit(solution)/shard_map/ppermute | solution.py:842
  26.5 11.4 %collective-permute-start.7 = (bf16[416,384]{1,0:T(8,128)(2,1)S(1)}, bf16[416,384]{1,0:T(8,128)(2,1)S(1)}, u32[]{:S(2)}, u32[]{:S(2)}) collective-permute-start(bf16[416,384]{1,0:T(8,128)(2,1)S(1)} %get-tuple-element.96), channel_id=1, source_target_pairs={{0,3},{1,2},{2,1},{3,0},{4,7},{5,6},{6,5},{7,4},{8,11},{9,10},{10,... | collective-permute-start | bytes 958472 | tf_op jit(solution)/shard_map/ppermute | solution.py:842
  28.0 14.5 %collective-permute-start.8 = (bf16[416,384]{1,0:T(8,128)(2,1)S(1)}, bf16[416,384]{1,0:T(8,128)(2,1)S(1)}, u32[]{:S(2)}, u32[]{:S(2)}) collective-permute-start(bf16[416,384]{1,0:T(8,128)(2,1)S(1)} %get-tuple-element.97), channel_id=1, source_target_pairs={{0,2},{1,3},{2,0},{3,1},{4,6},{5,7},{6,4},{7,5},{8,10},{9,11},{10,... | collective-permute-start | bytes 958472 | tf_op jit(solution)/shard_map/ppermute | solution.py:842
  28.3 16.5 %collective-permute-start.9 = (bf16[416,384]{1,0:T(8,128)(2,1)S(1)}, bf16[416,384]{1,0:T(8,128)(2,1)S(1)}, u32[]{:S(2)}, u32[]{:S(2)}) collective-permute-start(bf16[416,384]{1,0:T(8,128)(2,1)S(1)} %get-tuple-element.98), channel_id=1, source_target_pairs={{0,1},{1,0},{2,3},{3,2},{4,5},{5,4},{6,7},{7,6},{8,9},{9,8},{10,11... | collective-permute-start | bytes 958472 | tf_op jit(solution)/shard_map/ppermute | solution.py:842
  31.2 28.1 %collective-permute-start.4 = (bf16[944,384]{1,0:T(8,128)(2,1)}, bf16[944,384]{1,0:T(8,128)(2,1)S(1)}, u32[]{:S(2)}, u32[]{:S(2)}) collective-permute-start(bf16[944,384]{1,0:T(8,128)(2,1)} %collective-permute-done.refs_1_), channel_id=1, source_target_pairs={{0,4},{4,0},{1,5},{5,1},{2,6},{6,2},{3,7},{7,3},{8,12},{12,8},{9,1... | collective-permute-start | bytes 2174984 | tf_op jit(solution)/shard_map/ppermute | solution.py:838
  31.2 28.1 %collective-permute-start.5 = (bf16[944,384]{1,0:T(8,128)(2,1)}, bf16[944,384]{1,0:T(8,128)(2,1)S(1)}, u32[]{:S(2)}, u32[]{:S(2)}) collective-permute-start(bf16[944,384]{1,0:T(8,128)(2,1)} %collective-permute-done.1.refs_2_), channel_id=1, source_target_pairs={{0,4},{4,0},{1,5},{5,1},{2,6},{6,2},{3,7},{7,3},{8,12},{12,8},{9,1... | collective-permute-start | bytes 2174984 | tf_op jit(solution)/shard_map/ppermute | solution.py:838
  37.8 12.4 %collective-permute-start.2 = (bf16[944,384]{1,0:T(8,128)(2,1)S(1)}, bf16[944,384]{1,0:T(8,128)(2,1)S(1)}, u32[]{:S(2)}, u32[]{:S(2)}) collective-permute-start(bf16[944,384]{1,0:T(8,128)(2,1)S(1)} %broadcast_select_fusion), channel_id=1, source_target_pairs={{0,2},{1,3},{2,0},{3,1},{4,5},{5,4},{6,7},{7,6},{8,10},{9,11},{10,... | collective-permute-start | bytes 2174984 | tf_op jit(solution)/shard_map/ppermute | solution.py:857
  57.4 24.7 %collective-permute-start.17 = (bf16[416,768]{1,0:T(8,128)(2,1)S(1)}, bf16[416,768]{1,0:T(8,128)(2,1)S(1)}, u32[]{:S(2)}, u32[]{:S(2)}) collective-permute-start(bf16[416,768]{1,0:T(8,128)(2,1)S(1)} %pad_maximum_fusion.4.refs_3_.refs_10_), channel_id=1, source_target_pairs={{0,1},{1,0},{2,3},{3,2},{4,5},{5,4},{6,7},{7,6},{8,9},{9,8},{10,11... | collective-permute-start | bytes 1916936 | tf_op jit(solution)/shard_map/ppermute | solution.py:842
  57.9 25.3 %collective-permute-start.18 = (bf16[416,768]{1,0:T(8,128)(2,1)S(1)}, bf16[416,768]{1,0:T(8,128)(2,1)S(1)}, u32[]{:S(2)}, u32[]{:S(2)}) collective-permute-start(bf16[416,768]{1,0:T(8,128)(2,1)S(1)} %pad_maximum_fusion.4.refs_3_.refs_10_), channel_id=1, source_target_pairs={{0,2},{1,3},{2,0},{3,1},{4,6},{5,7},{6,4},{7,5},{8,10},{9,11},{10,... | collective-permute-start | bytes 1916936 | tf_op jit(solution)/shard_map/ppermute | solution.py:842
  59.3 24.9 %collective-permute-start.13 = (bf16[416,768]{1,0:T(8,128)(2,1)S(1)}, bf16[416,768]{1,0:T(8,128)(2,1)S(1)}, u32[]{:S(2)}, u32[]{:S(2)}) collective-permute-start(bf16[416,768]{1,0:T(8,128)(2,1)S(1)} %pad_maximum_fusion.4.refs_3_.refs_10_), channel_id=1, source_target_pairs={{0,4},{4,0},{1,5},{5,1},{2,6},{6,2},{3,7},{7,3},{8,12},{12,8},{9,1... | collective-permute-start | bytes 1916936 | tf_op jit(solution)/shard_map/ppermute | solution.py:838
  81.1 17.4 %collective-permute-start.10 = (bf16[416,768]{1,0:T(8,128)(2,1)}, bf16[416,768]{1,0:T(8,128)(2,1)S(1)}, u32[]{:S(2)}, u32[]{:S(2)}) collective-permute-start(bf16[416,768]{1,0:T(8,128)(2,1)} %get-tuple-element.106.refs_1_.refs_6_), channel_id=1, source_target_pairs={{0,1},{1,0},{2,3},{3,2},{4,5},{5,4},{6,7},{7,6},{8,9},{9,8},{10,11... | collective-permute-start | bytes 1916936 | tf_op jit(solution)/shard_map/ppermute | solution.py:842
  82.1 16.5 %collective-permute-start.11 = (bf16[416,768]{1,0:T(8,128)(2,1)}, bf16[416,768]{1,0:T(8,128)(2,1)S(1)}, u32[]{:S(2)}, u32[]{:S(2)}) collective-permute-start(bf16[416,768]{1,0:T(8,128)(2,1)} %get-tuple-element.106.refs_1_.refs_6_), channel_id=1, source_target_pairs={{0,2},{1,3},{2,0},{3,1},{4,6},{5,7},{6,4},{7,5},{8,10},{9,11},{10,... | collective-permute-start | bytes 1916936 | tf_op jit(solution)/shard_map/ppermute | solution.py:842
  83.4 22.0 %collective-permute-start.22 = (bf16[416,768]{1,0:T(8,128)(2,1)S(1)}, bf16[416,768]{1,0:T(8,128)(2,1)S(1)}, u32[]{:S(2)}, u32[]{:S(2)}) collective-permute-start(bf16[416,768]{1,0:T(8,128)(2,1)S(1)} %broadcast_select_fusion.1), channel_id=1, source_target_pairs={{0,2},{1,3},{2,0},{3,1},{4,5},{5,4},{6,7},{7,6},{8,10},{9,11},{10,... | collective-permute-start | bytes 1916936 | tf_op jit(solution)/shard_map/ppermute | solution.py:857
  84.2 22.3 %collective-permute-start.19 = (bf16[416,768]{1,0:T(8,128)(2,1)S(1)}, bf16[416,768]{1,0:T(8,128)(2,1)S(1)}, u32[]{:S(2)}, u32[]{:S(2)}) collective-permute-start(bf16[416,768]{1,0:T(8,128)(2,1)S(1)} %collective-permute-done.17.refs_5_), channel_id=1, source_target_pairs={{0,4},{4,0},{1,5},{5,1},{2,6},{6,2},{3,7},{7,3},{8,12},{12,8},{9,1... | collective-permute-start | bytes 1916936 | tf_op jit(solution)/shard_map/ppermute | solution.py:838
  84.2 22.3 %collective-permute-start.20 = (bf16[416,768]{1,0:T(8,128)(2,1)S(1)}, bf16[416,768]{1,0:T(8,128)(2,1)S(1)}, u32[]{:S(2)}, u32[]{:S(2)}) collective-permute-start(bf16[416,768]{1,0:T(8,128)(2,1)S(1)} %collective-permute-done.18.refs_6_), channel_id=1, source_target_pairs={{0,4},{4,0},{1,5},{5,1},{2,6},{6,2},{3,7},{7,3},{8,12},{12,8},{9,1... | collective-permute-start | bytes 1916936 | tf_op jit(solution)/shard_map/ppermute | solution.py:838
  105.4 13.8 %collective-permute-start.14 = (bf16[416,768]{1,0:T(8,128)(2,1)S(1)}, bf16[416,768]{1,0:T(8,128)(2,1)S(1)}, u32[]{:S(2)}, u32[]{:S(2)}) collective-permute-start(bf16[416,768]{1,0:T(8,128)(2,1)S(1)} %broadcast_select_fusion.2), channel_id=1, source_target_pairs={{0,2},{1,3},{2,0},{3,1},{4,5},{5,4},{6,7},{7,6},{8,10},{9,11},{10,... | collective-permute-start | bytes 1916936 | tf_op jit(solution)/shard_map/ppermute | solution.py:857
  106.6 13.8 %collective-permute-start.23 = (bf16[416,768]{1,0:T(8,128)(2,1)S(1)}, bf16[416,768]{1,0:T(8,128)(2,1)S(1)}, u32[]{:S(2)}, u32[]{:S(2)}) collective-permute-start(bf16[416,768]{1,0:T(8,128)(2,1)S(1)} %collective-permute-done.22.refs_3_), channel_id=1, source_target_pairs={{0,4},{4,0},{1,5},{5,1},{2,6},{6,2},{3,7},{7,3},{8,12},{12,8},{9,1... | collective-permute-start | bytes 1916936 | tf_op jit(solution)/shard_map/ppermute | solution.py:838
  240.3 13.0 %collective-permute-start.31 = (bf16[832,768]{1,0:T(8,128)(2,1)}, bf16[832,768]{1,0:T(8,128)(2,1)}, u32[]{:S(2)}, u32[]{:S(2)}) collective-permute-start(bf16[832,768]{1,0:T(8,128)(2,1)} %get-tuple-element.133), channel_id=1, source_target_pairs={{0,4},{4,0},{1,5},{5,1},{2,6},{6,2},{3,7},{7,3},{8,12},{12,8},{9,1... | collective-permute-start | bytes 3833864 | tf_op jit(solution)/shard_map/ppermute | solution.py:838
  240.7 15.3 %collective-permute-start.30 = (bf16[832,768]{1,0:T(8,128)(2,1)}, bf16[832,768]{1,0:T(8,128)(2,1)}, u32[]{:S(2)}, u32[]{:S(2)}) collective-permute-start(bf16[832,768]{1,0:T(8,128)(2,1)} %get-tuple-element.131), channel_id=1, source_target_pairs={{0,4},{4,0},{1,5},{5,1},{2,6},{6,2},{3,7},{7,3},{8,12},{12,8},{9,1... | collective-permute-start | bytes 3833864 | tf_op jit(solution)/shard_map/ppermute | solution.py:838
  240.9 19.6 %collective-permute-start.26 = (bf16[832,896]{1,0:T(8,128)(2,1)S(1)}, bf16[832,896]{1,0:T(8,128)(2,1)}, u32[]{:S(2)}, u32[]{:S(2)}) collective-permute-start(bf16[832,896]{1,0:T(8,128)(2,1)S(1)} %add_convert_fusion), channel_id=1, source_target_pairs={{0,1},{1,0},{2,3},{3,2},{4,6},{5,7},{6,4},{7,5},{8,9},{9,8},{10,11... | collective-permute-start | bytes 4472840 | tf_op jit(solution)/shard_map/ppermute | solution.py:857
  241.3 11.5 %collective-permute-start.28 = (bf16[192,128]{1,0:T(8,128)(2,1)S(1)}, bf16[192,128]{1,0:T(8,128)(2,1)S(1)}, u32[]{:S(2)}, u32[]{:S(2)}) collective-permute-start(bf16[192,128]{1,0:T(8,128)(2,1)S(1)} %get-tuple-element.306), channel_id=1, source_target_pairs={{0,16},{8,24},{16,0},{24,8},{1,17},{9,25},{17,1},{25,9},{2,18},{10... | collective-permute-start | bytes 147464 | tf_op jit(solution)/shard_map/ppermute | solution.py:892
  263.2 11.6 %collective-permute-start.32 = (bf16[416,896]{1,0:T(8,128)(2,1)S(1)}, bf16[416,896]{1,0:T(8,128)(2,1)S(1)}, u32[]{:S(2)}, u32[]{:S(2)}) collective-permute-start(bf16[416,896]{1,0:T(8,128)(2,1)S(1)} %get-tuple-element.223), channel_id=1, source_target_pairs={{0,2},{1,3},{2,0},{3,1},{4,5},{5,4},{6,7},{7,6},{8,10},{9,11},{10,... | collective-permute-start | bytes 2236424 | tf_op jit(solution)/shard_map/ppermute | solution.py:857
  274.7 35.3 %collective-permute-start.36 = (bf16[416,768]{1,0:T(8,128)(2,1)}, bf16[416,768]{1,0:T(8,128)(2,1)S(1)}, u32[]{:S(2)}, u32[]{:S(2)}) collective-permute-start(bf16[416,768]{1,0:T(8,128)(2,1)} %get-tuple-element.147), channel_id=1, source_target_pairs={{0,2},{1,3},{2,0},{3,1},{4,5},{5,4},{6,7},{7,6},{8,10},{9,11},{10,... | collective-permute-start | bytes 1916936 | tf_op jit(solution)/shard_map/ppermute | solution.py:857
  275.7 34.4 %collective-permute-start.37 = (bf16[416,768]{1,0:T(8,128)(2,1)}, bf16[416,768]{1,0:T(8,128)(2,1)S(1)}, u32[]{:S(2)}, u32[]{:S(2)}) collective-permute-start(bf16[416,768]{1,0:T(8,128)(2,1)} %get-tuple-element.148), channel_id=1, source_target_pairs={{0,1},{1,0},{2,3},{3,2},{4,6},{5,7},{6,4},{7,5},{8,9},{9,8},{10,11... | collective-permute-start | bytes 1916936 | tf_op jit(solution)/shard_map/ppermute | solution.py:857
  276.0 34.1 %collective-permute-start.38 = (bf16[416,768]{1,0:T(8,128)(2,1)S(1)}, bf16[416,768]{1,0:T(8,128)(2,1)S(1)}, u32[]{:S(2)}, u32[]{:S(2)}) collective-permute-start(bf16[416,768]{1,0:T(8,128)(2,1)S(1)} %copy-done.30), channel_id=1, source_target_pairs={{0,3},{1,2},{2,1},{3,0},{4,7},{5,6},{6,5},{7,4},{8,11},{9,10},{10,... | collective-permute-start | bytes 1916936 | tf_op jit(solution)/shard_map/ppermute | solution.py:857
  320.0 14.1 %collective-permute-start.42 = (bf16[1088,128]{1,0:T(8,128)(2,1)}, bf16[1088,128]{1,0:T(8,128)(2,1)}, u32[]{:S(2)}, u32[]{:S(2)}) collective-permute-start(bf16[1088,128]{1,0:T(8,128)(2,1)} %get-tuple-element.241), channel_id=1, source_target_pairs={{0,3},{1,2},{2,1},{3,0},{4,7},{5,6},{6,5},{7,4},{8,11},{9,10},{10,... | collective-permute-start | bytes 835592 | tf_op jit(solution)/shard_map/ppermute | solution.py:842
  353.7 29.4 %collective-permute-start.43 = (bf16[416,384]{1,0:T(8,128)(2,1)}, bf16[416,384]{1,0:T(8,128)(2,1)S(1)}, u32[]{:S(2)}, u32[]{:S(2)}) collective-permute-start(bf16[416,384]{1,0:T(8,128)(2,1)} %get-tuple-element.235), channel_id=1, source_target_pairs={{0,1},{1,0},{2,3},{3,2},{4,5},{5,4},{6,7},{7,6},{8,9},{9,8},{10,11... | collective-permute-start | bytes 958472 | tf_op jit(solution)/shard_map/ppermute | solution.py:842
  355.2 27.9 %collective-permute-start.44 = (bf16[416,384]{1,0:T(8,128)(2,1)}, bf16[416,384]{1,0:T(8,128)(2,1)S(1)}, u32[]{:S(2)}, u32[]{:S(2)}) collective-permute-start(bf16[416,384]{1,0:T(8,128)(2,1)} %get-tuple-element.234), channel_id=1, source_target_pairs={{0,2},{1,3},{2,0},{3,1},{4,6},{5,7},{6,4},{7,5},{8,10},{9,11},{10,... | collective-permute-start | bytes 958472 | tf_op jit(solution)/shard_map/ppermute | solution.py:842
  357.6 19.3 %collective-permute-start.53 = (bf16[704,128]{1,0:T(8,128)(2,1)S(1)}, bf16[704,128]{1,0:T(8,128)(2,1)S(1)}, u32[]{:S(2)}, u32[]{:S(2)}) collective-permute-start(bf16[704,128]{1,0:T(8,128)(2,1)S(1)} %pad_maximum_fusion.15), channel_id=1, source_target_pairs={{0,2},{1,3},{2,0},{3,1},{4,6},{5,7},{6,4},{7,5},{8,10},{9,11},{10,... | collective-permute-start | bytes 540680 | tf_op jit(solution)/shard_map/ppermute | solution.py:842
  358.6 18.3 %collective-permute-start.54 = (bf16[704,128]{1,0:T(8,128)(2,1)S(1)}, bf16[704,128]{1,0:T(8,128)(2,1)S(1)}, u32[]{:S(2)}, u32[]{:S(2)}) collective-permute-start(bf16[704,128]{1,0:T(8,128)(2,1)S(1)} %pad_maximum_fusion.15), channel_id=1, source_target_pairs={{0,1},{1,0},{2,3},{3,2},{4,5},{5,4},{6,7},{7,6},{8,9},{9,8},{10,11... | collective-permute-start | bytes 540680 | tf_op jit(solution)/shard_map/ppermute | solution.py:842
  367.2 15.9 %collective-permute-start.45 = (bf16[416,384]{1,0:T(8,128)(2,1)}, bf16[416,384]{1,0:T(8,128)(2,1)S(1)}, u32[]{:S(2)}, u32[]{:S(2)}) collective-permute-start(bf16[416,384]{1,0:T(8,128)(2,1)} %get-tuple-element.232), channel_id=1, source_target_pairs={{0,3},{1,2},{2,1},{3,0},{4,7},{5,6},{6,5},{7,4},{8,11},{9,10},{10,... | collective-permute-start | bytes 958472 | tf_op jit(solution)/shard_map/ppermute | solution.py:842
  (72 other events, 435.6 us)
where the time goes:
time: 399 us; the launch traced here: 396 us
  Pallas kernels  176 us (44%)
  waiting for transfers between devices  66 us (17%)
  starting transfers between devices  64.4 us (16%)
  other arithmetic  55.1 us (14%)
  local copies, waits for them, and re-layouts  32.6 us (8%)
    pallas_call x1, Pallas kernels, moe_call(): pl.pallas_call(lambda *refs: moe_kernel(places, *refs), grid_spec=pltpu.P...  106 us
    ppermute x18, waiting for transfers between devices, across_col(): return lax.ppermute(value, 'col', [(i, i ^ step) for i in range(4)])  40.8 us
    ppermute x12, starting transfers between devices, across_dp(): return lax.ppermute(value, 'dp', [(i, i ^ step) for i in range(4)])  28.1 us
    ppermute x18, starting transfers between devices, across_col(): return lax.ppermute(value, 'col', [(i, i ^ step) for i in range(4)])  24.1 us
    unnamed x113, local copies, waits for them, and re-layouts  23.2 us
    pallas_call x3, Pallas kernels, table_call(): pl.pallas_call(lambda *refs: table_kernel(n, *refs), grid_spec=pltpu.Pref...  20.4 us
    pallas_call x1, Pallas kernels, qkv_back_call(): pl.pallas_call(qkv_back_kernel, grid_spec=pltpu.PrefetchScalarGridSpec(nu...  19.6 us
    pallas_call x1, Pallas kernels, attend_call(): pl.pallas_call(attend_kernel, grid_spec=pltpu.PrefetchScalarGridSpec(num_...  15.7 us
  transfers between devices with their start and end apart: 56, of which 21 were waited for; matrix products, arithmetic and copies ran while one was open for 14% of the time, Pallas kernels for 16%

commit v1 on v0

--- a/solution.py
+++ b/solution.py
@@ -484,6 +484,73 @@
     )(place, tokens, cotangent)
 
 
+def finish_kernel(place_ref, mine, one, two, three, far, dp_sums, *refs):
+    (
+        a_qkv, b_qkv, a_out, b_out, a_router, b_router, a_up, b_up, a_down, b_down, wide, tall, every,
+    ) = refs
+    row, col = place_ref[0], place_ref[1]
+    near_at = pl.multiple_of(row * 96, 32)
+    far_at = pl.multiple_of((1 - row) * 96, 32)
+    for p in range(4):
+        ours = mine[96 * p : 96 * p + 96, :].astype(f32)
+        theirs = far[96 * p : 96 * p + 96, :].astype(f32)
+        if p < 3:
+            a_qkv[p, pl.ds(near_at, 96), :] = ours
+            a_qkv[p, pl.ds(far_at, 96), :] = theirs
+        else:
+            wide[pl.ds(near_at, 96), :] = ours
+            wide[pl.ds(far_at, 96), :] = theirs
+    b_out[...] = wide[...].T[:, : D // 4]
+    share = BOTH_ROWS // 8
+    for s, got in enumerate((mine, one, two, three)):
+        base = 384 if s == 0 else 0
+        at = pl.multiple_of((col ^ s) * 96, 32)
+        for p in range(4):
+            piece = got[base + 96 * p : base + 96 * p + 96, :].astype(f32)
+            if p < 3:
+                tall[p, pl.ds(at, 96), :] = piece
+            else:
+                a_out[pl.ds(at, 96), :] = piece
+        ours = got[base + 384 : base + 384 + share, :].astype(f32)
+        theirs = far[384 + share * s : 384 + share * s + share, :].astype(f32)
+        every[pl.ds(pl.multiple_of((row * 4 + (col ^ s)) * share, 64), share), :] = ours
+        every[pl.ds(pl.multiple_of(((1 - row) * 4 + (col ^ s)) * share, 64), share), :] = theirs
+    for p in range(3):
+        b_qkv[p] = tall[p].T
+    a_router[...] = every[0:768, :]
+    a_up[...] = every[768:1536, :]
+    b_down[...] = every[1536:2304, :].T
+    b_router[...] = every[2304:2432, :].T[:, :EXPERTS]
+    b_up[...] = dp_sums[0:384, :].astype(f32).T
+    a_down[...] = dp_sums[384:768, :].astype(f32)
+
+
+def finish_call(place, mine, got, far, dp_sums):
+    inside = pl.BlockSpec(memory_space=pltpu.VMEM)
+    half = D // 2
+    shapes = [
+        (3, D // 4, ADAPT), (3, ADAPT, half), (half, ADAPT), (ADAPT, D // 4), (D, ADAPT), (ADAPT, EXPERTS),
+        (D, ADAPT), (ADAPT, half), (half, ADAPT), (ADAPT, D),
+    ]
+    return pl.pallas_call(
+        finish_kernel,
+        grid_spec=pltpu.PrefetchScalarGridSpec(
+            num_scalar_prefetch=1,
+            grid=(1,),
+            in_specs=[inside] * 6,
+            out_specs=[inside] * 10,
+            scratch_shapes=[
+                pltpu.VMEM((256, 128), f32),
+                pltpu.VMEM((3, half, 128), f32),
+                pltpu.VMEM((BOTH_ROWS, 128), f32),
+            ],
+        ),
+        out_shape=[jax.ShapeDtypeStruct(shape, f32) for shape in shapes],
+        compiler_params=pltpu.CompilerParams(vmem_limit_bytes=32 * 1024 * 1024),
+        cost_estimate=pl.CostEstimate(flops=1_000_000_000, bytes_accessed=4_000_000, transcendentals=0),
+    )(place, mine, *got, far, dp_sums)
+
+
 def merge_kernel(place_ref, *refs):
     blocks, refs = refs[:4], refs[4:]
     block_out, tokens_out, stage, tall, sem = refs
@@ -522,7 +589,7 @@
         ),
         out_shape=[jax.ShapeDtypeStruct((rows, width), bf16), jax.ShapeDtypeStruct((rows, width), f32)],
         compiler_params=pltpu.CompilerParams(vmem_limit_bytes=32 * 1024 * 1024),
-        cost_estimate=pl.CostEstimate(flops=1_000_000_000, bytes_accessed=3_000_000, transcendentals=0),
+        cost_estimate=pl.CostEstimate(flops=8_000_000_000, bytes_accessed=3_000_000, transcendentals=0),
     )(place, *blocks)
 
 
@@ -905,23 +972,8 @@
     return jnp.concatenate([col_parts, row_parts, both_parts], axis=1)
 
 
-def reduce_col(value, col):
-    found = [at_place(value, 0, col)]
-    for s in range(1, 4):
-        found.append(across_col(at_place(value, 0, col ^ s), s))
-    return added(*found).astype(bf16)
-
-
-def spread_parts(mine, row, col):
-    spread = by_place([mine[384:]] + [across_col(mine[384:], s) for s in range(1, 4)], col)
-    row_sums = jnp.stack([one[:384].reshape(4, 96, 128) for one in spread], axis=1).reshape(4, 384, 128)
-    near = jnp.concatenate([mine[:384]] + [one[384:] for one in spread])
-    far = across_row(near)
-    first = jnp.where(row == 0, near, far)
-    second = jnp.where(row == 0, far, near)
-    col_sums = jnp.stack([first[:384].reshape(4, 96, 128), second[:384].reshape(4, 96, 128)], axis=1).reshape(4, 192, 128)
-    both_sums = jnp.concatenate([first[384:], second[384:]])
-    return col_sums, row_sums, both_sums
+def exchange_col(value, col):
+    return [at_place(value, 0, col)] + [across_col(at_place(value, 0, col ^ s), s) for s in range(1, 4)]
 
 
 def to_features(first, second, col):
@@ -996,8 +1048,10 @@
     slim_router = jnp.concatenate([w_router, jnp.zeros((D, 96), bf16)], axis=1)
     slim_b_router = jnp.concatenate([b_router, jnp.zeros((ADAPT, 96), bf16)], axis=1)
 
-    x, token_list, tile_experts = lax.optimization_barrier((x, token_list, tile_experts))
-    cot, unused = lax.optimization_barrier((cot, far[3]))
+    x, token_list, tile_experts, wide_router, wide_b_router, slim_router, slim_b_router = lax.optimization_barrier(
+        (x, token_list, tile_experts, wide_router, wide_b_router, slim_router, slim_b_router)
+    )
+    cot, unused = lax.optimization_barrier((cot, near[3]))
     two, resid, normed, qkv, mixed, probs, lows = attend_call(
         picks, place, blocks, b_qkv, a_out, out_w, x, gain_one, gain_two, full_b_out
     )
@@ -1053,30 +1107,16 @@
     row_parts = jnp.concatenate([part_b_qkv, part_a_out])
     theirs = across_row(part_share(col_parts, row_parts, both_parts, 1 - row))
     shared = added(part_share(col_parts, row_parts, both_parts, row), theirs).astype(bf16)
-    mine = reduce_col(shared, col)
+    found = exchange_col(shared, col)
+    mine = added(*found).astype(bf16)
     mine, grad_tokens, base = lax.optimization_barrier((mine, grad_tokens, base))
     moves = to_features(grad_tokens, (base + added(*sums)).astype(bf16), col)
     mine = spread_dp(scatter_dp(mine)) if four_dp else lax.psum(mine, "dp")
+    got = [across_col(mine[384:], s) for s in range(1, 4)]
+    far = across_row(jnp.concatenate([mine[:384], mine[768:]] + [one[384:] for one in got]))
     block_out, grad_tokens = merge_call(place, moves, tokens.shape[0])
-    col_sums, row_sums, both_sums = spread_parts(mine, row, col)
-    col_sums = col_sums.astype(f32)
-    row_sums = row_sums.astype(f32)
-    both_sums = both_sums.astype(f32)
-    dp_sums = dp_sums.astype(f32)
-    return (
-        block_out,
-        grad_tokens,
-        col_sums[:3],
-        jnp.swapaxes(row_sums[:3], 1, 2),
-        row_sums[3],
-        col_sums[3].T,
-        both_sums[:768],
-        both_sums[2304:2336].T,
-        both_sums[768:1536],
-        dp_sums[:384].T,
-        dp_sums[384:],
-        both_sums[1536:2304].T,
-    )
+    far, block_out, grad_tokens = lax.optimization_barrier((far, block_out, grad_tokens))
+    return (block_out, grad_tokens, *finish_call(place, mine, got, far, dp_sums))
 
 
 def solution(mesh):

time: 399 us -> 385 us (0.965)
  starting transfers between devices: 64.4 us -> 52 us
  local copies, waits for them, and re-layouts: 32.6 us -> 23.9 us
  other arithmetic: 55.1 us -> 48.1 us
  waiting for transfers between devices: 66 us -> 72.3 us
  Pallas kernels: 176 us -> 180 us
    ppermute x12, starting transfers between devices: 28.1 us -> 17.9 us  [across_dp(): return lax.ppermute(value, 'dp', [(i, i ^ step) for i in range(4)])]
    unnamed x113 -> x93, local copies, waits for them, and re-layouts: 23.2 us -> 17 us
    ppermute x8, waiting for transfers between devices: 12.7 us -> 16.7 us  [across_chip(): return lax.ppermute(value, ('row', 'col'), pairs)]
  transfers between devices with their start and end apart: 56 -> 56, of which waited for: 21 -> 23; matrix products, arithmetic and copies ran while one was open for 14% -> 12% of each run, Pallas kernels for 16% -> 17%
where the time goes in v1:
time: 385 us; the launch traced here: 378 us
  Pallas kernels  180 us (47%)
  waiting for transfers between devices  72.3 us (19%)
  starting transfers between devices  52 us (14%)
  other arithmetic  48.1 us (12%)
  local copies, waits for them, and re-layouts  23.9 us (6%)
    pallas_call x1, Pallas kernels, moe_call(): pl.pallas_call(lambda *refs: moe_kernel(places, *refs), grid_spec=pltpu.P...  107 us
    ppermute x18, waiting for transfers between devices, across_col(): return lax.ppermute(value, 'col', [(i, i ^ step) for i in range(4)])  40.7 us
    ppermute x18, starting transfers between devices, across_col(): return lax.ppermute(value, 'col', [(i, i ^ step) for i in range(4)])  22.9 us
    pallas_call x3, Pallas kernels, table_call(): pl.pallas_call(lambda *refs: table_kernel(n, *refs), grid_spec=pltpu.Pref...  20.7 us
    pallas_call x1, Pallas kernels, qkv_back_call(): pl.pallas_call(qkv_back_kernel, grid_spec=pltpu.PrefetchScalarGridSpec(nu...  19.7 us
    ppermute x12, starting transfers between devices, across_dp(): return lax.ppermute(value, 'dp', [(i, i ^ step) for i in range(4)])  17.9 us
    unnamed x93, local copies, waits for them, and re-layouts  17 us
    ppermute x8, waiting for transfers between devices, across_chip(): return lax.ppermute(value, ('row', 'col'), pairs)  16.7 us
  transfers between devices with their start and end apart: 56, of which 23 were waited for; matrix products, arithmetic and copies ran while one was open for 12% of the time, Pallas kernels for 17%

profile of v1, /device:TPU:0, one launch (start us, length us, event | category | flops | bytes accessed | tf_op | source)
XLA Modules:
  0.0 378.4 jit_solution(13059753850567544487)
XLA Ops:
  5.5 2.9 collective-permute-start
  18.4 7.8 %sort.14 = (s32[14592]{0:T(1024)S(1)}, s32[14592]{0:T(1024)}) sort(s32[14592]{0:T(1024)S(1)} %pad_add_fusion, s32[14592]{0:T(1024)S(1)} %iota.71), dimensions={0}, to_apply=%region_1.2 | sort | flops 204288 | bytes 233472 | tf_op jit(solution)/shard_map/sort | solution.py:351
  34.1 4.9 %collective-permute-done.7 = bf16[416,384]{1,0:T(8,128)(2,1)S(1)} collective-permute-done((bf16[416,384]{1,0:T(8,128)(2,1)S(1)}, bf16[416,384]{1,0:T(8,128)(2,1)S(1)}, u32[]{:S(2)}, u32[]{:S(2)}) %collective-permute-start.7) | collective-permute-done | bytes 319520 | tf_op jit(solution)/shard_map/ppermute | solution.py:909
  39.6 3.7 collective-permute-done.8
  47.0 4.0 %collective-permute-done.2.refs_3_ = bf16[944,384]{1,0:T(8,128)(2,1)S(1)} collective-permute-done((bf16[944,384]{1,0:T(8,128)(2,1)S(1)}, bf16[944,384]{1,0:T(8,128)(2,1)S(1)}, u32[]{:S(2)}, u32[]{:S(2)}) %collective-permute-start.2) | collective-permute-done | bytes 725024 | tf_op jit(solution)/shard_map/ppermute | solution.py:924
  62.5 15.7 %shard_map.293 = (bf16[416,768]{1,0:T(8,128)(2,1)}, f32[416,768]{1,0:T(8,128)}, bf16[416,768]{1,0:T(8,128)(2,1)}, bf16[3,416,768]{2,1,0:T(8,128)(2,1)}, bf16[416...) custom-call(s32[16]{0:T(128)} %and_select_fusion.5.picks_ref, s32[2]{0:T(128)} %copy-done.5, ...), custom_call_target="tpu_custom_call" | custom-call | flops 4000000000 | bytes 15000000 | tf_op jit(solution)/shard_map/pallas_call | solution.py:683
  83.1 6.0 %shard_map.294.refs_4_ = bf16[832,16,128]{2,1,0:T(8,128)(2,1)S(1)} custom-call(s32[4]{0:T(128)S(1)} %pad_add_fusion.3.refs_0_, bf16[416,768]{1,0:T(8,128)(2,1)S(1)} %copy-done.1, bf16[416,768]{1,0:T(8,128)(2,1)S(1)} %collective-permute-done.12.refs_2_, bf16[416,768]{1,0:T(8,128)(2,1)S(1)} %pad_maximum_fusion.4.refs_3_.refs_10_, ...), custom_call_target="tpu_custom_call" | custom-call | flops 6000000000 | bytes 6000000 | tf_op jit(solution)/shard_map/pallas_call | solution.py:100
  90.9 5.3 %collective-permute-done.10.refs_1_ = bf16[416,768]{1,0:T(8,128)(2,1)S(1)} collective-permute-done((bf16[416,768]{1,0:T(8,128)(2,1)}, bf16[416,768]{1,0:T(8,128)(2,1)S(1)}, u32[]{:S(2)}, u32[]{:S(2)}) %collective-permute-start.10) | collective-permute-done | bytes 639008 | tf_op jit(solution)/shard_map/ppermute | solution.py:909
  97.5 6.2 %collective-permute-done.22.refs_3_ = bf16[416,768]{1,0:T(8,128)(2,1)S(1)} collective-permute-done((bf16[416,768]{1,0:T(8,128)(2,1)S(1)}, bf16[416,768]{1,0:T(8,128)(2,1)S(1)}, u32[]{:S(2)}, u32[]{:S(2)}) %collective-permute-start.22) | collective-permute-done | bytes 639008 | tf_op jit(solution)/shard_map/ppermute | solution.py:924
  104.5 9.7 %shard_map.295.refs_5_ = bf16[1664,16,128]{2,1,0:T(8,128)(2,1)S(1)} custom-call(s32[8]{0:T(128)S(1)} %pad_add_fusion.4.refs_0_, bf16[416,768]{1,0:T(8,128)(2,1)S(1)} %collective-permute-done.10.refs_1_, bf16[416,768]{1,0:T(8,128)(2,1)S(1)} %collective-permute-done.11.refs_2_, bf16[416,768]{1,0:T(8,128)(2,1)S(1)} %collective-permute-done.15.refs_3_, ...), custom_call_target="tpu_custom_call" | custom-call | flops 12000000000 | bytes 12000000 | tf_op jit(solution)/shard_map/pallas_call | solution.py:100
  114.2 2.7 copy-done.9
  119.0 5.1 %shard_map.296.refs_6_ = bf16[832,16,128]{2,1,0:T(8,128)(2,1)S(1)} custom-call(s32[4]{0:T(128)S(1)} %pad_add_fusion.5.refs_0_, bf16[416,768]{1,0:T(8,128)(2,1)S(1)} %collective-permute-done.14.refs_1_, bf16[416,768]{1,0:T(8,128)(2,1)S(1)} %collective-permute-done.21.refs_2_, bf16[416,768]{1,0:T(8,128)(2,1)S(1)} %collective-permute-done.22.refs_3_, ...), custom_call_target="tpu_custom_call" | custom-call | flops 6000000000 | bytes 6000000 | tf_op jit(solution)/shard_map/pallas_call | solution.py:100
  125.9 107.3 %shard_map.297 = (bf16[832,768]{1,0:T(8,128)(2,1)}, bf16[832,768]{1,0:T(8,128)(2,1)}, bf16[832,768]{1,0:T(8,128)(2,1)}, bf16[832,768]{1,0:T(8,128)(2,1)}, bf16[8...) custom-call(s32[14592]{0:T(1024)} %broadcast_and_fusion.refs_0_, ...), custom_call_target="tpu_custom_call" | custom-call | flops 20000000000 | bytes 60000000 | tf_op jit(solution)/shard_map/pallas_call | solution.py:287
  240.7 2.5 collective-permute-start.28
  243.2 2.3 collective-permute-done.27
  251.5 2.8 add_convert_fusion.6
  254.2 2.4 add_convert_fusion.8
  256.7 3.0 collective-permute-done.26
  259.7 2.6 add_convert_fusion.3
  265.0 2.4 collective-permute-start.35
  270.3 3.5 collective-permute-done.32.refs_12_
  277.3 11.0 %shard_map.298 = (f32[416,768]{1,0:T(8,128)}, bf16[416,768]{1,0:T(8,128)(2,1)}, f32[416,768]{1,0:T(8,128)}, bf16[2560,128]{1,0:T(8,128)(2,1)}, bf16[768,128]{1,0:T(8,128)(2,1)}, /*index=5*/bf16[768,128]{1,0:T(8,128)(2,1)}) custom-call(s32[16]{0:T(128)} %and_select_fusion.5.picks_ref, s32[2]{0:T(128)} %copy-done.5, bf16[1456,384]{1,0:T(8,128)(2,1)} %copy-done.32, ...), custom_call_target="tpu_custom_call" | custom-call | flops 6000000000 | bytes 15000000 | tf_op jit(solution)/shard_map/pallas_call | solution.py:781
  289.5 19.7 %shard_map.299 = (bf16[416,768]{1,0:T(8,128)(2,1)}, bf16[2304,128]{1,0:T(8,128)(2,1)}, bf16[2304,128]{1,0:T(8,128)(2,1)}) custom-call(s32[16]{0:T(128)} %and_select_fusion.5.picks_ref, s32[2]{0:T(128)} %copy-done.5, bf16[944,384]{1,0:T(8,128)(2,1)} %maximum_maximum_fusion.2.refs_0_, bf16[944,384]{1,0:T(8,128)(2,1)} %collective-permute-done.refs_1_, ...), custom_call_target="tpu_custom_call" | custom-call | flops 8999999488 | bytes 15000000 | tf_op jit(solution)/shard_map/pallas_call | solution.py:875
  313.2 3.0 collective-permute-done.39
  322.2 6.2 %collective-permute-done.40 = bf16[1088,128]{1,0:T(8,128)(2,1)S(1)} collective-permute-done((bf16[1088,128]{1,0:T(8,128)(2,1)}, bf16[1088,128]{1,0:T(8,128)(2,1)S(1)}, u32[]{:S(2)}, u32[]{:S(2)}) %collective-permute-start.40) | collective-permute-done | bytes 278560 | tf_op jit(solution)/shard_map/ppermute | solution.py:909
  328.4 5.5 %collective-permute-done.41 = bf16[1088,128]{1,0:T(8,128)(2,1)S(1)} collective-permute-done((bf16[1088,128]{1,0:T(8,128)(2,1)}, bf16[1088,128]{1,0:T(8,128)(2,1)S(1)}, u32[]{:S(2)}, u32[]{:S(2)}) %collective-permute-start.41) | collective-permute-done | bytes 278560 | tf_op jit(solution)/shard_map/ppermute | solution.py:909
  335.1 2.8 collective-permute-start.44
  345.6 2.3 collective-permute-start.46
  347.9 2.2 collective-permute-start.48
  355.5 8.1 %collective-permute-done.49.one = bf16[704,128]{1,0:T(8,128)(2,1)S(1)} collective-permute-done((bf16[704,128]{1,0:T(8,128)(2,1)S(1)}, bf16[704,128]{1,0:T(8,128)(2,1)S(1)}, u32[]{:S(2)}, u32[]{:S(2)}) %collective-permute-start.49) | collective-permute-done | bytes 180256 | tf_op jit(solution)/shard_map/ppermute | solution.py:909
  365.3 4.6 %collective-permute-done.51.three = bf16[704,128]{1,0:T(8,128)(2,1)S(1)} collective-permute-done((bf16[704,128]{1,0:T(8,128)(2,1)S(1)}, bf16[704,128]{1,0:T(8,128)(2,1)S(1)}, u32[]{:S(2)}, u32[]{:S(2)}) %collective-permute-start.51) | collective-permute-done | bytes 180256 | tf_op jit(solution)/shard_map/ppermute | solution.py:909
  371.8 2.4 shard_map.301
  (294 shorter events, 106.0 us)
Async XLA Ops:
  5.5 22.2 %collective-permute-start = (bf16[944,384]{1,0:T(8,128)(2,1)}, bf16[944,384]{1,0:T(8,128)(2,1)}, u32[]{:S(2)}, u32[]{:S(2)}) collective-permute-start(bf16[944,384]{1,0:T(8,128)(2,1)} %maximum_maximum_fusion.2.refs_0_), channel_id=1, source_target_pairs={{0,1},{1,0},{2,3},{3,2},{4,5},{5,4},{6,7},{7,6},{8,9},{9,8},{10,11... | collective-permute-start | bytes 2174984 | tf_op jit(solution)/shard_map/ppermute | solution.py:909
  8.4 19.2 %collective-permute-start.1 = (bf16[944,384]{1,0:T(8,128)(2,1)}, bf16[944,384]{1,0:T(8,128)(2,1)}, u32[]{:S(2)}, u32[]{:S(2)}) collective-permute-start(bf16[944,384]{1,0:T(8,128)(2,1)} %maximum_maximum_fusion.2.refs_0_), channel_id=1, source_target_pairs={{0,2},{1,3},{2,0},{3,1},{4,6},{5,7},{6,4},{7,5},{8,10},{9,11},{10,... | collective-permute-start | bytes 2174984 | tf_op jit(solution)/shard_map/ppermute | solution.py:909
  27.7 11.4 %collective-permute-start.7 = (bf16[416,384]{1,0:T(8,128)(2,1)S(1)}, bf16[416,384]{1,0:T(8,128)(2,1)S(1)}, u32[]{:S(2)}, u32[]{:S(2)}) collective-permute-start(bf16[416,384]{1,0:T(8,128)(2,1)S(1)} %get-tuple-element.113), channel_id=1, source_target_pairs={{0,3},{1,2},{2,1},{3,0},{4,7},{5,6},{6,5},{7,4},{8,11},{9,10},{10,... | collective-permute-start | bytes 958472 | tf_op jit(solution)/shard_map/ppermute | solution.py:909
  27.9 15.4 %collective-permute-start.8 = (bf16[416,384]{1,0:T(8,128)(2,1)S(1)}, bf16[416,384]{1,0:T(8,128)(2,1)S(1)}, u32[]{:S(2)}, u32[]{:S(2)}) collective-permute-start(bf16[416,384]{1,0:T(8,128)(2,1)S(1)} %get-tuple-element.114), channel_id=1, source_target_pairs={{0,2},{1,3},{2,0},{3,1},{4,6},{5,7},{6,4},{7,5},{8,10},{9,11},{10,... | collective-permute-start | bytes 958472 | tf_op jit(solution)/shard_map/ppermute | solution.py:909
  29.7 15.3 %collective-permute-start.9 = (bf16[416,384]{1,0:T(8,128)(2,1)S(1)}, bf16[416,384]{1,0:T(8,128)(2,1)S(1)}, u32[]{:S(2)}, u32[]{:S(2)}) collective-permute-start(bf16[416,384]{1,0:T(8,128)(2,1)S(1)} %get-tuple-element.115), channel_id=1, source_target_pairs={{0,1},{1,0},{2,3},{3,2},{4,5},{5,4},{6,7},{7,6},{8,9},{9,8},{10,11... | collective-permute-start | bytes 958472 | tf_op jit(solution)/shard_map/ppermute | solution.py:909
  32.4 27.0 %collective-permute-start.4 = (bf16[944,384]{1,0:T(8,128)(2,1)}, bf16[944,384]{1,0:T(8,128)(2,1)S(1)}, u32[]{:S(2)}, u32[]{:S(2)}) collective-permute-start(bf16[944,384]{1,0:T(8,128)(2,1)} %collective-permute-done.refs_1_), channel_id=1, source_target_pairs={{0,4},{4,0},{1,5},{5,1},{2,6},{6,2},{3,7},{7,3},{8,12},{12,8},{9,1... | collective-permute-start | bytes 2174984 | tf_op jit(solution)/shard_map/ppermute | solution.py:905
  32.4 27.3 %collective-permute-start.5 = (bf16[944,384]{1,0:T(8,128)(2,1)}, bf16[944,384]{1,0:T(8,128)(2,1)S(1)}, u32[]{:S(2)}, u32[]{:S(2)}) collective-permute-start(bf16[944,384]{1,0:T(8,128)(2,1)} %collective-permute-done.1.refs_2_), channel_id=1, source_target_pairs={{0,4},{4,0},{1,5},{5,1},{2,6},{6,2},{3,7},{7,3},{8,12},{12,8},{9,1... | collective-permute-start | bytes 2174984 | tf_op jit(solution)/shard_map/ppermute | solution.py:905
  39.0 12.0 %collective-permute-start.2 = (bf16[944,384]{1,0:T(8,128)(2,1)S(1)}, bf16[944,384]{1,0:T(8,128)(2,1)S(1)}, u32[]{:S(2)}, u32[]{:S(2)}) collective-permute-start(bf16[944,384]{1,0:T(8,128)(2,1)S(1)} %broadcast_select_fusion), channel_id=1, source_target_pairs={{0,2},{1,3},{2,0},{3,1},{4,5},{5,4},{6,7},{7,6},{8,10},{9,11},{10,... | collective-permute-start | bytes 2174984 | tf_op jit(solution)/shard_map/ppermute | solution.py:924
  51.1 29.3 %collective-permute-start.17 = (bf16[416,768]{1,0:T(8,128)(2,1)S(1)}, bf16[416,768]{1,0:T(8,128)(2,1)S(1)}, u32[]{:S(2)}, u32[]{:S(2)}) collective-permute-start(bf16[416,768]{1,0:T(8,128)(2,1)S(1)} %pad_maximum_fusion.4.refs_3_.refs_10_), channel_id=1, source_target_pairs={{0,1},{1,0},{2,3},{3,2},{4,5},{5,4},{6,7},{7,6},{8,9},{9,8},{10,11... | collective-permute-start | bytes 1916936 | tf_op jit(solution)/shard_map/ppermute | solution.py:909
  59.4 21.7 %collective-permute-start.18 = (bf16[416,768]{1,0:T(8,128)(2,1)S(1)}, bf16[416,768]{1,0:T(8,128)(2,1)S(1)}, u32[]{:S(2)}, u32[]{:S(2)}) collective-permute-start(bf16[416,768]{1,0:T(8,128)(2,1)S(1)} %pad_maximum_fusion.4.refs_3_.refs_10_), channel_id=1, source_target_pairs={{0,2},{1,3},{2,0},{3,1},{4,6},{5,7},{6,4},{7,5},{8,10},{9,11},{10,... | collective-permute-start | bytes 1916936 | tf_op jit(solution)/shard_map/ppermute | solution.py:909
  59.7 22.8 %collective-permute-start.13 = (bf16[416,768]{1,0:T(8,128)(2,1)S(1)}, bf16[416,768]{1,0:T(8,128)(2,1)}, u32[]{:S(2)}, u32[]{:S(2)}) collective-permute-start(bf16[416,768]{1,0:T(8,128)(2,1)S(1)} %pad_maximum_fusion.4.refs_3_.refs_10_), channel_id=1, source_target_pairs={{0,4},{4,0},{1,5},{5,1},{2,6},{6,2},{3,7},{7,3},{8,12},{12,8},{9,1... | collective-permute-start | bytes 1916936 | tf_op jit(solution)/shard_map/ppermute | solution.py:905
  78.7 17.4 %collective-permute-start.10 = (bf16[416,768]{1,0:T(8,128)(2,1)}, bf16[416,768]{1,0:T(8,128)(2,1)S(1)}, u32[]{:S(2)}, u32[]{:S(2)}) collective-permute-start(bf16[416,768]{1,0:T(8,128)(2,1)} %get-tuple-element.123.refs_1_.refs_6_), channel_id=1, source_target_pairs={{0,1},{1,0},{2,3},{3,2},{4,5},{5,4},{6,7},{7,6},{8,9},{9,8},{10,11... | collective-permute-start | bytes 1916936 | tf_op jit(solution)/shard_map/ppermute | solution.py:909
  80.4 16.4 %collective-permute-start.11 = (bf16[416,768]{1,0:T(8,128)(2,1)}, bf16[416,768]{1,0:T(8,128)(2,1)S(1)}, u32[]{:S(2)}, u32[]{:S(2)}) collective-permute-start(bf16[416,768]{1,0:T(8,128)(2,1)} %get-tuple-element.123.refs_1_.refs_6_), channel_id=1, source_target_pairs={{0,2},{1,3},{2,0},{3,1},{4,6},{5,7},{6,4},{7,5},{8,10},{9,11},{10,... | collective-permute-start | bytes 1916936 | tf_op jit(solution)/shard_map/ppermute | solution.py:909
  81.2 22.5 %collective-permute-start.22 = (bf16[416,768]{1,0:T(8,128)(2,1)S(1)}, bf16[416,768]{1,0:T(8,128)(2,1)S(1)}, u32[]{:S(2)}, u32[]{:S(2)}) collective-permute-start(bf16[416,768]{1,0:T(8,128)(2,1)S(1)} %broadcast_select_fusion.1), channel_id=1, source_target_pairs={{0,2},{1,3},{2,0},{3,1},{4,5},{5,4},{6,7},{7,6},{8,10},{9,11},{10,... | collective-permute-start | bytes 1916936 | tf_op jit(solution)/shard_map/ppermute | solution.py:924
  82.6 21.2 %collective-permute-start.19 = (bf16[416,768]{1,0:T(8,128)(2,1)S(1)}, bf16[416,768]{1,0:T(8,128)(2,1)S(1)}, u32[]{:S(2)}, u32[]{:S(2)}) collective-permute-start(bf16[416,768]{1,0:T(8,128)(2,1)S(1)} %collective-permute-done.17.refs_5_), channel_id=1, source_target_pairs={{0,4},{4,0},{1,5},{5,1},{2,6},{6,2},{3,7},{7,3},{8,12},{12,8},{9,1... | collective-permute-start | bytes 1916936 | tf_op jit(solution)/shard_map/ppermute | solution.py:905
  82.6 21.9 %collective-permute-start.20 = (bf16[416,768]{1,0:T(8,128)(2,1)S(1)}, bf16[416,768]{1,0:T(8,128)(2,1)S(1)}, u32[]{:S(2)}, u32[]{:S(2)}) collective-permute-start(bf16[416,768]{1,0:T(8,128)(2,1)S(1)} %collective-permute-done.18.refs_6_), channel_id=1, source_target_pairs={{0,4},{4,0},{1,5},{5,1},{2,6},{6,2},{3,7},{7,3},{8,12},{12,8},{9,1... | collective-permute-start | bytes 1916936 | tf_op jit(solution)/shard_map/ppermute | solution.py:905
  103.7 14.1 %collective-permute-start.23 = (bf16[416,768]{1,0:T(8,128)(2,1)S(1)}, bf16[416,768]{1,0:T(8,128)(2,1)S(1)}, u32[]{:S(2)}, u32[]{:S(2)}) collective-permute-start(bf16[416,768]{1,0:T(8,128)(2,1)S(1)} %collective-permute-done.22.refs_3_), channel_id=1, source_target_pairs={{0,4},{4,0},{1,5},{5,1},{2,6},{6,2},{3,7},{7,3},{8,12},{12,8},{9,1... | collective-permute-start | bytes 1916936 | tf_op jit(solution)/shard_map/ppermute | solution.py:905
  103.8 13.2 %collective-permute-start.14 = (bf16[416,768]{1,0:T(8,128)(2,1)S(1)}, bf16[416,768]{1,0:T(8,128)(2,1)S(1)}, u32[]{:S(2)}, u32[]{:S(2)}) collective-permute-start(bf16[416,768]{1,0:T(8,128)(2,1)S(1)} %broadcast_select_fusion.2), channel_id=1, source_target_pairs={{0,2},{1,3},{2,0},{3,1},{4,5},{5,4},{6,7},{7,6},{8,10},{9,11},{10,... | collective-permute-start | bytes 1916936 | tf_op jit(solution)/shard_map/ppermute | solution.py:924
  239.4 12.0 %collective-permute-start.31 = (bf16[832,768]{1,0:T(8,128)(2,1)}, bf16[832,768]{1,0:T(8,128)(2,1)}, u32[]{:S(2)}, u32[]{:S(2)}) collective-permute-start(bf16[832,768]{1,0:T(8,128)(2,1)} %get-tuple-element.152), channel_id=1, source_target_pairs={{0,4},{4,0},{1,5},{5,1},{2,6},{6,2},{3,7},{7,3},{8,12},{12,8},{9,1... | collective-permute-start | bytes 3833864 | tf_op jit(solution)/shard_map/ppermute | solution.py:905
  239.6 14.6 %collective-permute-start.30 = (bf16[832,768]{1,0:T(8,128)(2,1)}, bf16[832,768]{1,0:T(8,128)(2,1)}, u32[]{:S(2)}, u32[]{:S(2)}) collective-permute-start(bf16[832,768]{1,0:T(8,128)(2,1)} %get-tuple-element.150), channel_id=1, source_target_pairs={{0,4},{4,0},{1,5},{5,1},{2,6},{6,2},{3,7},{7,3},{8,12},{12,8},{9,1... | collective-permute-start | bytes 3833864 | tf_op jit(solution)/shard_map/ppermute | solution.py:905
  240.0 19.6 %collective-permute-start.26 = (bf16[832,896]{1,0:T(8,128)(2,1)S(1)}, bf16[832,896]{1,0:T(8,128)(2,1)}, u32[]{:S(2)}, u32[]{:S(2)}) collective-permute-start(bf16[832,896]{1,0:T(8,128)(2,1)S(1)} %add_convert_fusion), channel_id=1, source_target_pairs={{0,1},{1,0},{2,3},{3,2},{4,6},{5,7},{6,4},{7,5},{8,9},{9,8},{10,11... | collective-permute-start | bytes 4472840 | tf_op jit(solution)/shard_map/ppermute | solution.py:924
  262.2 11.6 %collective-permute-start.32 = (bf16[416,896]{1,0:T(8,128)(2,1)S(1)}, bf16[416,896]{1,0:T(8,128)(2,1)S(1)}, u32[]{:S(2)}, u32[]{:S(2)}) collective-permute-start(bf16[416,896]{1,0:T(8,128)(2,1)S(1)} %get-tuple-element.257), channel_id=1, source_target_pairs={{0,2},{1,3},{2,0},{3,1},{4,5},{5,4},{6,7},{7,6},{8,10},{9,11},{10,... | collective-permute-start | bytes 2236424 | tf_op jit(solution)/shard_map/ppermute | solution.py:924
  273.8 35.4 %collective-permute-start.36 = (bf16[416,768]{1,0:T(8,128)(2,1)}, bf16[416,768]{1,0:T(8,128)(2,1)S(1)}, u32[]{:S(2)}, u32[]{:S(2)}) collective-permute-start(bf16[416,768]{1,0:T(8,128)(2,1)} %get-tuple-element.168), channel_id=1, source_target_pairs={{0,2},{1,3},{2,0},{3,1},{4,5},{5,4},{6,7},{7,6},{8,10},{9,11},{10,... | collective-permute-start | bytes 1916936 | tf_op jit(solution)/shard_map/ppermute | solution.py:924
  274.5 34.7 %collective-permute-start.37 = (bf16[416,768]{1,0:T(8,128)(2,1)}, bf16[416,768]{1,0:T(8,128)(2,1)S(1)}, u32[]{:S(2)}, u32[]{:S(2)}) collective-permute-start(bf16[416,768]{1,0:T(8,128)(2,1)} %get-tuple-element.169), channel_id=1, source_target_pairs={{0,1},{1,0},{2,3},{3,2},{4,6},{5,7},{6,4},{7,5},{8,9},{9,8},{10,11... | collective-permute-start | bytes 1916936 | tf_op jit(solution)/shard_map/ppermute | solution.py:924
  275.7 33.5 %collective-permute-start.38 = (bf16[416,768]{1,0:T(8,128)(2,1)}, bf16[416,768]{1,0:T(8,128)(2,1)}, u32[]{:S(2)}, u32[]{:S(2)}) collective-permute-start(bf16[416,768]{1,0:T(8,128)(2,1)} %get-tuple-element.170), channel_id=1, source_target_pairs={{0,3},{1,2},{2,1},{3,0},{4,7},{5,6},{6,5},{7,4},{8,11},{9,10},{10,... | collective-permute-start | bytes 1916936 | tf_op jit(solution)/shard_map/ppermute | solution.py:924
  319.2 14.6 %collective-permute-start.41 = (bf16[1088,128]{1,0:T(8,128)(2,1)}, bf16[1088,128]{1,0:T(8,128)(2,1)S(1)}, u32[]{:S(2)}, u32[]{:S(2)}) collective-permute-start(bf16[1088,128]{1,0:T(8,128)(2,1)} %get-tuple-element.276), channel_id=1, source_target_pairs={{0,2},{1,3},{2,0},{3,1},{4,6},{5,7},{6,4},{7,5},{8,10},{9,11},{10,... | collective-permute-start | bytes 835592 | tf_op jit(solution)/shard_map/ppermute | solution.py:909
  320.6 13.3 %collective-permute-start.42 = (bf16[1088,128]{1,0:T(8,128)(2,1)S(1)}, bf16[1088,128]{1,0:T(8,128)(2,1)}, u32[]{:S(2)}, u32[]{:S(2)}) collective-permute-start(bf16[1088,128]{1,0:T(8,128)(2,1)S(1)} %get-tuple-element.275), channel_id=1, source_target_pairs={{0,3},{1,2},{2,1},{3,0},{4,7},{5,6},{6,5},{7,4},{8,11},{9,10},{10,... | collective-permute-start | bytes 835592 | tf_op jit(solution)/shard_map/ppermute | solution.py:909
  335.1 10.5 %collective-permute-start.43 = (bf16[272,128]{1,0:T(8,128)(2,1)S(1)}, bf16[272,128]{1,0:T(8,128)(2,1)S(1)}, u32[]{:S(2)}, u32[]{:S(2)}) collective-permute-start(bf16[272,128]{1,0:T(8,128)(2,1)S(1)} %get-tuple-element.303), channel_id=1, source_target_pairs={{0,8},{8,0},{16,24},{24,16},{1,9},{9,1},{17,25},{25,17},{2,10},{10... | collective-permute-start | bytes 208904 | tf_op jit(solution)/shard_map/ppermute | solution.py:959
  335.1 10.4 %collective-permute-start.44 = (bf16[272,128]{1,0:T(8,128)(2,1)S(1)}, bf16[272,128]{1,0:T(8,128)(2,1)S(1)}, u32[]{:S(2)}, u32[]{:S(2)}) collective-permute-start(bf16[272,128]{1,0:T(8,128)(2,1)S(1)} %get-tuple-element.305), channel_id=1, source_target_pairs={{0,16},{8,24},{16,0},{24,8},{1,17},{9,25},{17,1},{25,9},{2,18},{10... | collective-permute-start | bytes 208904 | tf_op jit(solution)/shard_map/ppermute | solution.py:959
  343.4 26.7 %collective-permute-start.53 = (bf16[416,384]{1,0:T(8,128)(2,1)S(1)}, bf16[416,384]{1,0:T(8,128)(2,1)S(1)}, u32[]{:S(2)}, u32[]{:S(2)}) collective-permute-start(bf16[416,384]{1,0:T(8,128)(2,1)S(1)} %get-tuple-element.269), channel_id=1, source_target_pairs={{0,1},{1,0},{2,3},{3,2},{4,5},{5,4},{6,7},{7,6},{8,9},{9,8},{10,11... | collective-permute-start | bytes 958472 | tf_op jit(solution)/shard_map/ppermute | solution.py:909
  344.9 25.2 %collective-permute-start.54 = (bf16[416,384]{1,0:T(8,128)(2,1)S(1)}, bf16[416,384]{1,0:T(8,128)(2,1)S(1)}, u32[]{:S(2)}, u32[]{:S(2)}) collective-permute-start(bf16[416,384]{1,0:T(8,128)(2,1)S(1)} %get-tuple-element.268), channel_id=1, source_target_pairs={{0,2},{1,3},{2,0},{3,1},{4,6},{5,7},{6,4},{7,5},{8,10},{9,11},{10,... | collective-permute-start | bytes 958472 | tf_op jit(solution)/shard_map/ppermute | solution.py:909
  351.8 18.3 %collective-permute-start.55 = (bf16[416,384]{1,0:T(8,128)(2,1)S(1)}, bf16[416,384]{1,0:T(8,128)(2,1)S(1)}, u32[]{:S(2)}, u32[]{:S(2)}) collective-permute-start(bf16[416,384]{1,0:T(8,128)(2,1)S(1)} %get-tuple-element.266), channel_id=1, source_target_pairs={{0,3},{1,2},{2,1},{3,0},{4,7},{5,6},{6,5},{7,4},{8,11},{9,10},{10,... | collective-permute-start | bytes 958472 | tf_op jit(solution)/shard_map/ppermute | solution.py:909
  (63 other events, 378.0 us)

commit v2 on v1

--- a/solution.py
+++ b/solution.py
@@ -126,9 +126,9 @@
     refs = refs[: n + 4] + refs[n + 12 :]
     (
         w_up_hbm, w_down_hbm, b_up, a_down,
-        gbu_out, gad_out,
+        gbu_bf, gad_bf,
         table, acc_e, acc_t, in_x, in_c, out_e, out_t, xb, cb, w_up, w_down, stage_ep, stage_tg,
-        in_sem, up_sem, down_sem, ep_sem, tg_sem,
+        gbu_out, gad_out, in_sem, up_sem, down_sem, ep_sem, tg_sem,
     ) = refs[n:]
     acc_e_flat = acc_e.reshape(TOK * 8, 128)
     acc_t_flat = acc_t.reshape(TOK * 8, 128)
@@ -239,6 +239,8 @@
     lax.fori_loop(0, n_tiles, tile, 0)
     give(n_tiles - 1)
 
+    gbu_bf[...] = gbu_out[...].astype(bf16)
+    gad_bf[...] = gad_out[...].astype(bf16)
     some = IMG_GRP // 4
     for side, (ep_out, tg_out) in enumerate(zip(ep_outs, tg_outs)):
 
@@ -305,6 +307,8 @@
                 pltpu.VMEM((2, half, D), bf16),
                 pltpu.VMEM((2, SEQP, D), bf16),
                 pltpu.VMEM((2, SEQP, D + 128), bf16),
+                pltpu.VMEM((half, ADAPT), f32),
+                pltpu.VMEM((half, ADAPT), f32),
                 pltpu.SemaphoreType.DMA((n_copies,)),
                 pltpu.SemaphoreType.DMA((2,)),
                 pltpu.SemaphoreType.DMA((2,)),
@@ -315,8 +319,8 @@
         out_shape=[
             *[jax.ShapeDtypeStruct((TOK // 4, D), bf16)] * 4,
             *[jax.ShapeDtypeStruct((TOK // 4, D + 128), bf16)] * 4,
-            jax.ShapeDtypeStruct((half, ADAPT), f32),
-            jax.ShapeDtypeStruct((half, ADAPT), f32),
+            jax.ShapeDtypeStruct((half, ADAPT), bf16),
+            jax.ShapeDtypeStruct((half, ADAPT), bf16),
         ],
         compiler_params=pltpu.CompilerParams(vmem_limit_bytes=58 * 1024 * 1024),
         cost_estimate=pl.CostEstimate(flops=20_000_000_000, bytes_accessed=60_000_000, transcendentals=10_000_000),
@@ -546,7 +550,7 @@
             ],
         ),
         out_shape=[jax.ShapeDtypeStruct(shape, f32) for shape in shapes],
-        compiler_params=pltpu.CompilerParams(vmem_limit_bytes=32 * 1024 * 1024),
+        compiler_params=pltpu.CompilerParams(vmem_limit_bytes=60 * 1024 * 1024),
         cost_estimate=pl.CostEstimate(flops=1_000_000_000, bytes_accessed=4_000_000, transcendentals=0),
     )(place, mine, *got, far, dp_sums)
 
@@ -588,7 +592,7 @@
             ],
         ),
         out_shape=[jax.ShapeDtypeStruct((rows, width), bf16), jax.ShapeDtypeStruct((rows, width), f32)],
-        compiler_params=pltpu.CompilerParams(vmem_limit_bytes=32 * 1024 * 1024),
+        compiler_params=pltpu.CompilerParams(vmem_limit_bytes=60 * 1024 * 1024),
         cost_estimate=pl.CostEstimate(flops=8_000_000_000, bytes_accessed=3_000_000, transcendentals=0),
     )(place, *blocks)
 
@@ -616,6 +620,20 @@
                 a_out[down, :] = blocks[4][W_ROWS + 384 : W_ROWS + 512, 128 * p : 128 * p + 128]
 
 
+def two_masks(picks_ref):
+    row = lax.broadcasted_iota(jnp.int32, (BLK, 1), 0)
+    pick = jnp.where(row < SEQP, picks_ref[0], picks_ref[1])
+    return (lane_iota((1, ADAPT)) // RANK) == pick, (row < SEQ) | ((row >= SEQP) & (row < SEQP + SEQ))
+
+
+def both_heads(value):
+    lane = lane_iota((1, 128))
+    nothing = jnp.zeros_like(value)
+    return jnp.concatenate(
+        [jnp.where(lane < HEAD_DIM, value, nothing), jnp.where(lane < HEAD_DIM, nothing, value)], axis=0
+    )
+
+
 def attend_kernel(picks_ref, place_ref, *refs):
     blocks, refs = refs[:8], refs[8:]
     (
@@ -623,13 +641,8 @@
         two_out, resid_out, normed_out, qkv_out, mixed_out, probs_out, lows_out,
         w_qkv, a_qkv, b_qkv, w_out, a_out,
     ) = refs
-    image = pl.program_id(0)
-
-    @pl.when(image == 0)
-    def start():
-        place_weights(place_ref, blocks, own_b, own_a, (out_near, out_far), w_qkv, a_qkv, b_qkv, w_out, a_out)
-
-    mask = pick_mask(picks_ref[image])
+    place_weights(place_ref, blocks, own_b, own_a, (out_near, out_far), w_qkv, a_qkv, b_qkv, w_out, a_out)
+    mask, real = two_masks(picks_ref)
     x = x_ref[...].astype(f32)
     unit, unused = norm_stats(x)
     normed = (unit * gain_one[...]).astype(bf16)
@@ -642,39 +655,27 @@
     key_lane = lane_iota((1, SEQP))
     for pair in range(HEADS // 2):
         at = slice(128 * pair, 128 * pair + 128)
-        q = qkv_out[0, :, at]
-        k = qkv_out[1, :, at]
-        v = qkv_out[2, :, at]
-        parts = []
-        for side in range(2):
-            own = (lane // HEAD_DIM) == side
-            scores = dot_nt(jnp.where(own, q, jnp.zeros_like(q)), k) * (HEAD_DIM**-0.5)
+        for image in range(2):
+            rows = slice(SEQP * image, SEQP * image + SEQP)
+            scores = dot_nt(both_heads(qkv_out[0, rows, at]), qkv_out[1, rows, at]) * (HEAD_DIM**-0.5)
             scores = jnp.where(key_lane < SEQ, scores, -1e30)
             power = jnp.exp(scores - jnp.max(scores, axis=1, keepdims=True))
             probs = (power / jnp.sum(power, axis=1, keepdims=True)).astype(bf16)
-            probs_out[0, 2 * pair + side] = probs
-            parts.append(dot(probs, v))
-        mixed_out[:, at] = jnp.where(lane < HEAD_DIM, parts[0], parts[1]).astype(bf16)
+            probs_out[image, pair] = probs
+            found = dot(probs, qkv_out[2, rows, at])
+            mixed_out[rows, at] = jnp.where(lane < HEAD_DIM, found[:SEQP], found[SEQP:]).astype(bf16)
     mixed = mixed_out[...]
     low = jnp.where(mask, dot(mixed, a_out[...]), 0.0).astype(bf16)
     lows_out[:, 384:512] = low
     resid = x + dot(mixed, w_out[...]) + dot(low, b_out[...])
     resid_out[...] = resid
     unit, unused = norm_stats(resid)
-    real = lax.broadcasted_iota(jnp.int32, (SEQP, 1), 0) < SEQ
     two_out[...] = jnp.where(real, unit * gain_two[...], 0.0).astype(bf16)
 
 
-def image_rows(lanes):
-    return pl.BlockSpec((SEQP, lanes), lambda i, *_: (i, 0))
-
-
-def kept(*shape):
-    return pl.BlockSpec(shape, lambda i, *_: (0,) * len(shape))
-
-
-QKV_SPEC = pl.BlockSpec((3, SEQP, D), lambda i, *_: (0, i, 0))
-PROBS_SPEC = pl.BlockSpec((1, HEADS, SEQP, SEQP), lambda i, *_: (i, 0, 0, 0))
+INSIDE = pl.BlockSpec(memory_space=pltpu.VMEM)
+
+
 ANYWHERE = pl.BlockSpec(memory_space=pl.ANY)
 
 
@@ -684,13 +685,9 @@
         attend_kernel,
         grid_spec=pltpu.PrefetchScalarGridSpec(
             num_scalar_prefetch=2,
-            grid=(2,),
-            in_specs=[kept(*block.shape) for block in (*blocks, own_b, own_a, *out_w)]
-            + [image_rows(D), kept(1, D), kept(1, D), kept(ADAPT, D)],
-            out_specs=[
-                image_rows(D), image_rows(D), image_rows(D), QKV_SPEC,
-                image_rows(D), PROBS_SPEC, image_rows(512),
-            ],
+            grid=(1,),
+            in_specs=[INSIDE] * (len(blocks) + 8),
+            out_specs=[INSIDE] * 7,
             scratch_shapes=QKV_SCRATCH[:-1] + OUT_SCRATCH[:-1],
         ),
         out_shape=[
@@ -699,10 +696,10 @@
             jax.ShapeDtypeStruct((rows, D), bf16),
             jax.ShapeDtypeStruct((3, rows, D), bf16),
             jax.ShapeDtypeStruct((rows, D), bf16),
-            jax.ShapeDtypeStruct((2, HEADS, SEQP, SEQP), bf16),
+            jax.ShapeDtypeStruct((2, HEADS // 2, BLK, SEQP), bf16),
             jax.ShapeDtypeStruct((rows, 512), bf16),
         ],
-        compiler_params=pltpu.CompilerParams(vmem_limit_bytes=60 * 1024 * 1024),
+        compiler_params=pltpu.CompilerParams(vmem_limit_bytes=48 * 1024 * 1024),
         cost_estimate=pl.CostEstimate(flops=4_000_000_000, bytes_accessed=15_000_000, transcendentals=2_000_000),
     )(picks, place, *blocks, own_b, own_a, *out_w, x, gain_one, gain_two, b_out)
 
@@ -712,26 +709,16 @@
         far_block, own_a, out_near, out_far, gain_two, b_out, two_ref, resid_ref, mixed_ref, lows_ref,
         cot_ref, grad_a, grad_b, w_router, a_router, b_router, a_up, b_down,
         resid_grad_out, mixed_grad_out, base_out, both_out, a_part_out, b_part_out,
-        w_out, a_out, sem, both, a_part, b_part,
+        w_out, a_out, sem,
     ) = refs
-    image = pl.program_id(0)
-
-    @pl.when(image == 0)
-    def start():
-        copies = out_copies(place_ref, far_block, own_a, (out_near, out_far), (w_out, a_out), sem)
-        for copy in copies:
-            copy.start()
-        for part in (both, a_part, b_part):
-            part[...] = jnp.zeros_like(part)
-        for copy in copies:
-            copy.wait()
-
-    mask = pick_mask(picks_ref[image])
+    copies = out_copies(place_ref, far_block, own_a, (out_near, out_far), (w_out, a_out), sem)
+    for copy in copies:
+        copy.start()
+    mask, unused = two_masks(picks_ref)
     lane = lane_iota((1, 128))
 
     def add_part(row, value):
-        at = slice(row, row + value.shape[0])
-        both[at, :] += value
+        both_out[row : row + value.shape[0], :] = value.astype(bf16)
 
     two = two_ref[...]
     received = grad_a[...].astype(f32) + grad_b[...].astype(f32)
@@ -761,15 +748,12 @@
     resid_grad_out[...] = grad_resid
     grad_attn = grad_resid.astype(bf16)
     grad_low = jnp.where(mask, dot_nt(grad_attn, b_out[...]), 0.0).astype(bf16)
+    for copy in copies:
+        copy.wait()
     mixed_grad_out[...] = (dot_nt(grad_attn, w_out[...]) + dot_nt(grad_low, a_out[...])).astype(bf16)
-    a_part[...] += dot_tn(mixed_ref[...], grad_low)
-    b_part[...] += dot_tn(grad_attn, lows_ref[:, 384:512])
-
-    @pl.when(image == 1)
-    def finish():
-        both_out[...] = both[...].astype(bf16)
-        a_part_out[...] = a_part[...].astype(bf16)
-        b_part_out[...] = b_part[...].astype(bf16)
+    a_part_out[...] = dot_tn(mixed_ref[...], grad_low).astype(bf16)
+    b_part_out[...] = dot_tn(grad_attn, lows_ref[:, 384:512]).astype(bf16)
+    both_out[2432:BOTH_ROWS, :] = jnp.zeros((BOTH_ROWS - 2432, 128), bf16)
 
 
 BOTH_ROWS = 2560
@@ -782,14 +766,10 @@
         out_back_kernel,
         grid_spec=pltpu.PrefetchScalarGridSpec(
             num_scalar_prefetch=2,
-            grid=(2,),
-            in_specs=[ANYWHERE] * 4
-            + [kept(1, D), kept(ADAPT, D), image_rows(D), image_rows(D), image_rows(D), image_rows(512)]
-            + [image_rows(D), image_rows(D + 128), image_rows(D + 128)]
-            + [kept(D, 128), kept(D, ADAPT), kept(ADAPT, 128), kept(D, ADAPT), kept(ADAPT, D)],
-            out_specs=[image_rows(D), image_rows(D), image_rows(D), kept(BOTH_ROWS, 128), kept(D, 128), kept(D, 128)],
-            scratch_shapes=OUT_SCRATCH
-            + [pltpu.VMEM((BOTH_ROWS, 128), f32), pltpu.VMEM((D, 128), f32), pltpu.VMEM((D, 128), f32)],
+            grid=(1,),
+            in_specs=[ANYWHERE] * 4 + [INSIDE] * 14,
+            out_specs=[INSIDE] * 6,
+            scratch_shapes=OUT_SCRATCH,
         ),
         out_shape=[
             jax.ShapeDtypeStruct((rows, D), f32),
@@ -810,64 +790,39 @@
     (
         own_b, x_ref, gain_one, normed_ref, qkv_ref, probs_ref, lows_ref, resid_grad, grad_mixed,
         tokens_out, a_part_out, b_part_out,
-        w_qkv, a_qkv, b_qkv, sem, a_part, b_part, grads,
+        w_qkv, a_qkv, b_qkv, sem, grads,
     ) = refs
-    image = pl.program_id(0)
     copies = qkv_copies(place_ref, blocks, own_b, (w_qkv, a_qkv, b_qkv), sem)
-
-    @pl.when(image == 0)
-    def start():
-        for copy in copies:
-            copy.start()
-        a_part[...] = jnp.zeros_like(a_part)
-        b_part[...] = jnp.zeros_like(b_part)
-
-    mask = pick_mask(picks_ref[image])
+    for copy in copies:
+        copy.start()
+    mask, unused = two_masks(picks_ref)
     lane = lane_iota((1, 128))
     for pair in range(HEADS // 2):
         at = slice(128 * pair, 128 * pair + 128)
-        q = qkv_ref[0, :, at]
-        k = qkv_ref[1, :, at]
-        v = qkv_ref[2, :, at]
-        gm = grad_mixed[:, at]
-        found = []
-        for side in range(2):
-            own = (lane // HEAD_DIM) == side
-            weights = probs_ref[0, 2 * pair + side]
+        for image in range(2):
+            rows = slice(SEQP * image, SEQP * image + SEQP)
+            grad_out = both_heads(grad_mixed[rows, at])
+            weights = probs_ref[image, pair]
             weights_f = weights.astype(f32)
-            grad_w = dot_nt(jnp.where(own, gm, jnp.zeros_like(gm)), v)
+            grad_w = dot_nt(grad_out, qkv_ref[2, rows, at])
             inner = jnp.sum(weights_f * grad_w, axis=1, keepdims=True)
-            grad_s = (weights_f * (grad_w - inner)).astype(bf16)
-            found.append(
-                (
-                    dot(grad_s, k) * (HEAD_DIM**-0.5),
-                    dot_tn(grad_s, q) * (HEAD_DIM**-0.5),
-                    dot_tn(weights, gm),
-                )
-            )
-        for p in range(3):
-            grads[p, :, at] = jnp.where(lane < HEAD_DIM, found[0][p], found[1][p]).astype(bf16)
-
-    @pl.when(image == 0)
-    def arrived():
-        for copy in copies:
-            copy.wait()
-
+            grad_s = (weights_f * (grad_w - inner) * (HEAD_DIM**-0.5)).astype(bf16)
+            found = dot(grad_s, qkv_ref[1, rows, at])
+            grads[0, rows, at] = jnp.where(lane < HEAD_DIM, found[:SEQP], found[SEQP:]).astype(bf16)
+            grads[1, rows, at] = dot_tn(grad_s, both_heads(qkv_ref[0, rows, at])).astype(bf16)
+            grads[2, rows, at] = dot_tn(weights, grad_out).astype(bf16)
+    for copy in copies:
+        copy.wait()
     normed = normed_ref[...]
-    grad_normed = jnp.zeros((SEQP, D), f32)
+    grad_normed = jnp.zeros((BLK, D), f32)
     for p in range(3):
         piece = grads[p]
         grad_low = jnp.where(mask, dot_nt(piece, b_qkv[p]), 0.0).astype(bf16)
         grad_normed = grad_normed + dot_nt(piece, w_qkv[p]) + dot_nt(grad_low, a_qkv[p])
-        a_part[D * p : D * p + D, :] += dot_tn(normed, grad_low)
-        b_part[D * p : D * p + D, :] += dot_tn(piece, lows_ref[:, 128 * p : 128 * p + 128])
+        a_part_out[D * p : D * p + D, :] = dot_tn(normed, grad_low).astype(bf16)
+        b_part_out[D * p : D * p + D, :] = dot_tn(piece, lows_ref[:, 128 * p : 128 * p + 128]).astype(bf16)
     unit, inverse = norm_stats(x_ref[...].astype(f32))
     tokens_out[...] = (resid_grad[...] + norm_back(grad_normed, gain_one[...], unit, inverse)).astype(bf16)
-
-    @pl.when(image == 1)
-    def finish():
-        a_part_out[...] = a_part[...].astype(bf16)
-        b_part_out[...] = b_part[...].astype(bf16)
 
 
 def qkv_back_call(picks, place, blocks, own_b, x, gain_one, normed, qkv, probs, lows, resid_grad, grad_mixed):
@@ -876,24 +831,17 @@
         qkv_back_kernel,
         grid_spec=pltpu.PrefetchScalarGridSpec(
             num_scalar_prefetch=2,
-            grid=(2,),
-            in_specs=[ANYWHERE] * (len(blocks) + 1)
-            + [image_rows(D), kept(1, D), image_rows(D), QKV_SPEC, PROBS_SPEC, image_rows(512)]
-            + [image_rows(D), image_rows(D)],
-            out_specs=[image_rows(D), kept(3 * D, 128), kept(3 * D, 128)],
-            scratch_shapes=QKV_SCRATCH
-            + [
-                pltpu.VMEM((3 * D, 128), f32),
-                pltpu.VMEM((3 * D, 128), f32),
-                pltpu.VMEM((3, SEQP, D), bf16),
-            ],
+            grid=(1,),
+            in_specs=[ANYWHERE] * (len(blocks) + 1) + [INSIDE] * 8,
+            out_specs=[INSIDE] * 3,
+            scratch_shapes=QKV_SCRATCH + [pltpu.VMEM((3, BLK, D), bf16)],
         ),
         out_shape=[
             jax.ShapeDtypeStruct((rows, D), bf16),
             jax.ShapeDtypeStruct((3 * D, 128), bf16),
             jax.ShapeDtypeStruct((3 * D, 128), bf16),
         ],
-        compiler_params=pltpu.CompilerParams(vmem_limit_bytes=60 * 1024 * 1024),
+        compiler_params=pltpu.CompilerParams(vmem_limit_bytes=44 * 1024 * 1024),
         cost_estimate=pl.CostEstimate(flops=9_000_000_000, bytes_accessed=15_000_000, transcendentals=1000),
     )(picks, place, *blocks, own_b, x, gain_one, normed, qkv, probs, lows, resid_grad, grad_mixed)
 
@@ -1077,7 +1025,7 @@
         token_list, tile_experts, spot_picks, place, tables, TABLES, w_up, w_down, b_up, a_down
     )
     sums, grads = moved[:4], moved[4:]
-    dp_parts = jnp.concatenate([part_b_up.astype(bf16), part_a_down.astype(bf16)])
+    dp_parts = jnp.concatenate([part_b_up, part_a_down])
     grad_sent = added(grads[1], across_row(grads[3])).astype(bf16)
     grad_kept = added(grads[0], across_row(grads[2])).astype(bf16)
     grad_sent, dp_parts, *sums = lax.optimization_barrier((grad_sent, dp_parts, *sums))

time: 385 us -> 392 us (1.018)
  local copies, waits for them, and re-layouts: 23.9 us -> 35.3 us
  starting transfers between devices: 52 us -> 63.1 us
  Pallas kernels: 180 us -> 172 us
    unnamed x93 -> x143, local copies, waits for them, and re-layouts: 17 us -> 29.5 us
    ppermute x12, starting transfers between devices: 17.9 us -> 28.1 us  [across_dp(): return lax.ppermute(value, 'dp', [(i, i ^ step) for i in range(4)])]
    ppermute x8, waiting for transfers between devices: 16.7 us -> 9.95 us  [across_chip(): return lax.ppermute(value, ('row', 'col'), pairs)]
    pallas_call x1, Pallas kernels: 19.7 us -> 15.2 us  [qkv_back_call(): pl.pallas_call(qkv_back_kernel, grid_spec=pltpu.PrefetchScalarGridSpec(nu...]
  transfers between devices with their start and end apart: 56 -> 56, of which waited for: 23 -> 23; matrix products, arithmetic and copies ran while one was open for 12% -> 12% of each run, Pallas kernels for 17% -> 15%
where the time goes in v2:
time: 392 us; the launch traced here: 388 us
  Pallas kernels  172 us (44%)
  waiting for transfers between devices  69.3 us (18%)
  starting transfers between devices  63.1 us (16%)
  other arithmetic  46.2 us (12%)
  local copies, waits for them, and re-layouts  35.3 us (9%)
    pallas_call x1, Pallas kernels, moe_call(): pl.pallas_call(lambda *refs: moe_kernel(places, *refs), grid_spec=pltpu.P...  104 us
    ppermute x18, waiting for transfers between devices, across_col(): return lax.ppermute(value, 'col', [(i, i ^ step) for i in range(4)])  42.6 us
    unnamed x143, local copies, waits for them, and re-layouts  29.5 us
    ppermute x12, starting transfers between devices, across_dp(): return lax.ppermute(value, 'dp', [(i, i ^ step) for i in range(4)])  28.1 us
    ppermute x18, starting transfers between devices, across_col(): return lax.ppermute(value, 'col', [(i, i ^ step) for i in range(4)])  23.2 us
    pallas_call x3, Pallas kernels, table_call(): pl.pallas_call(lambda *refs: table_kernel(n, *refs), grid_spec=pltpu.Pref...  20.1 us
    pallas_call x1, Pallas kernels, qkv_back_call(): pl.pallas_call(qkv_back_kernel, grid_spec=pltpu.PrefetchScalarGridSpec(nu...  15.2 us
    pallas_call x1, Pallas kernels, attend_call(): pl.pallas_call(attend_kernel, grid_spec=pltpu.PrefetchScalarGridSpec(num_...  13.4 us
  transfers between devices with their start and end apart: 56, of which 23 were waited for; matrix products, arithmetic and copies ran while one was open for 12% of the time, Pallas kernels for 15%

profile of v2, /device:TPU:0, one launch (start us, length us, event | category | flops | bytes accessed | tf_op | source)
XLA Modules:
  0.0 387.8 jit_solution(9872036355435532403)
XLA Ops:
  6.2 2.9 collective-permute-start
  23.3 8.6 %sort.14 = (s32[14592]{0:T(1024)S(1)}, s32[14592]{0:T(1024)}) sort(s32[14592]{0:T(1024)} %pad_add_fusion, s32[14592]{0:T(1024)S(1)} %iota.71), dimensions={0}, to_apply=%region_1.2 | sort | flops 204288 | bytes 233472 | tf_op jit(solution)/shard_map/sort | solution.py:355
  38.8 6.2 %collective-permute-done.7 = bf16[416,384]{1,0:T(8,128)(2,1)S(1)} collective-permute-done((bf16[416,384]{1,0:T(8,128)(2,1)}, bf16[416,384]{1,0:T(8,128)(2,1)S(1)}, u32[]{:S(2)}, u32[]{:S(2)}) %collective-permute-start.7) | collective-permute-done | bytes 319520 | tf_op jit(solution)/shard_map/ppermute | solution.py:857
  45.5 3.8 collective-permute-done.8
  53.4 3.6 collective-permute-done.2.refs_3_
  65.1 13.4 %shard_map.293 = (bf16[416,768]{1,0:T(8,128)(2,1)S(1)}, f32[416,768]{1,0:T(8,128)}, bf16[416,768]{1,0:T(8,128)(2,1)S(1)}, bf16[3,416,768]{2,1,0:T(8,128)(2,1)}, ...) custom-call(s32[16]{0:T(128)S(1)} %and_select_fusion.5.picks_ref, ...), custom_call_target="tpu_custom_call" | custom-call | flops 4000000000 | bytes 15000000 | tf_op jit(solution)/shard_map/pallas_call | solution.py:684
  83.7 5.2 %shard_map.294.refs_4_ = bf16[832,16,128]{2,1,0:T(8,128)(2,1)S(1)} custom-call(s32[4]{0:T(128)S(1)} %pad_add_fusion.3.refs_0_, bf16[416,768]{1,0:T(8,128)(2,1)S(1)} %get-tuple-element.123.refs_1_.refs_6_, bf16[416,768]{1,0:T(8,128)(2,1)S(1)} %collective-permute-done.12.refs_2_, bf16[416,768]{1,0:T(8,128)(2,1)S(1)} %pad_maximum_fusion.4.refs_3_.refs_10_, ...), custom_call_target="tpu_custom_call" | custom-call | flops 6000000000 | bytes 6000000 | tf_op jit(solution)/shard_map/pallas_call | solution.py:100
  88.9 7.9 %collective-permute-done.10.refs_1_ = bf16[416,768]{1,0:T(8,128)(2,1)S(1)} collective-permute-done((bf16[416,768]{1,0:T(8,128)(2,1)S(1)}, bf16[416,768]{1,0:T(8,128)(2,1)S(1)}, u32[]{:S(2)}, u32[]{:S(2)}) %collective-permute-start.10) | collective-permute-done | bytes 639008 | tf_op jit(solution)/shard_map/ppermute | solution.py:857
  97.8 6.2 %collective-permute-done.22.refs_3_ = bf16[416,768]{1,0:T(8,128)(2,1)S(1)} collective-permute-done((bf16[416,768]{1,0:T(8,128)(2,1)S(1)}, bf16[416,768]{1,0:T(8,128)(2,1)S(1)}, u32[]{:S(2)}, u32[]{:S(2)}) %collective-permute-start.22) | collective-permute-done | bytes 639008 | tf_op jit(solution)/shard_map/ppermute | solution.py:872
  105.0 9.8 %shard_map.295.refs_5_ = bf16[1664,16,128]{2,1,0:T(8,128)(2,1)S(1)} custom-call(s32[8]{0:T(128)S(1)} %pad_add_fusion.4.refs_0_, bf16[416,768]{1,0:T(8,128)(2,1)S(1)} %collective-permute-done.10.refs_1_, bf16[416,768]{1,0:T(8,128)(2,1)S(1)} %collective-permute-done.11.refs_2_, bf16[416,768]{1,0:T(8,128)(2,1)S(1)} %collective-permute-done.15.refs_3_, ...), custom_call_target="tpu_custom_call" | custom-call | flops 12000000000 | bytes 12000000 | tf_op jit(solution)/shard_map/pallas_call | solution.py:100
  114.8 2.8 copy-done.30
  119.7 5.1 %shard_map.296.refs_6_ = bf16[832,16,128]{2,1,0:T(8,128)(2,1)S(1)} custom-call(s32[4]{0:T(128)S(1)} %pad_add_fusion.5.refs_0_, bf16[416,768]{1,0:T(8,128)(2,1)S(1)} %collective-permute-done.14.refs_1_, bf16[416,768]{1,0:T(8,128)(2,1)S(1)} %collective-permute-done.21.refs_2_, bf16[416,768]{1,0:T(8,128)(2,1)S(1)} %collective-permute-done.22.refs_3_, ...), custom_call_target="tpu_custom_call" | custom-call | flops 6000000000 | bytes 6000000 | tf_op jit(solution)/shard_map/pallas_call | solution.py:100
  126.6 103.9 %shard_map.297 = (bf16[832,768]{1,0:T(8,128)(2,1)}, bf16[832,768]{1,0:T(8,128)(2,1)}, bf16[832,768]{1,0:T(8,128)(2,1)}, bf16[832,768]{1,0:T(8,128)(2,1)}, bf16[8...) custom-call(s32[14592]{0:T(1024)} %broadcast_and_fusion.refs_0_, ...), custom_call_target="tpu_custom_call" | custom-call | flops 20000000000 | bytes 60000000 | tf_op jit(solution)/shard_map/pallas_call | solution.py:289
  234.0 2.9 add_convert_fusion
  238.6 9.2 %collective-permute-start.27 = (bf16[192,128]{1,0:T(8,128)(2,1)S(1)}, bf16[192,128]{1,0:T(8,128)(2,1)S(1)}, u32[]{:S(2)}, u32[]{:S(2)}) collective-permute-start(bf16[192,128]{1,0:T(8,128)(2,1)S(1)} %get-tuple-element.328), channel_id=1, source_target_pairs={{0,8},{8,0},{16,24},{24,16},{1,9},{9,1},{17,25},{25,17},{2,10},{10... | collective-permute-start | bytes 147464 | tf_op jit(solution)/shard_map/ppermute | solution.py:907
  253.1 2.7 collective-permute-done.29
  255.9 2.8 add_convert_fusion.6
  258.7 2.7 add_convert_fusion.8
  261.3 2.8 add_convert_fusion.3
  266.4 4.7 %collective-permute-start.34 = (bf16[192,128]{1,0:T(8,128)(2,1)S(1)}, bf16[192,128]{1,0:T(8,128)(2,1)S(1)}, u32[]{:S(2)}, u32[]{:S(2)}) collective-permute-start(bf16[192,128]{1,0:T(8,128)(2,1)S(1)} %fusion.9), channel_id=1, source_target_pairs={{0,16},{8,24},{16,0},{24,8},{1,17},{9,25},{17,1},{25,9},{2,18},{10... | collective-permute-start | bytes 147464 | tf_op jit(solution)/shard_map/ppermute | solution.py:907
  271.1 3.5 collective-permute-done.34
  279.6 9.4 %shard_map.298 = (f32[416,768]{1,0:T(8,128)}, bf16[416,768]{1,0:T(8,128)(2,1)}, f32[416,768]{1,0:T(8,128)}, bf16[2560,128]{1,0:T(8,128)(2,1)}, bf16[768,128]{1,0:T(8,128)(2,1)}, /*index=5*/bf16[768,128]{1,0:T(8,128)(2,1)}) custom-call(s32[16]{0:T(128)} %copy-done.13, s32[2]{0:T(128)} %copy-done.23, bf16[1456,384]{1,0:T(8,128)(2,1)} %copy-done.52, ...), custom_call_target="tpu_custom_call" | custom-call | flops 6000000000 | bytes 15000000 | tf_op jit(solution)/shard_map/pallas_call | solution.py:765
  296.7 15.2 %shard_map.299 = (bf16[416,768]{1,0:T(8,128)(2,1)S(1)}, bf16[2304,128]{1,0:T(8,128)(2,1)S(1)}, bf16[2304,128]{1,0:T(8,128)(2,1)S(1)}) custom-call(s32[16]{0:T(128)S(1)} %copy-done.14, s32[2]{0:T(128)S(1)} %copy-done.24, bf16[944,384]{1,0:T(8,128)(2,1)} %maximum_maximum_fusion.2.refs_0_, bf16[944,384]{1,0:T(8,128)(2,1)S(1)} %collective-permute-done.refs_1_, ...), custom_call_target="tpu_custom_call" | custom-call | flops 8999999488 | bytes 15000000 | tf_op jit(solution)/shard_map/pallas_call | solution.py:830
  313.4 2.8 collective-permute-done.39
  322.1 6.2 %collective-permute-done.40 = bf16[1088,128]{1,0:T(8,128)(2,1)S(1)} collective-permute-done((bf16[1088,128]{1,0:T(8,128)(2,1)}, bf16[1088,128]{1,0:T(8,128)(2,1)S(1)}, u32[]{:S(2)}, u32[]{:S(2)}) %collective-permute-start.40) | collective-permute-done | bytes 278560 | tf_op jit(solution)/shard_map/ppermute | solution.py:857
  328.3 6.0 %collective-permute-done.41 = bf16[1088,128]{1,0:T(8,128)(2,1)S(1)} collective-permute-done((bf16[1088,128]{1,0:T(8,128)(2,1)}, bf16[1088,128]{1,0:T(8,128)(2,1)S(1)}, u32[]{:S(2)}, u32[]{:S(2)}) %collective-permute-start.41) | collective-permute-done | bytes 278560 | tf_op jit(solution)/shard_map/ppermute | solution.py:857
  335.4 5.2 %collective-permute-start.43 = (bf16[272,128]{1,0:T(8,128)(2,1)S(1)}, bf16[272,128]{1,0:T(8,128)(2,1)S(1)}, u32[]{:S(2)}, u32[]{:S(2)}) collective-permute-start(bf16[272,128]{1,0:T(8,128)(2,1)S(1)} %get-tuple-element.303), channel_id=1, source_target_pairs={{0,8},{8,0},{16,24},{24,16},{1,9},{9,1},{17,25},{25,17},{2,10},{10... | collective-permute-start | bytes 208904 | tf_op jit(solution)/shard_map/ppermute | solution.py:907
  340.6 2.4 collective-permute-start.45
  360.2 5.4 %collective-permute-done.49.one = bf16[704,128]{1,0:T(8,128)(2,1)S(1)} collective-permute-done((bf16[704,128]{1,0:T(8,128)(2,1)S(1)}, bf16[704,128]{1,0:T(8,128)(2,1)S(1)}, u32[]{:S(2)}, u32[]{:S(2)}) %collective-permute-start.49) | collective-permute-done | bytes 180256 | tf_op jit(solution)/shard_map/ppermute | solution.py:857
  368.3 3.7 collective-permute-done.51.three
  373.0 3.8 shard_map.300
  377.6 4.1 %shard_map.301 = (f32[3,192,128]{2,1,0:T(8,128)}, f32[3,128,384]{2,1,0:T(8,128)}, f32[384,128]{1,0:T(8,128)}, f32[128,192]{1,0:T(8,128)}, f32[768,128]{1,0:T(8,1...) custom-call(s32[2]{0:T(128)} %copy-done.23, ...), custom_call_target="tpu_custom_call" | custom-call | flops 1000000000 | bytes 4000000 | tf_op jit(solution)/shard_map/pallas_call | solution.py:539
  (342 shorter events, 111.0 us)
Async XLA Ops:
  6.2 27.2 %collective-permute-start = (bf16[944,384]{1,0:T(8,128)(2,1)}, bf16[944,384]{1,0:T(8,128)(2,1)S(1)}, u32[]{:S(2)}, u32[]{:S(2)}) collective-permute-start(bf16[944,384]{1,0:T(8,128)(2,1)} %maximum_maximum_fusion.2.refs_0_), channel_id=1, source_target_pairs={{0,1},{1,0},{2,3},{3,2},{4,5},{5,4},{6,7},{7,6},{8,9},{9,8},{10,11... | collective-permute-start | bytes 2174984 | tf_op jit(solution)/shard_map/ppermute | solution.py:857
  9.1 24.3 %collective-permute-start.1 = (bf16[944,384]{1,0:T(8,128)(2,1)}, bf16[944,384]{1,0:T(8,128)(2,1)S(1)}, u32[]{:S(2)}, u32[]{:S(2)}) collective-permute-start(bf16[944,384]{1,0:T(8,128)(2,1)} %maximum_maximum_fusion.2.refs_0_), channel_id=1, source_target_pairs={{0,2},{1,3},{2,0},{3,1},{4,6},{5,7},{6,4},{7,5},{8,10},{9,11},{10,... | collective-permute-start | bytes 2174984 | tf_op jit(solution)/shard_map/ppermute | solution.py:857
  33.4 11.6 %collective-permute-start.7 = (bf16[416,384]{1,0:T(8,128)(2,1)}, bf16[416,384]{1,0:T(8,128)(2,1)S(1)}, u32[]{:S(2)}, u32[]{:S(2)}) collective-permute-start(bf16[416,384]{1,0:T(8,128)(2,1)} %copy-done.19), channel_id=1, source_target_pairs={{0,3},{1,2},{2,1},{3,0},{4,7},{5,6},{6,5},{7,4},{8,11},{9,10},{10,... | collective-permute-start | bytes 958472 | tf_op jit(solution)/shard_map/ppermute | solution.py:857
  33.4 15.9 %collective-permute-start.8 = (bf16[416,384]{1,0:T(8,128)(2,1)}, bf16[416,384]{1,0:T(8,128)(2,1)}, u32[]{:S(2)}, u32[]{:S(2)}) collective-permute-start(bf16[416,384]{1,0:T(8,128)(2,1)} %copy-done.18), channel_id=1, source_target_pairs={{0,2},{1,3},{2,0},{3,1},{4,6},{5,7},{6,4},{7,5},{8,10},{9,11},{10,... | collective-permute-start | bytes 958472 | tf_op jit(solution)/shard_map/ppermute | solution.py:857
  35.4 15.6 %collective-permute-start.9 = (bf16[416,384]{1,0:T(8,128)(2,1)}, bf16[416,384]{1,0:T(8,128)(2,1)}, u32[]{:S(2)}, u32[]{:S(2)}) collective-permute-start(bf16[416,384]{1,0:T(8,128)(2,1)} %copy-done.17), channel_id=1, source_target_pairs={{0,1},{1,0},{2,3},{3,2},{4,5},{5,4},{6,7},{7,6},{8,9},{9,8},{10,11... | collective-permute-start | bytes 958472 | tf_op jit(solution)/shard_map/ppermute | solution.py:857
  38.1 23.4 %collective-permute-start.4 = (bf16[944,384]{1,0:T(8,128)(2,1)S(1)}, bf16[944,384]{1,0:T(8,128)(2,1)S(1)}, u32[]{:S(2)}, u32[]{:S(2)}) collective-permute-start(bf16[944,384]{1,0:T(8,128)(2,1)S(1)} %collective-permute-done.refs_1_), channel_id=1, source_target_pairs={{0,4},{4,0},{1,5},{5,1},{2,6},{6,2},{3,7},{7,3},{8,12},{12,8},{9,1... | collective-permute-start | bytes 2174984 | tf_op jit(solution)/shard_map/ppermute | solution.py:853
  38.1 23.7 %collective-permute-start.5 = (bf16[944,384]{1,0:T(8,128)(2,1)S(1)}, bf16[944,384]{1,0:T(8,128)(2,1)S(1)}, u32[]{:S(2)}, u32[]{:S(2)}) collective-permute-start(bf16[944,384]{1,0:T(8,128)(2,1)S(1)} %collective-permute-done.1.refs_2_), channel_id=1, source_target_pairs={{0,4},{4,0},{1,5},{5,1},{2,6},{6,2},{3,7},{7,3},{8,12},{12,8},{9,1... | collective-permute-start | bytes 2174984 | tf_op jit(solution)/shard_map/ppermute | solution.py:853
  45.0 12.0 %collective-permute-start.2 = (bf16[944,384]{1,0:T(8,128)(2,1)S(1)}, bf16[944,384]{1,0:T(8,128)(2,1)S(1)}, u32[]{:S(2)}, u32[]{:S(2)}) collective-permute-start(bf16[944,384]{1,0:T(8,128)(2,1)S(1)} %broadcast_select_fusion), channel_id=1, source_target_pairs={{0,2},{1,3},{2,0},{3,1},{4,5},{5,4},{6,7},{7,6},{8,10},{9,11},{10,... | collective-permute-start | bytes 2174984 | tf_op jit(solution)/shard_map/ppermute | solution.py:872
  57.0 23.9 %collective-permute-start.17 = (bf16[416,768]{1,0:T(8,128)(2,1)S(1)}, bf16[416,768]{1,0:T(8,128)(2,1)S(1)}, u32[]{:S(2)}, u32[]{:S(2)}) collective-permute-start(bf16[416,768]{1,0:T(8,128)(2,1)S(1)} %pad_maximum_fusion.4.refs_3_.refs_10_), channel_id=1, source_target_pairs={{0,1},{1,0},{2,3},{3,2},{4,5},{5,4},{6,7},{7,6},{8,9},{9,8},{10,11... | collective-permute-start | bytes 1916936 | tf_op jit(solution)/shard_map/ppermute | solution.py:857
  61.5 20.1 %collective-permute-start.18 = (bf16[416,768]{1,0:T(8,128)(2,1)S(1)}, bf16[416,768]{1,0:T(8,128)(2,1)S(1)}, u32[]{:S(2)}, u32[]{:S(2)}) collective-permute-start(bf16[416,768]{1,0:T(8,128)(2,1)S(1)} %pad_maximum_fusion.4.refs_3_.refs_10_), channel_id=1, source_target_pairs={{0,2},{1,3},{2,0},{3,1},{4,6},{5,7},{6,4},{7,5},{8,10},{9,11},{10,... | collective-permute-start | bytes 1916936 | tf_op jit(solution)/shard_map/ppermute | solution.py:857
  61.9 21.3 %collective-permute-start.13 = (bf16[416,768]{1,0:T(8,128)(2,1)S(1)}, bf16[416,768]{1,0:T(8,128)(2,1)S(1)}, u32[]{:S(2)}, u32[]{:S(2)}) collective-permute-start(bf16[416,768]{1,0:T(8,128)(2,1)S(1)} %pad_maximum_fusion.4.refs_3_.refs_10_), channel_id=1, source_target_pairs={{0,4},{4,0},{1,5},{5,1},{2,6},{6,2},{3,7},{7,3},{8,12},{12,8},{9,1... | collective-permute-start | bytes 1916936 | tf_op jit(solution)/shard_map/ppermute | solution.py:853
  79.6 17.2 %collective-permute-start.10 = (bf16[416,768]{1,0:T(8,128)(2,1)S(1)}, bf16[416,768]{1,0:T(8,128)(2,1)S(1)}, u32[]{:S(2)}, u32[]{:S(2)}) collective-permute-start(bf16[416,768]{1,0:T(8,128)(2,1)S(1)} %get-tuple-element.123.refs_1_.refs_6_), channel_id=1, source_target_pairs={{0,1},{1,0},{2,3},{3,2},{4,5},{5,4},{6,7},{7,6},{8,9},{9,8},{10,11... | collective-permute-start | bytes 1916936 | tf_op jit(solution)/shard_map/ppermute | solution.py:857
  81.0 16.2 %collective-permute-start.11 = (bf16[416,768]{1,0:T(8,128)(2,1)S(1)}, bf16[416,768]{1,0:T(8,128)(2,1)S(1)}, u32[]{:S(2)}, u32[]{:S(2)}) collective-permute-start(bf16[416,768]{1,0:T(8,128)(2,1)S(1)} %get-tuple-element.123.refs_1_.refs_6_), channel_id=1, source_target_pairs={{0,2},{1,3},{2,0},{3,1},{4,6},{5,7},{6,4},{7,5},{8,10},{9,11},{10,... | collective-permute-start | bytes 1916936 | tf_op jit(solution)/shard_map/ppermute | solution.py:857
  81.7 22.3 %collective-permute-start.22 = (bf16[416,768]{1,0:T(8,128)(2,1)S(1)}, bf16[416,768]{1,0:T(8,128)(2,1)S(1)}, u32[]{:S(2)}, u32[]{:S(2)}) collective-permute-start(bf16[416,768]{1,0:T(8,128)(2,1)S(1)} %broadcast_select_fusion.1), channel_id=1, source_target_pairs={{0,2},{1,3},{2,0},{3,1},{4,5},{5,4},{6,7},{7,6},{8,10},{9,11},{10,... | collective-permute-start | bytes 1916936 | tf_op jit(solution)/shard_map/ppermute | solution.py:872
  83.1 21.0 %collective-permute-start.19 = (bf16[416,768]{1,0:T(8,128)(2,1)S(1)}, bf16[416,768]{1,0:T(8,128)(2,1)S(1)}, u32[]{:S(2)}, u32[]{:S(2)}) collective-permute-start(bf16[416,768]{1,0:T(8,128)(2,1)S(1)} %collective-permute-done.17.refs_5_), channel_id=1, source_target_pairs={{0,4},{4,0},{1,5},{5,1},{2,6},{6,2},{3,7},{7,3},{8,12},{12,8},{9,1... | collective-permute-start | bytes 1916936 | tf_op jit(solution)/shard_map/ppermute | solution.py:853
  83.1 21.9 %collective-permute-start.20 = (bf16[416,768]{1,0:T(8,128)(2,1)S(1)}, bf16[416,768]{1,0:T(8,128)(2,1)S(1)}, u32[]{:S(2)}, u32[]{:S(2)}) collective-permute-start(bf16[416,768]{1,0:T(8,128)(2,1)S(1)} %collective-permute-done.18.refs_6_), channel_id=1, source_target_pairs={{0,4},{4,0},{1,5},{5,1},{2,6},{6,2},{3,7},{7,3},{8,12},{12,8},{9,1... | collective-permute-start | bytes 1916936 | tf_op jit(solution)/shard_map/ppermute | solution.py:853
  104.0 14.5 %collective-permute-start.23 = (bf16[416,768]{1,0:T(8,128)(2,1)S(1)}, bf16[416,768]{1,0:T(8,128)(2,1)S(1)}, u32[]{:S(2)}, u32[]{:S(2)}) collective-permute-start(bf16[416,768]{1,0:T(8,128)(2,1)S(1)} %collective-permute-done.22.refs_3_), channel_id=1, source_target_pairs={{0,4},{4,0},{1,5},{5,1},{2,6},{6,2},{3,7},{7,3},{8,12},{12,8},{9,1... | collective-permute-start | bytes 1916936 | tf_op jit(solution)/shard_map/ppermute | solution.py:853
  104.1 13.5 %collective-permute-start.14 = (bf16[416,768]{1,0:T(8,128)(2,1)S(1)}, bf16[416,768]{1,0:T(8,128)(2,1)S(1)}, u32[]{:S(2)}, u32[]{:S(2)}) collective-permute-start(bf16[416,768]{1,0:T(8,128)(2,1)S(1)} %broadcast_select_fusion.2), channel_id=1, source_target_pairs={{0,2},{1,3},{2,0},{3,1},{4,5},{5,4},{6,7},{7,6},{8,10},{9,11},{10,... | collective-permute-start | bytes 1916936 | tf_op jit(solution)/shard_map/ppermute | solution.py:872
  230.7 17.0 %collective-permute-start.24 = (bf16[832,896]{1,0:T(8,128)(2,1)}, bf16[832,896]{1,0:T(8,128)(2,1)}, u32[]{:S(2)}, u32[]{:S(2)}) collective-permute-start(bf16[832,896]{1,0:T(8,128)(2,1)} %get-tuple-element.138), channel_id=1, source_target_pairs={{0,4},{4,0},{1,5},{5,1},{2,6},{6,2},{3,7},{7,3},{8,12},{12,8},{9,1... | collective-permute-start | bytes 4472840 | tf_op jit(solution)/shard_map/ppermute | solution.py:853
  236.9 19.0 %collective-permute-start.31 = (bf16[832,768]{1,0:T(8,128)(2,1)}, bf16[832,768]{1,0:T(8,128)(2,1)}, u32[]{:S(2)}, u32[]{:S(2)}) collective-permute-start(bf16[832,768]{1,0:T(8,128)(2,1)} %get-tuple-element.152), channel_id=1, source_target_pairs={{0,4},{4,0},{1,5},{5,1},{2,6},{6,2},{3,7},{7,3},{8,12},{12,8},{9,1... | collective-permute-start | bytes 3833864 | tf_op jit(solution)/shard_map/ppermute | solution.py:853
  237.1 21.5 %collective-permute-start.30 = (bf16[832,768]{1,0:T(8,128)(2,1)}, bf16[832,768]{1,0:T(8,128)(2,1)}, u32[]{:S(2)}, u32[]{:S(2)}) collective-permute-start(bf16[832,768]{1,0:T(8,128)(2,1)} %get-tuple-element.150), channel_id=1, source_target_pairs={{0,4},{4,0},{1,5},{5,1},{2,6},{6,2},{3,7},{7,3},{8,12},{12,8},{9,1... | collective-permute-start | bytes 3833864 | tf_op jit(solution)/shard_map/ppermute | solution.py:853
  237.4 23.9 %collective-permute-start.26 = (bf16[832,896]{1,0:T(8,128)(2,1)}, bf16[832,896]{1,0:T(8,128)(2,1)}, u32[]{:S(2)}, u32[]{:S(2)}) collective-permute-start(bf16[832,896]{1,0:T(8,128)(2,1)} %add_convert_fusion), channel_id=1, source_target_pairs={{0,1},{1,0},{2,3},{3,2},{4,6},{5,7},{6,4},{7,5},{8,9},{9,8},{10,11... | collective-permute-start | bytes 4472840 | tf_op jit(solution)/shard_map/ppermute | solution.py:872
  264.2 11.9 %collective-permute-start.32 = (bf16[416,896]{1,0:T(8,128)(2,1)}, bf16[416,896]{1,0:T(8,128)(2,1)}, u32[]{:S(2)}, u32[]{:S(2)}) collective-permute-start(bf16[416,896]{1,0:T(8,128)(2,1)} %get-tuple-element.257), channel_id=1, source_target_pairs={{0,2},{1,3},{2,0},{3,1},{4,5},{5,4},{6,7},{7,6},{8,10},{9,11},{10,... | collective-permute-start | bytes 2236424 | tf_op jit(solution)/shard_map/ppermute | solution.py:872
  276.1 35.9 %collective-permute-start.36 = (bf16[416,768]{1,0:T(8,128)(2,1)}, bf16[416,768]{1,0:T(8,128)(2,1)}, u32[]{:S(2)}, u32[]{:S(2)}) collective-permute-start(bf16[416,768]{1,0:T(8,128)(2,1)} %get-tuple-element.168), channel_id=1, source_target_pairs={{0,2},{1,3},{2,0},{3,1},{4,5},{5,4},{6,7},{7,6},{8,10},{9,11},{10,... | collective-permute-start | bytes 1916936 | tf_op jit(solution)/shard_map/ppermute | solution.py:872
  276.7 35.3 %collective-permute-start.37 = (bf16[416,768]{1,0:T(8,128)(2,1)}, bf16[416,768]{1,0:T(8,128)(2,1)}, u32[]{:S(2)}, u32[]{:S(2)}) collective-permute-start(bf16[416,768]{1,0:T(8,128)(2,1)} %get-tuple-element.169), channel_id=1, source_target_pairs={{0,1},{1,0},{2,3},{3,2},{4,6},{5,7},{6,4},{7,5},{8,9},{9,8},{10,11... | collective-permute-start | bytes 1916936 | tf_op jit(solution)/shard_map/ppermute | solution.py:872
  278.7 33.3 %collective-permute-start.38 = (bf16[416,768]{1,0:T(8,128)(2,1)}, bf16[416,768]{1,0:T(8,128)(2,1)}, u32[]{:S(2)}, u32[]{:S(2)}) collective-permute-start(bf16[416,768]{1,0:T(8,128)(2,1)} %get-tuple-element.170), channel_id=1, source_target_pairs={{0,3},{1,2},{2,1},{3,0},{4,7},{5,6},{6,5},{7,4},{8,11},{9,10},{10,... | collective-permute-start | bytes 1916936 | tf_op jit(solution)/shard_map/ppermute | solution.py:872
  319.7 14.6 %collective-permute-start.41 = (bf16[1088,128]{1,0:T(8,128)(2,1)}, bf16[1088,128]{1,0:T(8,128)(2,1)S(1)}, u32[]{:S(2)}, u32[]{:S(2)}) collective-permute-start(bf16[1088,128]{1,0:T(8,128)(2,1)} %get-tuple-element.276), channel_id=1, source_target_pairs={{0,2},{1,3},{2,0},{3,1},{4,6},{5,7},{6,4},{7,5},{8,10},{9,11},{10,... | collective-permute-start | bytes 835592 | tf_op jit(solution)/shard_map/ppermute | solution.py:857
  321.3 13.0 %collective-permute-start.42 = (bf16[1088,128]{1,0:T(8,128)(2,1)S(1)}, bf16[1088,128]{1,0:T(8,128)(2,1)}, u32[]{:S(2)}, u32[]{:S(2)}) collective-permute-start(bf16[1088,128]{1,0:T(8,128)(2,1)S(1)} %get-tuple-element.275), channel_id=1, source_target_pairs={{0,3},{1,2},{2,1},{3,0},{4,7},{5,6},{6,5},{7,4},{8,11},{9,10},{10,... | collective-permute-start | bytes 835592 | tf_op jit(solution)/shard_map/ppermute | solution.py:857
  335.4 12.7 %collective-permute-start.43 = (bf16[272,128]{1,0:T(8,128)(2,1)S(1)}, bf16[272,128]{1,0:T(8,128)(2,1)S(1)}, u32[]{:S(2)}, u32[]{:S(2)}) collective-permute-start(bf16[272,128]{1,0:T(8,128)(2,1)S(1)} %get-tuple-element.303), channel_id=1, source_target_pairs={{0,8},{8,0},{16,24},{24,16},{1,9},{9,1},{17,25},{25,17},{2,10},{10... | collective-permute-start | bytes 208904 | tf_op jit(solution)/shard_map/ppermute | solution.py:907
  346.2 25.8 %collective-permute-start.53 = (bf16[416,384]{1,0:T(8,128)(2,1)S(1)}, bf16[416,384]{1,0:T(8,128)(2,1)S(1)}, u32[]{:S(2)}, u32[]{:S(2)}) collective-permute-start(bf16[416,384]{1,0:T(8,128)(2,1)S(1)} %get-tuple-element.269), channel_id=1, source_target_pairs={{0,1},{1,0},{2,3},{3,2},{4,5},{5,4},{6,7},{7,6},{8,9},{9,8},{10,11... | collective-permute-start | bytes 958472 | tf_op jit(solution)/shard_map/ppermute | solution.py:857
  346.7 25.4 %collective-permute-start.54 = (bf16[416,384]{1,0:T(8,128)(2,1)S(1)}, bf16[416,384]{1,0:T(8,128)(2,1)S(1)}, u32[]{:S(2)}, u32[]{:S(2)}) collective-permute-start(bf16[416,384]{1,0:T(8,128)(2,1)S(1)} %get-tuple-element.268), channel_id=1, source_target_pairs={{0,2},{1,3},{2,0},{3,1},{4,6},{5,7},{6,4},{7,5},{8,10},{9,11},{10,... | collective-permute-start | bytes 958472 | tf_op jit(solution)/shard_map/ppermute | solution.py:857
  354.5 17.6 %collective-permute-start.55 = (bf16[416,384]{1,0:T(8,128)(2,1)S(1)}, bf16[416,384]{1,0:T(8,128)(2,1)S(1)}, u32[]{:S(2)}, u32[]{:S(2)}) collective-permute-start(bf16[416,384]{1,0:T(8,128)(2,1)S(1)} %get-tuple-element.266), channel_id=1, source_target_pairs={{0,3},{1,2},{2,1},{3,0},{4,7},{5,6},{6,5},{7,4},{8,11},{9,10},{10,... | collective-permute-start | bytes 958472 | tf_op jit(solution)/shard_map/ppermute | solution.py:857
  (88 other events, 624.4 us)

commit v3 on v2

--- a/solution.py
+++ b/solution.py
@@ -550,7 +550,7 @@
             ],
         ),
         out_shape=[jax.ShapeDtypeStruct(shape, f32) for shape in shapes],
-        compiler_params=pltpu.CompilerParams(vmem_limit_bytes=60 * 1024 * 1024),
+        compiler_params=pltpu.CompilerParams(vmem_limit_bytes=32 * 1024 * 1024),
         cost_estimate=pl.CostEstimate(flops=1_000_000_000, bytes_accessed=4_000_000, transcendentals=0),
     )(place, mine, *got, far, dp_sums)
 
@@ -592,7 +592,7 @@
             ],
         ),
         out_shape=[jax.ShapeDtypeStruct((rows, width), bf16), jax.ShapeDtypeStruct((rows, width), f32)],
-        compiler_params=pltpu.CompilerParams(vmem_limit_bytes=60 * 1024 * 1024),
+        compiler_params=pltpu.CompilerParams(vmem_limit_bytes=32 * 1024 * 1024),
         cost_estimate=pl.CostEstimate(flops=8_000_000_000, bytes_accessed=3_000_000, transcendentals=0),
     )(place, *blocks)
 
@@ -788,11 +788,14 @@
 def qkv_back_kernel(picks_ref, place_ref, *refs):
     blocks, refs = refs[:8], refs[8:]
     (
-        own_b, x_ref, gain_one, normed_ref, qkv_ref, probs_ref, lows_ref, resid_grad, grad_mixed,
+        own_b, x_hbm, gain_one, normed_hbm, qkv_ref, probs_ref, lows_hbm, resid_hbm, grad_mixed,
         tokens_out, a_part_out, b_part_out,
-        w_qkv, a_qkv, b_qkv, sem, grads,
+        w_qkv, a_qkv, b_qkv, sem, grads, x_ref, normed_ref, lows_ref, resid_grad, late_sem,
     ) = refs
     copies = qkv_copies(place_ref, blocks, own_b, (w_qkv, a_qkv, b_qkv), sem)
+    late = ((x_hbm, x_ref), (normed_hbm, normed_ref), (lows_hbm, lows_ref), (resid_hbm, resid_grad))
+    for k, (source, target) in enumerate(late):
+        copies.append(pltpu.make_async_copy(source, target, late_sem.at[k]))
     for copy in copies:
         copy.start()
     mask, unused = two_masks(picks_ref)
@@ -832,16 +835,25 @@
         grid_spec=pltpu.PrefetchScalarGridSpec(
             num_scalar_prefetch=2,
             grid=(1,),
-            in_specs=[ANYWHERE] * (len(blocks) + 1) + [INSIDE] * 8,
+            in_specs=[ANYWHERE] * (len(blocks) + 2)
+            + [INSIDE, ANYWHERE, INSIDE, INSIDE, ANYWHERE, ANYWHERE, INSIDE],
             out_specs=[INSIDE] * 3,
-            scratch_shapes=QKV_SCRATCH + [pltpu.VMEM((3, BLK, D), bf16)],
+            scratch_shapes=QKV_SCRATCH
+            + [
+                pltpu.VMEM((3, BLK, D), bf16),
+                pltpu.VMEM((BLK, D), bf16),
+                pltpu.VMEM((BLK, D), bf16),
+                pltpu.VMEM((BLK, 512), bf16),
+                pltpu.VMEM((BLK, D), f32),
+                pltpu.SemaphoreType.DMA((4,)),
+            ],
         ),
         out_shape=[
             jax.ShapeDtypeStruct((rows, D), bf16),
             jax.ShapeDtypeStruct((3 * D, 128), bf16),
             jax.ShapeDtypeStruct((3 * D, 128), bf16),
         ],
-        compiler_params=pltpu.CompilerParams(vmem_limit_bytes=44 * 1024 * 1024),
+        compiler_params=pltpu.CompilerParams(vmem_limit_bytes=60 * 1024 * 1024),
         cost_estimate=pl.CostEstimate(flops=9_000_000_000, bytes_accessed=15_000_000, transcendentals=1000),
     )(picks, place, *blocks, own_b, x, gain_one, normed, qkv, probs, lows, resid_grad, grad_mixed)
 
@@ -963,8 +975,8 @@
     )
     pairs = split_call(place, tokens, cotangent)
     from_x, from_y = across_col(packed, 1), across_col(packed, 2)
-    from_x, from_y, *pairs = lax.optimization_barrier((from_x, from_y, *pairs))
     near = [packed, from_x, from_y, across_chip(jnp.where(row == 0, from_x, from_y), 2, 1)]
+    near[3], *pairs = lax.optimization_barrier((near[3], *pairs))
     pairs = by_place([pairs[0]] + [across_col(pairs[s], s) for s in range(1, 4)], col)
     x = jnp.concatenate([pair[:, :width] for pair in pairs], axis=1)
     cot = jnp.concatenate([pair[:, width:] for pair in pairs], axis=1)
@@ -1012,15 +1024,15 @@
             twos, cots, a_up, b_down, wide_router, a_router, wide_b_router,
         )
 
-    cot_far = [across_row(block) for block in cot_near]
+    cot_far = [across_row(block) for block in cot_near[:3]]
     tables = [table(TABLES[0], [two, across_row(two)], [cot, cot_far[0]])]
     two_x, two_y, tables[0] = lax.optimization_barrier((two_x, two_y, tables[0]))
     diag = across_chip(jnp.where(row == 0, two_x, two_y), 2, 1)
     tables.append(
         table(TABLES[1], [two_x, two_y, across_row(two_x), across_row(two_y)], [cot_near[1], cot_near[2], cot_far[1], cot_far[2]])
     )
-    diag, *tables = lax.optimization_barrier((diag, *tables))
-    tables.append(table(TABLES[2], [diag, across_row(diag)], [cot_near[3], cot_far[3]]))
+    diag, cot_diag, *tables = lax.optimization_barrier((diag, cot_near[3], *tables))
+    tables.append(table(TABLES[2], [diag, across_row(diag)], [cot_diag, across_row(cot_diag)]))
     *moved, part_b_up, part_a_down = moe_call(
         token_list, tile_experts, spot_picks, place, tables, TABLES, w_up, w_down, b_up, a_down
     )

time: 392 us -> 381 us (0.972)
  starting transfers between devices: 63.1 us -> 49.5 us
  waiting for transfers between devices: 69.3 us -> 77.2 us
  local copies, waits for them, and re-layouts: 35.3 us -> 29 us
    ppermute x12, starting transfers between devices: 28.1 us -> 14.5 us  [across_dp(): return lax.ppermute(value, 'dp', [(i, i ^ step) for i in range(4)])]
    unnamed x143 -> x127, local copies, waits for them, and re-layouts: 29.5 us -> 23.2 us
    ppermute x18, waiting for transfers between devices: 42.6 us -> 48.6 us  [across_col(): return lax.ppermute(value, 'col', [(i, i ^ step) for i in range(4)])]
    pallas_call x1, Pallas kernels: 104 us -> 109 us  [moe_call(): pl.pallas_call(lambda *refs: moe_kernel(places, *refs), grid_spec=pltpu.P...]
  transfers between devices with their start and end apart: 56 -> 56, of which waited for: 23 -> 24; matrix products, arithmetic and copies ran while one was open for 12% -> 11% of each run, Pallas kernels for 15% -> 15%
where the time goes in v3:
time: 381 us; the launch traced here: 376 us
  Pallas kernels  172 us (45%)
  waiting for transfers between devices  77.2 us (20%)
  starting transfers between devices  49.5 us (13%)
  other arithmetic  45.6 us (12%)
  local copies, waits for them, and re-layouts  29 us (8%)
    pallas_call x1, Pallas kernels, moe_call(): pl.pallas_call(lambda *refs: moe_kernel(places, *refs), grid_spec=pltpu.P...  109 us
    ppermute x18, waiting for transfers between devices, across_col(): return lax.ppermute(value, 'col', [(i, i ^ step) for i in range(4)])  48.6 us
    ppermute x18, starting transfers between devices, across_col(): return lax.ppermute(value, 'col', [(i, i ^ step) for i in range(4)])  23.2 us
    unnamed x127, local copies, waits for them, and re-layouts  23.2 us
    pallas_call x3, Pallas kernels, table_call(): pl.pallas_call(lambda *refs: table_kernel(n, *refs), grid_spec=pltpu.Pref...  20 us
    pallas_call x1, Pallas kernels, qkv_back_call(): pl.pallas_call(qkv_back_kernel, grid_spec=pltpu.PrefetchScalarGridSpec(nu...  15.4 us
    ppermute x12, starting transfers between devices, across_dp(): return lax.ppermute(value, 'dp', [(i, i ^ step) for i in range(4)])  14.5 us
    pallas_call x1, Pallas kernels, attend_call(): pl.pallas_call(attend_kernel, grid_spec=pltpu.PrefetchScalarGridSpec(num_...  13.3 us
  transfers between devices with their start and end apart: 56, of which 24 were waited for; matrix products, arithmetic and copies ran while one was open for 11% of the time, Pallas kernels for 15%

profile of v3, /device:TPU:0, one launch (start us, length us, event | category | flops | bytes accessed | tf_op | source)
XLA Modules:
  0.0 375.6 jit_solution(7576345771285566356)
XLA Ops:
  6.2 2.9 collective-permute-start
  19.3 6.2 %collective-permute-done.refs_1_ = bf16[944,384]{1,0:T(8,128)(2,1)S(1)} collective-permute-done((bf16[944,384]{1,0:T(8,128)(2,1)}, bf16[944,384]{1,0:T(8,128)(2,1)S(1)}, u32[]{:S(2)}, u32[]{:S(2)}) %collective-permute-start) | collective-permute-done | bytes 725024 | tf_op jit(solution)/shard_map/ppermute | solution.py:869
  34.8 8.7 %sort.14 = (s32[14592]{0:T(1024)S(1)}, s32[14592]{0:T(1024)}) sort(s32[14592]{0:T(1024)} %pad_add_fusion, s32[14592]{0:T(1024)S(1)} %iota.71), dimensions={0}, to_apply=%region_1.2 | sort | flops 204288 | bytes 233472 | tf_op jit(solution)/shard_map/sort | solution.py:355
  53.5 3.0 collective-permute-done.7
  56.4 5.6 %collective-permute-done.8 = bf16[416,384]{1,0:T(8,128)(2,1)S(1)} collective-permute-done((bf16[416,384]{1,0:T(8,128)(2,1)}, bf16[416,384]{1,0:T(8,128)(2,1)S(1)}, u32[]{:S(2)}, u32[]{:S(2)}) %collective-permute-start.8) | collective-permute-done | bytes 319520 | tf_op jit(solution)/shard_map/ppermute | solution.py:869
  67.9 13.3 %shard_map.293 = (bf16[416,768]{1,0:T(8,128)(2,1)S(1)}, f32[416,768]{1,0:T(8,128)}, bf16[416,768]{1,0:T(8,128)(2,1)S(1)}, bf16[3,416,768]{2,1,0:T(8,128)(2,1)}, ...) custom-call(s32[16]{0:T(128)S(1)} %and_select_fusion.5.picks_ref, ...), custom_call_target="tpu_custom_call" | custom-call | flops 4000000000 | bytes 15000000 | tf_op jit(solution)/shard_map/pallas_call | solution.py:684
  85.1 5.1 %shard_map.294.refs_4_ = bf16[832,16,128]{2,1,0:T(8,128)(2,1)S(1)} custom-call(s32[4]{0:T(128)S(1)} %pad_add_fusion.3.refs_0_, bf16[416,768]{1,0:T(8,128)(2,1)S(1)} %get-tuple-element.122.refs_1_.refs_6_, bf16[416,768]{1,0:T(8,128)(2,1)S(1)} %collective-permute-done.12.refs_2_, bf16[416,768]{1,0:T(8,128)(2,1)S(1)} %pad_maximum_fusion.4.refs_3_.refs_10_, ...), custom_call_target="tpu_custom_call" | custom-call | flops 6000000000 | bytes 6000000 | tf_op jit(solution)/shard_map/pallas_call | solution.py:100
  92.0 7.0 %collective-permute-done.10.refs_1_ = bf16[416,768]{1,0:T(8,128)(2,1)S(1)} collective-permute-done((bf16[416,768]{1,0:T(8,128)(2,1)S(1)}, bf16[416,768]{1,0:T(8,128)(2,1)S(1)}, u32[]{:S(2)}, u32[]{:S(2)}) %collective-permute-start.10) | collective-permute-done | bytes 639008 | tf_op jit(solution)/shard_map/ppermute | solution.py:869
  103.3 9.8 %shard_map.295.refs_5_ = bf16[1664,16,128]{2,1,0:T(8,128)(2,1)S(1)} custom-call(s32[8]{0:T(128)S(1)} %pad_add_fusion.4.refs_0_, bf16[416,768]{1,0:T(8,128)(2,1)S(1)} %collective-permute-done.10.refs_1_, bf16[416,768]{1,0:T(8,128)(2,1)S(1)} %collective-permute-done.11.refs_2_, bf16[416,768]{1,0:T(8,128)(2,1)S(1)} %collective-permute-done.18.refs_3_, ...), custom_call_target="tpu_custom_call" | custom-call | flops 12000000000 | bytes 12000000 | tf_op jit(solution)/shard_map/pallas_call | solution.py:100
  113.1 2.8 copy-done.23
  115.9 2.4 collective-permute-done.14.refs_1_
  121.3 5.1 %shard_map.296.refs_6_ = bf16[832,16,128]{2,1,0:T(8,128)(2,1)S(1)} custom-call(s32[4]{0:T(128)S(1)} %pad_add_fusion.5.refs_0_, bf16[416,768]{1,0:T(8,128)(2,1)S(1)} %collective-permute-done.14.refs_1_, bf16[416,768]{1,0:T(8,128)(2,1)S(1)} %collective-permute-done.22.refs_2_, bf16[416,768]{1,0:T(8,128)(2,1)S(1)} %collective-permute-done.17.refs_3_, ...), custom_call_target="tpu_custom_call" | custom-call | flops 6000000000 | bytes 6000000 | tf_op jit(solution)/shard_map/pallas_call | solution.py:100
  128.2 108.5 %shard_map.297 = (bf16[832,768]{1,0:T(8,128)(2,1)}, bf16[832,768]{1,0:T(8,128)(2,1)}, bf16[832,768]{1,0:T(8,128)(2,1)}, bf16[832,768]{1,0:T(8,128)(2,1)}, bf16[8...) custom-call(s32[14592]{0:T(1024)} %broadcast_and_fusion.refs_0_, ...), custom_call_target="tpu_custom_call" | custom-call | flops 20000000000 | bytes 60000000 | tf_op jit(solution)/shard_map/pallas_call | solution.py:289
  238.3 3.3 collective-permute-done.25
  245.4 4.0 %collective-permute-done.27 = bf16[192,128]{1,0:T(8,128)(2,1)S(1)} collective-permute-done((bf16[192,128]{1,0:T(8,128)(2,1)S(1)}, bf16[192,128]{1,0:T(8,128)(2,1)S(1)}, u32[]{:S(2)}, u32[]{:S(2)}) %collective-permute-start.27) | collective-permute-done | bytes 49184 | tf_op jit(solution)/shard_map/ppermute | solution.py:919
  251.7 3.6 collective-permute-done.29
  255.4 2.8 add_convert_fusion.6
  258.2 2.5 add_convert_fusion.8
  260.7 2.9 collective-permute-done.26
  263.5 2.6 add_convert_fusion.3
  266.9 4.4 %collective-permute-start.35 = (bf16[192,128]{1,0:T(8,128)(2,1)S(1)}, bf16[192,128]{1,0:T(8,128)(2,1)S(1)}, u32[]{:S(2)}, u32[]{:S(2)}) collective-permute-start(bf16[192,128]{1,0:T(8,128)(2,1)S(1)} %fusion.9), channel_id=1, source_target_pairs={{0,8},{8,0},{16,24},{24,16},{1,9},{9,1},{17,25},{25,17},{2,10},{10... | collective-permute-start | bytes 147464 | tf_op jit(solution)/shard_map/ppermute | solution.py:919
  273.4 4.2 %collective-permute-done.32.refs_12_ = bf16[416,896]{1,0:T(8,128)(2,1)S(1)} collective-permute-done((bf16[416,896]{1,0:T(8,128)(2,1)S(1)}, bf16[416,896]{1,0:T(8,128)(2,1)S(1)}, u32[]{:S(2)}, u32[]{:S(2)}) %collective-permute-start.32) | collective-permute-done | bytes 745504 | tf_op jit(solution)/shard_map/ppermute | solution.py:884
  279.5 2.6 collective-permute-start.38
  282.1 9.3 %shard_map.298 = (f32[416,768]{1,0:T(8,128)}, bf16[416,768]{1,0:T(8,128)(2,1)}, f32[416,768]{1,0:T(8,128)}, bf16[2560,128]{1,0:T(8,128)(2,1)}, bf16[768,128]{1,0:T(8,128)(2,1)}, /*index=5*/bf16[768,128]{1,0:T(8,128)(2,1)}) custom-call(s32[16]{0:T(128)} %copy-done.7, s32[2]{0:T(128)} %copy-done.17, bf16[1456,384]{1,0:T(8,128)(2,1)} %copy-done.50, ...), custom_call_target="tpu_custom_call" | custom-call | flops 6000000000 | bytes 15000000 | tf_op jit(solution)/shard_map/pallas_call | solution.py:765
  292.5 15.4 %shard_map.299 = (bf16[416,768]{1,0:T(8,128)(2,1)}, bf16[2304,128]{1,0:T(8,128)(2,1)}, bf16[2304,128]{1,0:T(8,128)(2,1)}) custom-call(s32[16]{0:T(128)} %copy-done.7, s32[2]{0:T(128)} %copy-done.17, bf16[944,384]{1,0:T(8,128)(2,1)} %maximum_maximum_fusion.2.refs_0_, bf16[944,384]{1,0:T(8,128)(2,1)} %copy-done, bf16[944,384]{1,0:T(8,128)(2,1)} %copy-done.1, ...), custom_call_target="tpu_custom_call" | custom-call | flops 8999999488 | bytes 15000000 | tf_op jit(solution)/shard_map/pallas_call | solution.py:833
  311.1 2.8 collective-permute-done.39
  319.8 6.2 %collective-permute-done.40 = bf16[1088,128]{1,0:T(8,128)(2,1)S(1)} collective-permute-done((bf16[1088,128]{1,0:T(8,128)(2,1)}, bf16[1088,128]{1,0:T(8,128)(2,1)S(1)}, u32[]{:S(2)}, u32[]{:S(2)}) %collective-permute-start.40) | collective-permute-done | bytes 278560 | tf_op jit(solution)/shard_map/ppermute | solution.py:869
  326.1 6.0 %collective-permute-done.41 = bf16[1088,128]{1,0:T(8,128)(2,1)} collective-permute-done((bf16[1088,128]{1,0:T(8,128)(2,1)}, bf16[1088,128]{1,0:T(8,128)(2,1)}, u32[]{:S(2)}, u32[]{:S(2)}) %collective-permute-start.41) | collective-permute-done | bytes 278560 | tf_op jit(solution)/shard_map/ppermute | solution.py:869
  333.9 3.8 %collective-permute-start.45 = (bf16[272,128]{1,0:T(8,128)(2,1)S(1)}, bf16[272,128]{1,0:T(8,128)(2,1)S(1)}, u32[]{:S(2)}, u32[]{:S(2)}) collective-permute-start(bf16[272,128]{1,0:T(8,128)(2,1)S(1)} %get-tuple-element.304), channel_id=1, source_target_pairs={{0,24},{8,16},{16,8},{24,0},{1,25},{9,17},{17,9},{25,1},{2,26},{10... | collective-permute-start | bytes 208904 | tf_op jit(solution)/shard_map/ppermute | solution.py:919
  343.9 3.6 collective-permute-start.48
  353.1 7.6 %collective-permute-done.49.one = bf16[704,128]{1,0:T(8,128)(2,1)S(1)} collective-permute-done((bf16[704,128]{1,0:T(8,128)(2,1)S(1)}, bf16[704,128]{1,0:T(8,128)(2,1)S(1)}, u32[]{:S(2)}, u32[]{:S(2)}) %collective-permute-start.49) | collective-permute-done | bytes 180256 | tf_op jit(solution)/shard_map/ppermute | solution.py:869
  362.9 4.2 %collective-permute-done.51.three = bf16[704,128]{1,0:T(8,128)(2,1)S(1)} collective-permute-done((bf16[704,128]{1,0:T(8,128)(2,1)S(1)}, bf16[704,128]{1,0:T(8,128)(2,1)S(1)}, u32[]{:S(2)}, u32[]{:S(2)}) %collective-permute-start.51) | collective-permute-done | bytes 180256 | tf_op jit(solution)/shard_map/ppermute | solution.py:869
  (326 shorter events, 101.6 us)
Async XLA Ops:
  6.2 19.4 %collective-permute-start = (bf16[944,384]{1,0:T(8,128)(2,1)}, bf16[944,384]{1,0:T(8,128)(2,1)S(1)}, u32[]{:S(2)}, u32[]{:S(2)}) collective-permute-start(bf16[944,384]{1,0:T(8,128)(2,1)} %maximum_maximum_fusion.2.refs_0_), channel_id=1, source_target_pairs={{0,1},{1,0},{2,3},{3,2},{4,5},{5,4},{6,7},{7,6},{8,9},{9,8},{10,11... | collective-permute-start | bytes 2174984 | tf_op jit(solution)/shard_map/ppermute | solution.py:869
  9.1 17.9 %collective-permute-start.1 = (bf16[944,384]{1,0:T(8,128)(2,1)}, bf16[944,384]{1,0:T(8,128)(2,1)S(1)}, u32[]{:S(2)}, u32[]{:S(2)}) collective-permute-start(bf16[944,384]{1,0:T(8,128)(2,1)} %maximum_maximum_fusion.2.refs_0_), channel_id=1, source_target_pairs={{0,2},{1,3},{2,0},{3,1},{4,6},{5,7},{6,4},{7,5},{8,10},{9,11},{10,... | collective-permute-start | bytes 2174984 | tf_op jit(solution)/shard_map/ppermute | solution.py:869
  28.1 16.8 %collective-permute-start.2 = (bf16[944,384]{1,0:T(8,128)(2,1)}, bf16[944,384]{1,0:T(8,128)(2,1)}, u32[]{:S(2)}, u32[]{:S(2)}) collective-permute-start(bf16[944,384]{1,0:T(8,128)(2,1)} %broadcast_select_fusion), channel_id=1, source_target_pairs={{0,2},{1,3},{2,0},{3,1},{4,5},{5,4},{6,7},{7,6},{8,10},{9,11},{10,... | collective-permute-start | bytes 2174984 | tf_op jit(solution)/shard_map/ppermute | solution.py:884
  44.9 18.9 %collective-permute-start.4 = (bf16[944,384]{1,0:T(8,128)(2,1)S(1)}, bf16[944,384]{1,0:T(8,128)(2,1)S(1)}, u32[]{:S(2)}, u32[]{:S(2)}) collective-permute-start(bf16[944,384]{1,0:T(8,128)(2,1)S(1)} %collective-permute-done.refs_1_), channel_id=1, source_target_pairs={{0,4},{4,0},{1,5},{5,1},{2,6},{6,2},{3,7},{7,3},{8,12},{12,8},{9,1... | collective-permute-start | bytes 2174984 | tf_op jit(solution)/shard_map/ppermute | solution.py:865
  44.9 11.5 %collective-permute-start.7 = (bf16[416,384]{1,0:T(8,128)(2,1)}, bf16[416,384]{1,0:T(8,128)(2,1)S(1)}, u32[]{:S(2)}, u32[]{:S(2)}) collective-permute-start(bf16[416,384]{1,0:T(8,128)(2,1)} %copy-done.13), channel_id=1, source_target_pairs={{0,3},{1,2},{2,1},{3,0},{4,7},{5,6},{6,5},{7,4},{8,11},{9,10},{10,... | collective-permute-start | bytes 958472 | tf_op jit(solution)/shard_map/ppermute | solution.py:869
  45.2 16.7 %collective-permute-start.8 = (bf16[416,384]{1,0:T(8,128)(2,1)}, bf16[416,384]{1,0:T(8,128)(2,1)S(1)}, u32[]{:S(2)}, u32[]{:S(2)}) collective-permute-start(bf16[416,384]{1,0:T(8,128)(2,1)} %copy-done.12), channel_id=1, source_target_pairs={{0,2},{1,3},{2,0},{3,1},{4,6},{5,7},{6,4},{7,5},{8,10},{9,11},{10,... | collective-permute-start | bytes 958472 | tf_op jit(solution)/shard_map/ppermute | solution.py:869
  46.9 15.1 %collective-permute-start.9 = (bf16[416,384]{1,0:T(8,128)(2,1)}, bf16[416,384]{1,0:T(8,128)(2,1)S(1)}, u32[]{:S(2)}, u32[]{:S(2)}) collective-permute-start(bf16[416,384]{1,0:T(8,128)(2,1)} %copy-done.11), channel_id=1, source_target_pairs={{0,1},{1,0},{2,3},{3,2},{4,5},{5,4},{6,7},{7,6},{8,9},{9,8},{10,11... | collective-permute-start | bytes 958472 | tf_op jit(solution)/shard_map/ppermute | solution.py:869
  52.0 13.7 %collective-permute-start.3 = (bf16[1456,384]{1,0:T(8,128)(2,1)S(1)}, bf16[1456,384]{1,0:T(8,128)(2,1)S(1)}, u32[]{:S(2)}, u32[]{:S(2)}) collective-permute-start(bf16[1456,384]{1,0:T(8,128)(2,1)S(1)} %maximum_dynamic-update-slice_fusion), channel_id=1, source_target_pairs={{0,4},{4,0},{1,5},{5,1},{2,6},{6,2},{3,7},{7,3},{8,12},{12,8},{9,1... | collective-permute-start | bytes 3354632 | tf_op jit(solution)/shard_map/ppermute | solution.py:865
  62.9 20.9 %collective-permute-start.13 = (bf16[416,768]{1,0:T(8,128)(2,1)S(1)}, bf16[416,768]{1,0:T(8,128)(2,1)S(1)}, u32[]{:S(2)}, u32[]{:S(2)}) collective-permute-start(bf16[416,768]{1,0:T(8,128)(2,1)S(1)} %pad_maximum_fusion.4.refs_3_.refs_10_), channel_id=1, source_target_pairs={{0,4},{4,0},{1,5},{5,1},{2,6},{6,2},{3,7},{7,3},{8,12},{12,8},{9,1... | collective-permute-start | bytes 1916936 | tf_op jit(solution)/shard_map/ppermute | solution.py:865
  63.8 20.8 %collective-permute-start.15 = (bf16[416,768]{1,0:T(8,128)(2,1)S(1)}, bf16[416,768]{1,0:T(8,128)(2,1)S(1)}, u32[]{:S(2)}, u32[]{:S(2)}) collective-permute-start(bf16[416,768]{1,0:T(8,128)(2,1)S(1)} %pad_maximum_fusion.4.refs_3_.refs_10_), channel_id=1, source_target_pairs={{0,1},{1,0},{2,3},{3,2},{4,5},{5,4},{6,7},{7,6},{8,9},{9,8},{10,11... | collective-permute-start | bytes 1916936 | tf_op jit(solution)/shard_map/ppermute | solution.py:869
  65.3 19.3 %collective-permute-start.16 = (bf16[416,768]{1,0:T(8,128)(2,1)S(1)}, bf16[416,768]{1,0:T(8,128)(2,1)S(1)}, u32[]{:S(2)}, u32[]{:S(2)}) collective-permute-start(bf16[416,768]{1,0:T(8,128)(2,1)S(1)} %pad_maximum_fusion.4.refs_3_.refs_10_), channel_id=1, source_target_pairs={{0,2},{1,3},{2,0},{3,1},{4,6},{5,7},{6,4},{7,5},{8,10},{9,11},{10,... | collective-permute-start | bytes 1916936 | tf_op jit(solution)/shard_map/ppermute | solution.py:869
  82.2 16.8 %collective-permute-start.10 = (bf16[416,768]{1,0:T(8,128)(2,1)S(1)}, bf16[416,768]{1,0:T(8,128)(2,1)S(1)}, u32[]{:S(2)}, u32[]{:S(2)}) collective-permute-start(bf16[416,768]{1,0:T(8,128)(2,1)S(1)} %get-tuple-element.122.refs_1_.refs_6_), channel_id=1, source_target_pairs={{0,1},{1,0},{2,3},{3,2},{4,5},{5,4},{6,7},{7,6},{8,9},{9,8},{10,11... | collective-permute-start | bytes 1916936 | tf_op jit(solution)/shard_map/ppermute | solution.py:869
  83.8 16.5 %collective-permute-start.11 = (bf16[416,768]{1,0:T(8,128)(2,1)S(1)}, bf16[416,768]{1,0:T(8,128)(2,1)S(1)}, u32[]{:S(2)}, u32[]{:S(2)}) collective-permute-start(bf16[416,768]{1,0:T(8,128)(2,1)S(1)} %get-tuple-element.122.refs_1_.refs_6_), channel_id=1, source_target_pairs={{0,2},{1,3},{2,0},{3,1},{4,6},{5,7},{6,4},{7,5},{8,10},{9,11},{10,... | collective-permute-start | bytes 1916936 | tf_op jit(solution)/shard_map/ppermute | solution.py:869
  84.6 17.2 %collective-permute-start.20 = (bf16[416,768]{1,0:T(8,128)(2,1)S(1)}, bf16[416,768]{1,0:T(8,128)(2,1)S(1)}, u32[]{:S(2)}, u32[]{:S(2)}) collective-permute-start(bf16[416,768]{1,0:T(8,128)(2,1)S(1)} %collective-permute-done.15.refs_5_), channel_id=1, source_target_pairs={{0,4},{4,0},{1,5},{5,1},{2,6},{6,2},{3,7},{7,3},{8,12},{12,8},{9,1... | collective-permute-start | bytes 1916936 | tf_op jit(solution)/shard_map/ppermute | solution.py:865
  84.6 18.6 %collective-permute-start.21 = (bf16[416,768]{1,0:T(8,128)(2,1)S(1)}, bf16[416,768]{1,0:T(8,128)(2,1)S(1)}, u32[]{:S(2)}, u32[]{:S(2)}) collective-permute-start(bf16[416,768]{1,0:T(8,128)(2,1)S(1)} %collective-permute-done.16.refs_6_), channel_id=1, source_target_pairs={{0,4},{4,0},{1,5},{5,1},{2,6},{6,2},{3,7},{7,3},{8,12},{12,8},{9,1... | collective-permute-start | bytes 1916936 | tf_op jit(solution)/shard_map/ppermute | solution.py:865
  101.0 14.9 %collective-permute-start.17 = (bf16[416,768]{1,0:T(8,128)(2,1)S(1)}, bf16[416,768]{1,0:T(8,128)(2,1)S(1)}, u32[]{:S(2)}, u32[]{:S(2)}) collective-permute-start(bf16[416,768]{1,0:T(8,128)(2,1)S(1)} %broadcast_select_fusion.1), channel_id=1, source_target_pairs={{0,2},{1,3},{2,0},{3,1},{4,5},{5,4},{6,7},{7,6},{8,10},{9,11},{10,... | collective-permute-start | bytes 1916936 | tf_op jit(solution)/shard_map/ppermute | solution.py:884
  101.8 16.5 %collective-permute-start.14 = (bf16[416,768]{1,0:T(8,128)(2,1)S(1)}, bf16[416,768]{1,0:T(8,128)(2,1)S(1)}, u32[]{:S(2)}, u32[]{:S(2)}) collective-permute-start(bf16[416,768]{1,0:T(8,128)(2,1)S(1)} %broadcast_select_fusion.2), channel_id=1, source_target_pairs={{0,2},{1,3},{2,0},{3,1},{4,5},{5,4},{6,7},{7,6},{8,10},{9,11},{10,... | collective-permute-start | bytes 1916936 | tf_op jit(solution)/shard_map/ppermute | solution.py:884
  243.3 12.1 %collective-permute-start.31 = (bf16[832,768]{1,0:T(8,128)(2,1)}, bf16[832,768]{1,0:T(8,128)(2,1)}, u32[]{:S(2)}, u32[]{:S(2)}) collective-permute-start(bf16[832,768]{1,0:T(8,128)(2,1)} %get-tuple-element.152), channel_id=1, source_target_pairs={{0,4},{4,0},{1,5},{5,1},{2,6},{6,2},{3,7},{7,3},{8,12},{12,8},{9,1... | collective-permute-start | bytes 3833864 | tf_op jit(solution)/shard_map/ppermute | solution.py:865
  243.5 14.7 %collective-permute-start.30 = (bf16[832,768]{1,0:T(8,128)(2,1)}, bf16[832,768]{1,0:T(8,128)(2,1)}, u32[]{:S(2)}, u32[]{:S(2)}) collective-permute-start(bf16[832,768]{1,0:T(8,128)(2,1)} %get-tuple-element.150), channel_id=1, source_target_pairs={{0,4},{4,0},{1,5},{5,1},{2,6},{6,2},{3,7},{7,3},{8,12},{12,8},{9,1... | collective-permute-start | bytes 3833864 | tf_op jit(solution)/shard_map/ppermute | solution.py:865
  243.9 19.6 %collective-permute-start.26 = (bf16[832,896]{1,0:T(8,128)(2,1)S(1)}, bf16[832,896]{1,0:T(8,128)(2,1)}, u32[]{:S(2)}, u32[]{:S(2)}) collective-permute-start(bf16[832,896]{1,0:T(8,128)(2,1)S(1)} %add_convert_fusion), channel_id=1, source_target_pairs={{0,1},{1,0},{2,3},{3,2},{4,6},{5,7},{6,4},{7,5},{8,9},{9,8},{10,11... | collective-permute-start | bytes 4472840 | tf_op jit(solution)/shard_map/ppermute | solution.py:884
  266.1 11.6 %collective-permute-start.32 = (bf16[416,896]{1,0:T(8,128)(2,1)S(1)}, bf16[416,896]{1,0:T(8,128)(2,1)S(1)}, u32[]{:S(2)}, u32[]{:S(2)}) collective-permute-start(bf16[416,896]{1,0:T(8,128)(2,1)S(1)} %get-tuple-element.257), channel_id=1, source_target_pairs={{0,2},{1,3},{2,0},{3,1},{4,5},{5,4},{6,7},{7,6},{8,10},{9,11},{10,... | collective-permute-start | bytes 2236424 | tf_op jit(solution)/shard_map/ppermute | solution.py:884
  278.6 29.3 %collective-permute-start.36 = (bf16[416,768]{1,0:T(8,128)(2,1)}, bf16[416,768]{1,0:T(8,128)(2,1)S(1)}, u32[]{:S(2)}, u32[]{:S(2)}) collective-permute-start(bf16[416,768]{1,0:T(8,128)(2,1)} %get-tuple-element.168), channel_id=1, source_target_pairs={{0,2},{1,3},{2,0},{3,1},{4,5},{5,4},{6,7},{7,6},{8,10},{9,11},{10,... | collective-permute-start | bytes 1916936 | tf_op jit(solution)/shard_map/ppermute | solution.py:884
  279.4 28.5 %collective-permute-start.37 = (bf16[416,768]{1,0:T(8,128)(2,1)}, bf16[416,768]{1,0:T(8,128)(2,1)S(1)}, u32[]{:S(2)}, u32[]{:S(2)}) collective-permute-start(bf16[416,768]{1,0:T(8,128)(2,1)} %get-tuple-element.169), channel_id=1, source_target_pairs={{0,1},{1,0},{2,3},{3,2},{4,6},{5,7},{6,4},{7,5},{8,9},{9,8},{10,11... | collective-permute-start | bytes 1916936 | tf_op jit(solution)/shard_map/ppermute | solution.py:884
  279.5 28.5 %collective-permute-start.38 = (bf16[416,768]{1,0:T(8,128)(2,1)}, bf16[416,768]{1,0:T(8,128)(2,1)S(1)}, u32[]{:S(2)}, u32[]{:S(2)}) collective-permute-start(bf16[416,768]{1,0:T(8,128)(2,1)} %get-tuple-element.170), channel_id=1, source_target_pairs={{0,3},{1,2},{2,1},{3,0},{4,7},{5,6},{6,5},{7,4},{8,11},{9,10},{10,... | collective-permute-start | bytes 1916936 | tf_op jit(solution)/shard_map/ppermute | solution.py:884
  316.4 9.7 %collective-permute-start.40 = (bf16[1088,128]{1,0:T(8,128)(2,1)}, bf16[1088,128]{1,0:T(8,128)(2,1)S(1)}, u32[]{:S(2)}, u32[]{:S(2)}) collective-permute-start(bf16[1088,128]{1,0:T(8,128)(2,1)} %get-tuple-element.274), channel_id=1, source_target_pairs={{0,1},{1,0},{2,3},{3,2},{4,5},{5,4},{6,7},{7,6},{8,9},{9,8},{10,11... | collective-permute-start | bytes 835592 | tf_op jit(solution)/shard_map/ppermute | solution.py:869
  317.3 14.7 %collective-permute-start.41 = (bf16[1088,128]{1,0:T(8,128)(2,1)}, bf16[1088,128]{1,0:T(8,128)(2,1)}, u32[]{:S(2)}, u32[]{:S(2)}) collective-permute-start(bf16[1088,128]{1,0:T(8,128)(2,1)} %get-tuple-element.276), channel_id=1, source_target_pairs={{0,2},{1,3},{2,0},{3,1},{4,6},{5,7},{6,4},{7,5},{8,10},{9,11},{10,... | collective-permute-start | bytes 835592 | tf_op jit(solution)/shard_map/ppermute | solution.py:869
  318.1 13.9 %collective-permute-start.42 = (bf16[1088,128]{1,0:T(8,128)(2,1)}, bf16[1088,128]{1,0:T(8,128)(2,1)}, u32[]{:S(2)}, u32[]{:S(2)}) collective-permute-start(bf16[1088,128]{1,0:T(8,128)(2,1)} %get-tuple-element.275), channel_id=1, source_target_pairs={{0,3},{1,2},{2,1},{3,0},{4,7},{5,6},{6,5},{7,4},{8,11},{9,10},{10,... | collective-permute-start | bytes 835592 | tf_op jit(solution)/shard_map/ppermute | solution.py:869
  333.3 9.8 %collective-permute-start.43 = (bf16[272,128]{1,0:T(8,128)(2,1)S(1)}, bf16[272,128]{1,0:T(8,128)(2,1)S(1)}, u32[]{:S(2)}, u32[]{:S(2)}) collective-permute-start(bf16[272,128]{1,0:T(8,128)(2,1)S(1)} %get-tuple-element.303), channel_id=1, source_target_pairs={{0,8},{8,0},{16,24},{24,16},{1,9},{9,1},{17,25},{25,17},{2,10},{10... | collective-permute-start | bytes 208904 | tf_op jit(solution)/shard_map/ppermute | solution.py:919
  341.1 26.1 %collective-permute-start.53 = (bf16[416,384]{1,0:T(8,128)(2,1)S(1)}, bf16[416,384]{1,0:T(8,128)(2,1)S(1)}, u32[]{:S(2)}, u32[]{:S(2)}) collective-permute-start(bf16[416,384]{1,0:T(8,128)(2,1)S(1)} %get-tuple-element.269), channel_id=1, source_target_pairs={{0,1},{1,0},{2,3},{3,2},{4,5},{5,4},{6,7},{7,6},{8,9},{9,8},{10,11... | collective-permute-start | bytes 958472 | tf_op jit(solution)/shard_map/ppermute | solution.py:869
  342.2 25.0 %collective-permute-start.54 = (bf16[416,384]{1,0:T(8,128)(2,1)S(1)}, bf16[416,384]{1,0:T(8,128)(2,1)S(1)}, u32[]{:S(2)}, u32[]{:S(2)}) collective-permute-start(bf16[416,384]{1,0:T(8,128)(2,1)S(1)} %get-tuple-element.268), channel_id=1, source_target_pairs={{0,2},{1,3},{2,0},{3,1},{4,6},{5,7},{6,4},{7,5},{8,10},{9,11},{10,... | collective-permute-start | bytes 958472 | tf_op jit(solution)/shard_map/ppermute | solution.py:869
  349.4 17.8 %collective-permute-start.55 = (bf16[416,384]{1,0:T(8,128)(2,1)S(1)}, bf16[416,384]{1,0:T(8,128)(2,1)S(1)}, u32[]{:S(2)}, u32[]{:S(2)}) collective-permute-start(bf16[416,384]{1,0:T(8,128)(2,1)S(1)} %get-tuple-element.266), channel_id=1, source_target_pairs={{0,3},{1,2},{2,1},{3,0},{4,7},{5,6},{6,5},{7,4},{8,11},{9,10},{10,... | collective-permute-start | bytes 958472 | tf_op jit(solution)/shard_map/ppermute | solution.py:869
  352.2 10.7 %collective-permute-start.50 = (bf16[704,128]{1,0:T(8,128)(2,1)S(1)}, bf16[704,128]{1,0:T(8,128)(2,1)S(1)}, u32[]{:S(2)}, u32[]{:S(2)}) collective-permute-start(bf16[704,128]{1,0:T(8,128)(2,1)S(1)} %pad_maximum_fusion.16), channel_id=1, source_target_pairs={{0,2},{1,3},{2,0},{3,1},{4,6},{5,7},{6,4},{7,5},{8,10},{9,11},{10,... | collective-permute-start | bytes 540680 | tf_op jit(solution)/shard_map/ppermute | solution.py:869
  (80 other events, 696.3 us)

commit v4 on v3

--- a/solution.py
+++ b/solution.py
@@ -975,8 +975,8 @@
     )
     pairs = split_call(place, tokens, cotangent)
     from_x, from_y = across_col(packed, 1), across_col(packed, 2)
-    near = [packed, from_x, from_y, across_chip(jnp.where(row == 0, from_x, from_y), 2, 1)]
-    near[3], *pairs = lax.optimization_barrier((near[3], *pairs))
+    chosen, *pairs = lax.optimization_barrier((jnp.where(row == 0, from_x, from_y), *pairs))
+    near = [packed, from_x, from_y, across_chip(chosen, 2, 1)]
     pairs = by_place([pairs[0]] + [across_col(pairs[s], s) for s in range(1, 4)], col)
     x = jnp.concatenate([pair[:, :width] for pair in pairs], axis=1)
     cot = jnp.concatenate([pair[:, width:] for pair in pairs], axis=1)
@@ -1072,6 +1072,7 @@
     mine, grad_tokens, base = lax.optimization_barrier((mine, grad_tokens, base))
     moves = to_features(grad_tokens, (base + added(*sums)).astype(bf16), col)
     mine = spread_dp(scatter_dp(mine)) if four_dp else lax.psum(mine, "dp")
+    mine, moves[1] = lax.optimization_barrier((mine, moves[1]))
     got = [across_col(mine[384:], s) for s in range(1, 4)]
     far = across_row(jnp.concatenate([mine[:384], mine[768:]] + [one[384:] for one in got]))
     block_out, grad_tokens = merge_call(place, moves, tokens.shape[0])

time: 381 us -> 381 us (level)
  starting transfers between devices: 49.5 us -> 53.4 us
    ppermute x12, starting transfers between devices: 14.5 us -> 20.4 us  [across_dp(): return lax.ppermute(value, 'dp', [(i, i ^ step) for i in range(4)])]
  transfers between devices with their start and end apart: 56 -> 56, of which waited for: 24 -> 30; matrix products, arithmetic and copies ran while one was open for 11% -> 10% of each run, Pallas kernels for 15% -> 15%
where the time goes in v4:
time: 381 us; the launch traced here: 377 us
  Pallas kernels  172 us (45%)
  waiting for transfers between devices  78.3 us (21%)
  starting transfers between devices  53.4 us (14%)
  other arithmetic  43.5 us (11%)
  local copies, waits for them, and re-layouts  27.6 us (7%)
    pallas_call x1, Pallas kernels, moe_call(): pl.pallas_call(lambda *refs: moe_kernel(places, *refs), grid_spec=pltpu.P...  109 us
    ppermute x18, waiting for transfers between devices, across_col(): return lax.ppermute(value, 'col', [(i, i ^ step) for i in range(4)])  46.3 us
    ppermute x18, starting transfers between devices, across_col(): return lax.ppermute(value, 'col', [(i, i ^ step) for i in range(4)])  22.5 us
    unnamed x127, local copies, waits for them, and re-layouts  22.4 us
    ppermute x12, starting transfers between devices, across_dp(): return lax.ppermute(value, 'dp', [(i, i ^ step) for i in range(4)])  20.4 us
    pallas_call x3, Pallas kernels, table_call(): pl.pallas_call(lambda *refs: table_kernel(n, *refs), grid_spec=pltpu.Pref...  20.1 us
    pallas_call x1, Pallas kernels, qkv_back_call(): pl.pallas_call(qkv_back_kernel, grid_spec=pltpu.PrefetchScalarGridSpec(nu...  15.4 us
    ppermute x12, waiting for transfers between devices, across_dp(): return lax.ppermute(value, 'dp', [(i, i ^ step) for i in range(4)])  13.8 us
  transfers between devices with their start and end apart: 56, of which 30 were waited for; matrix products, arithmetic and copies ran while one was open for 10% of the time, Pallas kernels for 15%

profile of v4, /device:TPU:0, one launch (start us, length us, event | category | flops | bytes accessed | tf_op | source)
XLA Modules:
  0.0 377.1 jit_solution(14883114014035124720)
XLA Ops:
  6.2 2.9 collective-permute-start
  22.6 8.6 %sort.14 = (s32[14592]{0:T(1024)S(1)}, s32[14592]{0:T(1024)}) sort(s32[14592]{0:T(1024)} %pad_add_fusion, s32[14592]{0:T(1024)S(1)} %iota.71), dimensions={0}, to_apply=%region_1.2 | sort | flops 204288 | bytes 233472 | tf_op jit(solution)/shard_map/sort | solution.py:355
  38.2 5.3 %collective-permute-done.7 = bf16[416,384]{1,0:T(8,128)(2,1)S(1)} collective-permute-done((bf16[416,384]{1,0:T(8,128)(2,1)S(1)}, bf16[416,384]{1,0:T(8,128)(2,1)S(1)}, u32[]{:S(2)}, u32[]{:S(2)}) %collective-permute-start.7) | collective-permute-done | bytes 319520 | tf_op jit(solution)/shard_map/ppermute | solution.py:869
  43.5 4.3 %collective-permute-done.8 = bf16[416,384]{1,0:T(8,128)(2,1)S(1)} collective-permute-done((bf16[416,384]{1,0:T(8,128)(2,1)S(1)}, bf16[416,384]{1,0:T(8,128)(2,1)S(1)}, u32[]{:S(2)}, u32[]{:S(2)}) %collective-permute-start.8) | collective-permute-done | bytes 319520 | tf_op jit(solution)/shard_map/ppermute | solution.py:869
  50.7 4.8 %collective-permute-done.2.refs_3_ = bf16[944,384]{1,0:T(8,128)(2,1)S(1)} collective-permute-done((bf16[944,384]{1,0:T(8,128)(2,1)S(1)}, bf16[944,384]{1,0:T(8,128)(2,1)S(1)}, u32[]{:S(2)}, u32[]{:S(2)}) %collective-permute-start.2) | collective-permute-done | bytes 725024 | tf_op jit(solution)/shard_map/ppermute | solution.py:884
  63.1 13.2 %shard_map.293 = (bf16[416,768]{1,0:T(8,128)(2,1)S(1)}, f32[416,768]{1,0:T(8,128)}, bf16[416,768]{1,0:T(8,128)(2,1)S(1)}, bf16[3,416,768]{2,1,0:T(8,128)(2,1)}, ...) custom-call(s32[16]{0:T(128)S(1)} %and_select_fusion.5.picks_ref, ...), custom_call_target="tpu_custom_call" | custom-call | flops 4000000000 | bytes 15000000 | tf_op jit(solution)/shard_map/pallas_call | solution.py:684
  80.3 5.1 %shard_map.294.refs_4_ = bf16[832,16,128]{2,1,0:T(8,128)(2,1)S(1)} custom-call(s32[4]{0:T(128)S(1)} %pad_add_fusion.3.refs_0_, bf16[416,768]{1,0:T(8,128)(2,1)S(1)} %get-tuple-element.124.refs_1_.refs_6_, bf16[416,768]{1,0:T(8,128)(2,1)S(1)} %collective-permute-done.12.refs_2_, bf16[416,768]{1,0:T(8,128)(2,1)S(1)} %pad_maximum_fusion.4.refs_3_.refs_10_, ...), custom_call_target="tpu_custom_call" | custom-call | flops 6000000000 | bytes 6000000 | tf_op jit(solution)/shard_map/pallas_call | solution.py:100
  87.2 7.0 %collective-permute-done.10.refs_1_ = bf16[416,768]{1,0:T(8,128)(2,1)S(1)} collective-permute-done((bf16[416,768]{1,0:T(8,128)(2,1)S(1)}, bf16[416,768]{1,0:T(8,128)(2,1)S(1)}, u32[]{:S(2)}, u32[]{:S(2)}) %collective-permute-start.10) | collective-permute-done | bytes 639008 | tf_op jit(solution)/shard_map/ppermute | solution.py:869
  98.6 9.8 %shard_map.295.refs_5_ = bf16[1664,16,128]{2,1,0:T(8,128)(2,1)S(1)} custom-call(s32[8]{0:T(128)S(1)} %pad_add_fusion.4.refs_0_, bf16[416,768]{1,0:T(8,128)(2,1)S(1)} %collective-permute-done.10.refs_1_, bf16[416,768]{1,0:T(8,128)(2,1)S(1)} %collective-permute-done.11.refs_2_, bf16[416,768]{1,0:T(8,128)(2,1)S(1)} %collective-permute-done.18.refs_3_, ...), custom_call_target="tpu_custom_call" | custom-call | flops 12000000000 | bytes 12000000 | tf_op jit(solution)/shard_map/pallas_call | solution.py:100
  108.3 2.8 copy-done.26
  111.1 2.4 collective-permute-done.14.refs_1_
  116.5 5.1 %shard_map.296.refs_6_ = bf16[832,16,128]{2,1,0:T(8,128)(2,1)S(1)} custom-call(s32[4]{0:T(128)S(1)} %pad_add_fusion.5.refs_0_, bf16[416,768]{1,0:T(8,128)(2,1)S(1)} %collective-permute-done.14.refs_1_, bf16[416,768]{1,0:T(8,128)(2,1)S(1)} %collective-permute-done.22.refs_2_, bf16[416,768]{1,0:T(8,128)(2,1)S(1)} %collective-permute-done.17.refs_3_, ...), custom_call_target="tpu_custom_call" | custom-call | flops 6000000000 | bytes 6000000 | tf_op jit(solution)/shard_map/pallas_call | solution.py:100
  123.5 108.6 %shard_map.297 = (bf16[832,768]{1,0:T(8,128)(2,1)}, bf16[832,768]{1,0:T(8,128)(2,1)}, bf16[832,768]{1,0:T(8,128)(2,1)}, bf16[832,768]{1,0:T(8,128)(2,1)}, bf16[8...) custom-call(s32[14592]{0:T(1024)} %broadcast_and_fusion.refs_0_, ...), custom_call_target="tpu_custom_call" | custom-call | flops 20000000000 | bytes 60000000 | tf_op jit(solution)/shard_map/pallas_call | solution.py:289
  233.6 2.7 collective-permute-done.25
  239.4 3.2 collective-permute-start.27
  242.7 2.5 collective-permute-done.27
  248.4 2.7 collective-permute-done.29
  251.2 2.8 add_convert_fusion.6
  254.0 2.5 add_convert_fusion.8
  258.3 2.6 add_convert_fusion.3
  262.5 4.6 %collective-permute-start.34 = (bf16[192,128]{1,0:T(8,128)(2,1)S(1)}, bf16[192,128]{1,0:T(8,128)(2,1)S(1)}, u32[]{:S(2)}, u32[]{:S(2)}) collective-permute-start(bf16[192,128]{1,0:T(8,128)(2,1)S(1)} %fusion.8), channel_id=1, source_target_pairs={{0,16},{8,24},{16,0},{24,8},{1,17},{9,25},{17,1},{25,9},{2,18},{10... | collective-permute-start | bytes 147464 | tf_op jit(solution)/shard_map/ppermute | solution.py:919
  267.4 2.8 collective-permute-done.34
  276.0 9.3 %shard_map.298 = (f32[416,768]{1,0:T(8,128)}, bf16[416,768]{1,0:T(8,128)(2,1)}, f32[416,768]{1,0:T(8,128)}, bf16[2560,128]{1,0:T(8,128)(2,1)}, bf16[768,128]{1,0:T(8,128)(2,1)}, /*index=5*/bf16[768,128]{1,0:T(8,128)(2,1)}) custom-call(s32[16]{0:T(128)} %copy-done.7, s32[2]{0:T(128)} %copy-done.20, bf16[1456,384]{1,0:T(8,128)(2,1)} %copy-done.49, ...), custom_call_target="tpu_custom_call" | custom-call | flops 6000000000 | bytes 15000000 | tf_op jit(solution)/shard_map/pallas_call | solution.py:765
  286.4 15.4 %shard_map.299 = (bf16[416,768]{1,0:T(8,128)(2,1)}, bf16[2304,128]{1,0:T(8,128)(2,1)}, bf16[2304,128]{1,0:T(8,128)(2,1)}) custom-call(s32[16]{0:T(128)} %copy-done.7, s32[2]{0:T(128)} %copy-done.20, bf16[944,384]{1,0:T(8,128)(2,1)} %maximum_maximum_fusion.2.refs_0_, bf16[944,384]{1,0:T(8,128)(2,1)} %copy-done, bf16[944,384]{1,0:T(8,128)(2,1)} %copy-done.1, ...), custom_call_target="tpu_custom_call" | custom-call | flops 8999999488 | bytes 15000000 | tf_op jit(solution)/shard_map/pallas_call | solution.py:833
  305.8 3.0 collective-permute-done.39
  314.8 6.2 %collective-permute-done.40 = bf16[1088,128]{1,0:T(8,128)(2,1)S(1)} collective-permute-done((bf16[1088,128]{1,0:T(8,128)(2,1)}, bf16[1088,128]{1,0:T(8,128)(2,1)S(1)}, u32[]{:S(2)}, u32[]{:S(2)}) %collective-permute-start.40) | collective-permute-done | bytes 278560 | tf_op jit(solution)/shard_map/ppermute | solution.py:869
  321.0 4.8 %collective-permute-done.41 = bf16[1088,128]{1,0:T(8,128)(2,1)S(1)} collective-permute-done((bf16[1088,128]{1,0:T(8,128)(2,1)}, bf16[1088,128]{1,0:T(8,128)(2,1)S(1)}, u32[]{:S(2)}, u32[]{:S(2)}) %collective-permute-start.41) | collective-permute-done | bytes 278560 | tf_op jit(solution)/shard_map/ppermute | solution.py:869
  331.5 3.5 collective-permute-start.43
  334.9 2.4 collective-permute-start.45
  339.2 3.3 collective-permute-done.44
  350.5 7.6 %collective-permute-done.49.refs_1_ = bf16[416,384]{1,0:T(8,128)(2,1)S(1)} collective-permute-done((bf16[416,384]{1,0:T(8,128)(2,1)S(1)}, bf16[416,384]{1,0:T(8,128)(2,1)S(1)}, u32[]{:S(2)}, u32[]{:S(2)}) %collective-permute-start.49) | collective-permute-done | bytes 319520 | tf_op jit(solution)/shard_map/ppermute | solution.py:869
  361.7 5.1 %collective-permute-done.50.one = bf16[704,128]{1,0:T(8,128)(2,1)S(1)} collective-permute-done((bf16[704,128]{1,0:T(8,128)(2,1)S(1)}, bf16[704,128]{1,0:T(8,128)(2,1)S(1)}, u32[]{:S(2)}, u32[]{:S(2)}) %collective-permute-start.50) | collective-permute-done | bytes 180256 | tf_op jit(solution)/shard_map/ppermute | solution.py:869
  (324 shorter events, 108.0 us)
Async XLA Ops:
  6.2 25.7 %collective-permute-start = (bf16[944,384]{1,0:T(8,128)(2,1)}, bf16[944,384]{1,0:T(8,128)(2,1)S(1)}, u32[]{:S(2)}, u32[]{:S(2)}) collective-permute-start(bf16[944,384]{1,0:T(8,128)(2,1)} %maximum_maximum_fusion.2.refs_0_), channel_id=1, source_target_pairs={{0,1},{1,0},{2,3},{3,2},{4,5},{5,4},{6,7},{7,6},{8,9},{9,8},{10,11... | collective-permute-start | bytes 2174984 | tf_op jit(solution)/shard_map/ppermute | solution.py:869
  9.1 22.8 %collective-permute-start.1 = (bf16[944,384]{1,0:T(8,128)(2,1)}, bf16[944,384]{1,0:T(8,128)(2,1)S(1)}, u32[]{:S(2)}, u32[]{:S(2)}) collective-permute-start(bf16[944,384]{1,0:T(8,128)(2,1)} %maximum_maximum_fusion.2.refs_0_), channel_id=1, source_target_pairs={{0,2},{1,3},{2,0},{3,1},{4,6},{5,7},{6,4},{7,5},{8,10},{9,11},{10,... | collective-permute-start | bytes 2174984 | tf_op jit(solution)/shard_map/ppermute | solution.py:869
  32.0 11.4 %collective-permute-start.7 = (bf16[416,384]{1,0:T(8,128)(2,1)S(1)}, bf16[416,384]{1,0:T(8,128)(2,1)S(1)}, u32[]{:S(2)}, u32[]{:S(2)}) collective-permute-start(bf16[416,384]{1,0:T(8,128)(2,1)S(1)} %copy-done.16), channel_id=1, source_target_pairs={{0,3},{1,2},{2,1},{3,0},{4,7},{5,6},{6,5},{7,4},{8,11},{9,10},{10,... | collective-permute-start | bytes 958472 | tf_op jit(solution)/shard_map/ppermute | solution.py:869
  32.1 15.6 %collective-permute-start.8 = (bf16[416,384]{1,0:T(8,128)(2,1)S(1)}, bf16[416,384]{1,0:T(8,128)(2,1)S(1)}, u32[]{:S(2)}, u32[]{:S(2)}) collective-permute-start(bf16[416,384]{1,0:T(8,128)(2,1)S(1)} %copy-done.14), channel_id=1, source_target_pairs={{0,2},{1,3},{2,0},{3,1},{4,6},{5,7},{6,4},{7,5},{8,10},{9,11},{10,... | collective-permute-start | bytes 958472 | tf_op jit(solution)/shard_map/ppermute | solution.py:869
  34.1 15.3 %collective-permute-start.9 = (bf16[416,384]{1,0:T(8,128)(2,1)S(1)}, bf16[416,384]{1,0:T(8,128)(2,1)S(1)}, u32[]{:S(2)}, u32[]{:S(2)}) collective-permute-start(bf16[416,384]{1,0:T(8,128)(2,1)S(1)} %copy-done.12), channel_id=1, source_target_pairs={{0,1},{1,0},{2,3},{3,2},{4,5},{5,4},{6,7},{7,6},{8,9},{9,8},{10,11... | collective-permute-start | bytes 958472 | tf_op jit(solution)/shard_map/ppermute | solution.py:869
  37.6 17.9 %collective-permute-start.2 = (bf16[944,384]{1,0:T(8,128)(2,1)S(1)}, bf16[944,384]{1,0:T(8,128)(2,1)S(1)}, u32[]{:S(2)}, u32[]{:S(2)}) collective-permute-start(bf16[944,384]{1,0:T(8,128)(2,1)S(1)} %broadcast_select_fusion), channel_id=1, source_target_pairs={{0,2},{1,3},{2,0},{3,1},{4,5},{5,4},{6,7},{7,6},{8,10},{9,11},{10,... | collective-permute-start | bytes 2174984 | tf_op jit(solution)/shard_map/ppermute | solution.py:884
  38.2 20.5 %collective-permute-start.4 = (bf16[944,384]{1,0:T(8,128)(2,1)S(1)}, bf16[944,384]{1,0:T(8,128)(2,1)S(1)}, u32[]{:S(2)}, u32[]{:S(2)}) collective-permute-start(bf16[944,384]{1,0:T(8,128)(2,1)S(1)} %collective-permute-done.refs_1_), channel_id=1, source_target_pairs={{0,4},{4,0},{1,5},{5,1},{2,6},{6,2},{3,7},{7,3},{8,12},{12,8},{9,1... | collective-permute-start | bytes 2174984 | tf_op jit(solution)/shard_map/ppermute | solution.py:865
  43.5 16.6 %collective-permute-start.5 = (bf16[944,384]{1,0:T(8,128)(2,1)S(1)}, bf16[944,384]{1,0:T(8,128)(2,1)S(1)}, u32[]{:S(2)}, u32[]{:S(2)}) collective-permute-start(bf16[944,384]{1,0:T(8,128)(2,1)S(1)} %collective-permute-done.1.refs_2_), channel_id=1, source_target_pairs={{0,4},{4,0},{1,5},{5,1},{2,6},{6,2},{3,7},{7,3},{8,12},{12,8},{9,1... | collective-permute-start | bytes 2174984 | tf_op jit(solution)/shard_map/ppermute | solution.py:865
  55.5 23.6 %collective-permute-start.13 = (bf16[416,768]{1,0:T(8,128)(2,1)S(1)}, bf16[416,768]{1,0:T(8,128)(2,1)S(1)}, u32[]{:S(2)}, u32[]{:S(2)}) collective-permute-start(bf16[416,768]{1,0:T(8,128)(2,1)S(1)} %pad_maximum_fusion.4.refs_3_.refs_10_), channel_id=1, source_target_pairs={{0,4},{4,0},{1,5},{5,1},{2,6},{6,2},{3,7},{7,3},{8,12},{12,8},{9,1... | collective-permute-start | bytes 1916936 | tf_op jit(solution)/shard_map/ppermute | solution.py:865
  58.7 21.0 %collective-permute-start.15 = (bf16[416,768]{1,0:T(8,128)(2,1)S(1)}, bf16[416,768]{1,0:T(8,128)(2,1)S(1)}, u32[]{:S(2)}, u32[]{:S(2)}) collective-permute-start(bf16[416,768]{1,0:T(8,128)(2,1)S(1)} %pad_maximum_fusion.4.refs_3_.refs_10_), channel_id=1, source_target_pairs={{0,1},{1,0},{2,3},{3,2},{4,5},{5,4},{6,7},{7,6},{8,9},{9,8},{10,11... | collective-permute-start | bytes 1916936 | tf_op jit(solution)/shard_map/ppermute | solution.py:869
  60.0 19.7 %collective-permute-start.16 = (bf16[416,768]{1,0:T(8,128)(2,1)S(1)}, bf16[416,768]{1,0:T(8,128)(2,1)S(1)}, u32[]{:S(2)}, u32[]{:S(2)}) collective-permute-start(bf16[416,768]{1,0:T(8,128)(2,1)S(1)} %pad_maximum_fusion.4.refs_3_.refs_10_), channel_id=1, source_target_pairs={{0,2},{1,3},{2,0},{3,1},{4,6},{5,7},{6,4},{7,5},{8,10},{9,11},{10,... | collective-permute-start | bytes 1916936 | tf_op jit(solution)/shard_map/ppermute | solution.py:869
  77.4 16.8 %collective-permute-start.10 = (bf16[416,768]{1,0:T(8,128)(2,1)S(1)}, bf16[416,768]{1,0:T(8,128)(2,1)S(1)}, u32[]{:S(2)}, u32[]{:S(2)}) collective-permute-start(bf16[416,768]{1,0:T(8,128)(2,1)S(1)} %get-tuple-element.124.refs_1_.refs_6_), channel_id=1, source_target_pairs={{0,1},{1,0},{2,3},{3,2},{4,5},{5,4},{6,7},{7,6},{8,9},{9,8},{10,11... | collective-permute-start | bytes 1916936 | tf_op jit(solution)/shard_map/ppermute | solution.py:869
  79.1 16.5 %collective-permute-start.11 = (bf16[416,768]{1,0:T(8,128)(2,1)S(1)}, bf16[416,768]{1,0:T(8,128)(2,1)S(1)}, u32[]{:S(2)}, u32[]{:S(2)}) collective-permute-start(bf16[416,768]{1,0:T(8,128)(2,1)S(1)} %get-tuple-element.124.refs_1_.refs_6_), channel_id=1, source_target_pairs={{0,2},{1,3},{2,0},{3,1},{4,6},{5,7},{6,4},{7,5},{8,10},{9,11},{10,... | collective-permute-start | bytes 1916936 | tf_op jit(solution)/shard_map/ppermute | solution.py:869
  79.7 17.2 %collective-permute-start.20 = (bf16[416,768]{1,0:T(8,128)(2,1)S(1)}, bf16[416,768]{1,0:T(8,128)(2,1)S(1)}, u32[]{:S(2)}, u32[]{:S(2)}) collective-permute-start(bf16[416,768]{1,0:T(8,128)(2,1)S(1)} %collective-permute-done.15.refs_5_), channel_id=1, source_target_pairs={{0,4},{4,0},{1,5},{5,1},{2,6},{6,2},{3,7},{7,3},{8,12},{12,8},{9,1... | collective-permute-start | bytes 1916936 | tf_op jit(solution)/shard_map/ppermute | solution.py:865
  79.7 18.7 %collective-permute-start.21 = (bf16[416,768]{1,0:T(8,128)(2,1)S(1)}, bf16[416,768]{1,0:T(8,128)(2,1)S(1)}, u32[]{:S(2)}, u32[]{:S(2)}) collective-permute-start(bf16[416,768]{1,0:T(8,128)(2,1)S(1)} %collective-permute-done.16.refs_6_), channel_id=1, source_target_pairs={{0,4},{4,0},{1,5},{5,1},{2,6},{6,2},{3,7},{7,3},{8,12},{12,8},{9,1... | collective-permute-start | bytes 1916936 | tf_op jit(solution)/shard_map/ppermute | solution.py:865
  96.2 14.9 %collective-permute-start.17 = (bf16[416,768]{1,0:T(8,128)(2,1)S(1)}, bf16[416,768]{1,0:T(8,128)(2,1)S(1)}, u32[]{:S(2)}, u32[]{:S(2)}) collective-permute-start(bf16[416,768]{1,0:T(8,128)(2,1)S(1)} %broadcast_select_fusion.1), channel_id=1, source_target_pairs={{0,2},{1,3},{2,0},{3,1},{4,5},{5,4},{6,7},{7,6},{8,10},{9,11},{10,... | collective-permute-start | bytes 1916936 | tf_op jit(solution)/shard_map/ppermute | solution.py:884
  97.0 16.6 %collective-permute-start.14 = (bf16[416,768]{1,0:T(8,128)(2,1)S(1)}, bf16[416,768]{1,0:T(8,128)(2,1)S(1)}, u32[]{:S(2)}, u32[]{:S(2)}) collective-permute-start(bf16[416,768]{1,0:T(8,128)(2,1)S(1)} %broadcast_select_fusion.2), channel_id=1, source_target_pairs={{0,2},{1,3},{2,0},{3,1},{4,5},{5,4},{6,7},{7,6},{8,10},{9,11},{10,... | collective-permute-start | bytes 1916936 | tf_op jit(solution)/shard_map/ppermute | solution.py:884
  232.3 10.4 %collective-permute-start.24 = (bf16[832,896]{1,0:T(8,128)(2,1)}, bf16[832,896]{1,0:T(8,128)(2,1)}, u32[]{:S(2)}, u32[]{:S(2)}) collective-permute-start(bf16[832,896]{1,0:T(8,128)(2,1)} %get-tuple-element.140), channel_id=1, source_target_pairs={{0,4},{4,0},{1,5},{5,1},{2,6},{6,2},{3,7},{7,3},{8,12},{12,8},{9,1... | collective-permute-start | bytes 4472840 | tf_op jit(solution)/shard_map/ppermute | solution.py:865
  238.1 13.1 %collective-permute-start.31 = (bf16[832,768]{1,0:T(8,128)(2,1)}, bf16[832,768]{1,0:T(8,128)(2,1)}, u32[]{:S(2)}, u32[]{:S(2)}) collective-permute-start(bf16[832,768]{1,0:T(8,128)(2,1)} %get-tuple-element.154), channel_id=1, source_target_pairs={{0,4},{4,0},{1,5},{5,1},{2,6},{6,2},{3,7},{7,3},{8,12},{12,8},{9,1... | collective-permute-start | bytes 3833864 | tf_op jit(solution)/shard_map/ppermute | solution.py:865
  238.3 15.7 %collective-permute-start.30 = (bf16[832,768]{1,0:T(8,128)(2,1)}, bf16[832,768]{1,0:T(8,128)(2,1)}, u32[]{:S(2)}, u32[]{:S(2)}) collective-permute-start(bf16[832,768]{1,0:T(8,128)(2,1)} %get-tuple-element.152), channel_id=1, source_target_pairs={{0,4},{4,0},{1,5},{5,1},{2,6},{6,2},{3,7},{7,3},{8,12},{12,8},{9,1... | collective-permute-start | bytes 3833864 | tf_op jit(solution)/shard_map/ppermute | solution.py:865
  238.7 19.6 %collective-permute-start.26 = (bf16[832,896]{1,0:T(8,128)(2,1)S(1)}, bf16[832,896]{1,0:T(8,128)(2,1)}, u32[]{:S(2)}, u32[]{:S(2)}) collective-permute-start(bf16[832,896]{1,0:T(8,128)(2,1)S(1)} %add_convert_fusion), channel_id=1, source_target_pairs={{0,1},{1,0},{2,3},{3,2},{4,6},{5,7},{6,4},{7,5},{8,9},{9,8},{10,11... | collective-permute-start | bytes 4472840 | tf_op jit(solution)/shard_map/ppermute | solution.py:884
  260.9 11.6 %collective-permute-start.32 = (bf16[416,896]{1,0:T(8,128)(2,1)S(1)}, bf16[416,896]{1,0:T(8,128)(2,1)S(1)}, u32[]{:S(2)}, u32[]{:S(2)}) collective-permute-start(bf16[416,896]{1,0:T(8,128)(2,1)S(1)} %get-tuple-element.261), channel_id=1, source_target_pairs={{0,2},{1,3},{2,0},{3,1},{4,5},{5,4},{6,7},{7,6},{8,10},{9,11},{10,... | collective-permute-start | bytes 2236424 | tf_op jit(solution)/shard_map/ppermute | solution.py:884
  272.5 29.3 %collective-permute-start.36 = (bf16[416,768]{1,0:T(8,128)(2,1)}, bf16[416,768]{1,0:T(8,128)(2,1)S(1)}, u32[]{:S(2)}, u32[]{:S(2)}) collective-permute-start(bf16[416,768]{1,0:T(8,128)(2,1)} %get-tuple-element.170), channel_id=1, source_target_pairs={{0,2},{1,3},{2,0},{3,1},{4,5},{5,4},{6,7},{7,6},{8,10},{9,11},{10,... | collective-permute-start | bytes 1916936 | tf_op jit(solution)/shard_map/ppermute | solution.py:884
  272.7 29.1 %collective-permute-start.37 = (bf16[416,768]{1,0:T(8,128)(2,1)}, bf16[416,768]{1,0:T(8,128)(2,1)S(1)}, u32[]{:S(2)}, u32[]{:S(2)}) collective-permute-start(bf16[416,768]{1,0:T(8,128)(2,1)} %get-tuple-element.171), channel_id=1, source_target_pairs={{0,1},{1,0},{2,3},{3,2},{4,6},{5,7},{6,4},{7,5},{8,9},{9,8},{10,11... | collective-permute-start | bytes 1916936 | tf_op jit(solution)/shard_map/ppermute | solution.py:884
  274.8 27.1 %collective-permute-start.38 = (bf16[416,768]{1,0:T(8,128)(2,1)}, bf16[416,768]{1,0:T(8,128)(2,1)}, u32[]{:S(2)}, u32[]{:S(2)}) collective-permute-start(bf16[416,768]{1,0:T(8,128)(2,1)} %get-tuple-element.172), channel_id=1, source_target_pairs={{0,3},{1,2},{2,1},{3,0},{4,7},{5,6},{6,5},{7,4},{8,11},{9,10},{10,... | collective-permute-start | bytes 1916936 | tf_op jit(solution)/shard_map/ppermute | solution.py:884
  311.3 9.7 %collective-permute-start.40 = (bf16[1088,128]{1,0:T(8,128)(2,1)}, bf16[1088,128]{1,0:T(8,128)(2,1)S(1)}, u32[]{:S(2)}, u32[]{:S(2)}) collective-permute-start(bf16[1088,128]{1,0:T(8,128)(2,1)} %get-tuple-element.278), channel_id=1, source_target_pairs={{0,1},{1,0},{2,3},{3,2},{4,5},{5,4},{6,7},{7,6},{8,9},{9,8},{10,11... | collective-permute-start | bytes 835592 | tf_op jit(solution)/shard_map/ppermute | solution.py:869
  311.9 13.9 %collective-permute-start.41 = (bf16[1088,128]{1,0:T(8,128)(2,1)}, bf16[1088,128]{1,0:T(8,128)(2,1)S(1)}, u32[]{:S(2)}, u32[]{:S(2)}) collective-permute-start(bf16[1088,128]{1,0:T(8,128)(2,1)} %get-tuple-element.280), channel_id=1, source_target_pairs={{0,2},{1,3},{2,0},{3,1},{4,6},{5,7},{6,4},{7,5},{8,10},{9,11},{10,... | collective-permute-start | bytes 835592 | tf_op jit(solution)/shard_map/ppermute | solution.py:869
  313.6 13.4 %collective-permute-start.42 = (bf16[1088,128]{1,0:T(8,128)(2,1)S(1)}, bf16[1088,128]{1,0:T(8,128)(2,1)}, u32[]{:S(2)}, u32[]{:S(2)}) collective-permute-start(bf16[1088,128]{1,0:T(8,128)(2,1)S(1)} %get-tuple-element.279), channel_id=1, source_target_pairs={{0,3},{1,2},{2,1},{3,0},{4,7},{5,6},{6,5},{7,4},{8,11},{9,10},{10,... | collective-permute-start | bytes 835592 | tf_op jit(solution)/shard_map/ppermute | solution.py:869
  337.9 30.8 %collective-permute-start.54 = (bf16[416,384]{1,0:T(8,128)(2,1)S(1)}, bf16[416,384]{1,0:T(8,128)(2,1)S(1)}, u32[]{:S(2)}, u32[]{:S(2)}) collective-permute-start(bf16[416,384]{1,0:T(8,128)(2,1)S(1)} %get-tuple-element.272), channel_id=1, source_target_pairs={{0,2},{1,3},{2,0},{3,1},{4,6},{5,7},{6,4},{7,5},{8,10},{9,11},{10,... | collective-permute-start | bytes 958472 | tf_op jit(solution)/shard_map/ppermute | solution.py:869
  347.6 10.5 %collective-permute-start.49 = (bf16[416,384]{1,0:T(8,128)(2,1)S(1)}, bf16[416,384]{1,0:T(8,128)(2,1)S(1)}, u32[]{:S(2)}, u32[]{:S(2)}) collective-permute-start(bf16[416,384]{1,0:T(8,128)(2,1)S(1)} %get-tuple-element.271), channel_id=1, source_target_pairs={{0,1},{1,0},{2,3},{3,2},{4,5},{5,4},{6,7},{7,6},{8,9},{9,8},{10,11... | collective-permute-start | bytes 958472 | tf_op jit(solution)/shard_map/ppermute | solution.py:869
  348.8 19.9 %collective-permute-start.55 = (bf16[416,384]{1,0:T(8,128)(2,1)S(1)}, bf16[416,384]{1,0:T(8,128)(2,1)S(1)}, u32[]{:S(2)}, u32[]{:S(2)}) collective-permute-start(bf16[416,384]{1,0:T(8,128)(2,1)S(1)} %get-tuple-element.270), channel_id=1, source_target_pairs={{0,3},{1,2},{2,1},{3,0},{4,7},{5,6},{6,5},{7,4},{8,11},{9,10},{10,... | collective-permute-start | bytes 958472 | tf_op jit(solution)/shard_map/ppermute | solution.py:869
  358.1 8.7 %collective-permute-start.50 = (bf16[704,128]{1,0:T(8,128)(2,1)S(1)}, bf16[704,128]{1,0:T(8,128)(2,1)S(1)}, u32[]{:S(2)}, u32[]{:S(2)}) collective-permute-start(bf16[704,128]{1,0:T(8,128)(2,1)S(1)} %slice.317), channel_id=1, source_target_pairs={{0,1},{1,0},{2,3},{3,2},{4,5},{5,4},{6,7},{7,6},{8,9},{9,8},{10,11... | collective-permute-start | bytes 540680 | tf_op jit(solution)/shard_map/ppermute | solution.py:869
  (79 other events, 626.3 us)

commit v5 on v4

--- a/solution.py
+++ b/solution.py
@@ -704,6 +704,20 @@
     )(picks, place, *blocks, own_b, own_a, *out_w, x, gain_one, gain_two, b_out)
 
 
+def put_rows(part, p, value):
+    value = value.astype(bf16)
+    for r in range(2):
+        for c in range(4):
+            part[r, c, 96 * p : 96 * p + 96, :] = value[384 * r + 96 * c : 384 * r + 96 * c + 96, :]
+
+
+def put_cols(part, p, value):
+    value = value.astype(bf16)
+    for r in range(2):
+        for c in range(4):
+            part[r, c, 96 * p : 96 * p + 96, :] = value[192 * c + 96 * r : 192 * c + 96 * r + 96, :]
+
+
 def out_back_kernel(picks_ref, place_ref, *refs):
     (
         far_block, own_a, out_near, out_far, gain_two, b_out, two_ref, resid_ref, mixed_ref, lows_ref,
@@ -751,8 +765,8 @@
     for copy in copies:
         copy.wait()
     mixed_grad_out[...] = (dot_nt(grad_attn, w_out[...]) + dot_nt(grad_low, a_out[...])).astype(bf16)
-    a_part_out[...] = dot_tn(mixed_ref[...], grad_low).astype(bf16)
-    b_part_out[...] = dot_tn(grad_attn, lows_ref[:, 384:512]).astype(bf16)
+    put_rows(a_part_out, 0, dot_tn(mixed_ref[...], grad_low))
+    put_cols(b_part_out, 0, dot_tn(grad_attn, lows_ref[:, 384:512]))
     both_out[2432:BOTH_ROWS, :] = jnp.zeros((BOTH_ROWS - 2432, 128), bf16)
 
 
@@ -776,8 +790,8 @@
             jax.ShapeDtypeStruct((rows, D), bf16),
             jax.ShapeDtypeStruct((rows, D), f32),
             jax.ShapeDtypeStruct((BOTH_ROWS, 128), bf16),
-            jax.ShapeDtypeStruct((D, 128), bf16),
-            jax.ShapeDtypeStruct((D, 128), bf16),
+            jax.ShapeDtypeStruct((2, 4, 96, 128), bf16),
+            jax.ShapeDtypeStruct((2, 4, 96, 128), bf16),
         ],
         compiler_params=pltpu.CompilerParams(vmem_limit_bytes=60 * 1024 * 1024),
         cost_estimate=pl.CostEstimate(flops=6_000_000_000, bytes_accessed=15_000_000, transcendentals=100_000),
@@ -822,8 +836,8 @@
         piece = grads[p]
         grad_low = jnp.where(mask, dot_nt(piece, b_qkv[p]), 0.0).astype(bf16)
         grad_normed = grad_normed + dot_nt(piece, w_qkv[p]) + dot_nt(grad_low, a_qkv[p])
-        a_part_out[D * p : D * p + D, :] = dot_tn(normed, grad_low).astype(bf16)
-        b_part_out[D * p : D * p + D, :] = dot_tn(piece, lows_ref[:, 128 * p : 128 * p + 128]).astype(bf16)
+        put_cols(a_part_out, p, dot_tn(normed, grad_low))
+        put_rows(b_part_out, p, dot_tn(piece, lows_ref[:, 128 * p : 128 * p + 128]))
     unit, inverse = norm_stats(x_ref[...].astype(f32))
     tokens_out[...] = (resid_grad[...] + norm_back(grad_normed, gain_one[...], unit, inverse)).astype(bf16)
 
@@ -850,8 +864,8 @@
         ),
         out_shape=[
             jax.ShapeDtypeStruct((rows, D), bf16),
-            jax.ShapeDtypeStruct((3 * D, 128), bf16),
-            jax.ShapeDtypeStruct((3 * D, 128), bf16),
+            jax.ShapeDtypeStruct((2, 4, 288, 128), bf16),
+            jax.ShapeDtypeStruct((2, 4, 288, 128), bf16),
         ],
         compiler_params=pltpu.CompilerParams(vmem_limit_bytes=60 * 1024 * 1024),
         cost_estimate=pl.CostEstimate(flops=9_000_000_000, bytes_accessed=15_000_000, transcendentals=1000),
@@ -923,13 +937,8 @@
     return jnp.concatenate(by_place([value] + [across_dp(value, s) for s in range(1, 4)], lax.axis_index("dp")))
 
 
-def part_share(col_parts, row_parts, both_parts, place):
-    col_parts = at_place(col_parts.reshape(4, 4, 2, 96, 128), 2, place)
-    row_parts = at_place(row_parts.reshape(4, 2, 4, 96, 128), 1, place)
-    both_parts = at_place(both_parts.reshape(2, 4, BOTH_ROWS // 8, 128), 0, place)
-    col_parts = col_parts.swapaxes(0, 1).reshape(4, 384, 128)
-    row_parts = row_parts.swapaxes(0, 1).reshape(4, 384, 128)
-    return jnp.concatenate([col_parts, row_parts, both_parts], axis=1)
+def part_share(parts, place):
+    return jnp.concatenate([at_place(part, 0, place) for part in parts], axis=1)
 
 
 def exchange_col(value, col):
@@ -1063,16 +1072,14 @@
         picks, place, blocks, b_qkv, x, gain_one, normed, qkv, probs, lows, resid_grad, mixed_grad
     )
     part_a_qkv, part_b_qkv, *sums = lax.optimization_barrier((part_a_qkv, part_b_qkv, *sums))
-    col_parts = jnp.concatenate([part_a_qkv, part_b_out])
-    row_parts = jnp.concatenate([part_b_qkv, part_a_out])
-    theirs = across_row(part_share(col_parts, row_parts, both_parts, 1 - row))
-    shared = added(part_share(col_parts, row_parts, both_parts, row), theirs).astype(bf16)
+    parts = (part_a_qkv, part_b_out, part_b_qkv, part_a_out, both_parts.reshape(2, 4, BOTH_ROWS // 8, 128))
+    theirs = across_row(part_share(parts, 1 - row))
+    shared = added(part_share(parts, row), theirs).astype(bf16)
     found = exchange_col(shared, col)
     mine = added(*found).astype(bf16)
     mine, grad_tokens, base = lax.optimization_barrier((mine, grad_tokens, base))
     moves = to_features(grad_tokens, (base + added(*sums)).astype(bf16), col)
     mine = spread_dp(scatter_dp(mine)) if four_dp else lax.psum(mine, "dp")
-    mine, moves[1] = lax.optimization_barrier((mine, moves[1]))
     got = [across_col(mine[384:], s) for s in range(1, 4)]
     far = across_row(jnp.concatenate([mine[:384], mine[768:]] + [one[384:] for one in got]))
     block_out, grad_tokens = merge_call(place, moves, tokens.shape[0])

time: 381 us -> 378 us (level)
  starting transfers between devices: 53.4 us -> 45.6 us
  local copies, waits for them, and re-layouts: 27.6 us -> 32.2 us
  waiting for transfers between devices: 78.3 us -> 82.2 us
    ppermute x12, starting transfers between devices: 20.4 us -> 12.8 us  [across_dp(): return lax.ppermute(value, 'dp', [(i, i ^ step) for i in range(4)])]
    ppermute x8, waiting for transfers between devices: 10.4 us -> 16.7 us  [across_chip(): return lax.ppermute(value, ('row', 'col'), pairs)]
    unnamed x127 -> x137, local copies, waits for them, and re-layouts: 22.4 us -> 27.4 us
  transfers between devices with their start and end apart: 56 -> 56, of which waited for: 30 -> 28; matrix products, arithmetic and copies ran while one was open for 10% -> 10% of each run, Pallas kernels for 15% -> 15%
where the time goes in v5:
time: 378 us; the launch traced here: 374 us
  Pallas kernels  172 us (46%)
  waiting for transfers between devices  82.2 us (22%)
  starting transfers between devices  45.6 us (12%)
  other arithmetic  40.1 us (11%)
  local copies, waits for them, and re-layouts  32.2 us (9%)
    pallas_call x1, Pallas kernels, moe_call(): pl.pallas_call(lambda *refs: moe_kernel(places, *refs), grid_spec=pltpu.P...  108 us
    ppermute x18, waiting for transfers between devices, across_col(): return lax.ppermute(value, 'col', [(i, i ^ step) for i in range(4)])  43.6 us
    unnamed x137, local copies, waits for them, and re-layouts  27.4 us
    ppermute x18, starting transfers between devices, across_col(): return lax.ppermute(value, 'col', [(i, i ^ step) for i in range(4)])  22.2 us
    pallas_call x3, Pallas kernels, table_call(): pl.pallas_call(lambda *refs: table_kernel(n, *refs), grid_spec=pltpu.Pref...  20.1 us
    ppermute x8, waiting for transfers between devices, across_chip(): return lax.ppermute(value, ('row', 'col'), pairs)  16.7 us
    pallas_call x1, Pallas kernels, qkv_back_call(): pl.pallas_call(qkv_back_kernel, grid_spec=pltpu.PrefetchScalarGridSpec(nu...  15.3 us
    ppermute x12, waiting for transfers between devices, across_dp(): return lax.ppermute(value, 'dp', [(i, i ^ step) for i in range(4)])  13.3 us
  transfers between devices with their start and end apart: 56, of which 28 were waited for; matrix products, arithmetic and copies ran while one was open for 10% of the time, Pallas kernels for 15%

profile of v5, /device:TPU:0, one launch (start us, length us, event | category | flops | bytes accessed | tf_op | source)
XLA Modules:
  0.0 374.2 jit_solution(15616931458250838447)
XLA Ops:
  6.1 2.9 collective-permute-start
  22.5 8.6 %sort.14 = (s32[14592]{0:T(1024)S(1)}, s32[14592]{0:T(1024)}) sort(s32[14592]{0:T(1024)} %pad_add_fusion, s32[14592]{0:T(1024)S(1)} %iota.71), dimensions={0}, to_apply=%region_1.2 | sort | flops 204288 | bytes 233472 | tf_op jit(solution)/shard_map/sort | solution.py:355
  38.2 5.3 %collective-permute-done.7 = bf16[416,384]{1,0:T(8,128)(2,1)S(1)} collective-permute-done((bf16[416,384]{1,0:T(8,128)(2,1)S(1)}, bf16[416,384]{1,0:T(8,128)(2,1)S(1)}, u32[]{:S(2)}, u32[]{:S(2)}) %collective-permute-start.7) | collective-permute-done | bytes 319520 | tf_op jit(solution)/shard_map/ppermute | solution.py:883
  43.5 4.3 %collective-permute-done.8 = bf16[416,384]{1,0:T(8,128)(2,1)S(1)} collective-permute-done((bf16[416,384]{1,0:T(8,128)(2,1)S(1)}, bf16[416,384]{1,0:T(8,128)(2,1)S(1)}, u32[]{:S(2)}, u32[]{:S(2)}) %collective-permute-start.8) | collective-permute-done | bytes 319520 | tf_op jit(solution)/shard_map/ppermute | solution.py:883
  50.7 4.8 %collective-permute-done.2.refs_3_ = bf16[944,384]{1,0:T(8,128)(2,1)S(1)} collective-permute-done((bf16[944,384]{1,0:T(8,128)(2,1)S(1)}, bf16[944,384]{1,0:T(8,128)(2,1)S(1)}, u32[]{:S(2)}, u32[]{:S(2)}) %collective-permute-start.2) | collective-permute-done | bytes 725024 | tf_op jit(solution)/shard_map/ppermute | solution.py:898
  62.9 13.2 %shard_map.293 = (bf16[416,768]{1,0:T(8,128)(2,1)S(1)}, f32[416,768]{1,0:T(8,128)}, bf16[416,768]{1,0:T(8,128)(2,1)S(1)}, bf16[3,416,768]{2,1,0:T(8,128)(2,1)}, ...) custom-call(s32[16]{0:T(128)S(1)} %and_select_fusion.5.picks_ref, ...), custom_call_target="tpu_custom_call" | custom-call | flops 4000000000 | bytes 15000000 | tf_op jit(solution)/shard_map/pallas_call | solution.py:684
  80.2 5.1 %shard_map.294.refs_4_ = bf16[832,16,128]{2,1,0:T(8,128)(2,1)S(1)} custom-call(s32[4]{0:T(128)S(1)} %pad_add_fusion.3.refs_0_, bf16[416,768]{1,0:T(8,128)(2,1)S(1)} %get-tuple-element.122.refs_1_.refs_6_, bf16[416,768]{1,0:T(8,128)(2,1)S(1)} %collective-permute-done.12.refs_2_, bf16[416,768]{1,0:T(8,128)(2,1)S(1)} %pad_maximum_fusion.1.refs_3_.refs_10_, ...), custom_call_target="tpu_custom_call" | custom-call | flops 6000000000 | bytes 6000000 | tf_op jit(solution)/shard_map/pallas_call | solution.py:100
  87.1 6.9 %collective-permute-done.10.refs_1_ = bf16[416,768]{1,0:T(8,128)(2,1)S(1)} collective-permute-done((bf16[416,768]{1,0:T(8,128)(2,1)S(1)}, bf16[416,768]{1,0:T(8,128)(2,1)S(1)}, u32[]{:S(2)}, u32[]{:S(2)}) %collective-permute-start.10) | collective-permute-done | bytes 639008 | tf_op jit(solution)/shard_map/ppermute | solution.py:883
  98.4 9.8 %shard_map.295.refs_5_ = bf16[1664,16,128]{2,1,0:T(8,128)(2,1)S(1)} custom-call(s32[8]{0:T(128)S(1)} %pad_add_fusion.4.refs_0_, bf16[416,768]{1,0:T(8,128)(2,1)S(1)} %collective-permute-done.10.refs_1_, bf16[416,768]{1,0:T(8,128)(2,1)S(1)} %collective-permute-done.11.refs_2_, bf16[416,768]{1,0:T(8,128)(2,1)S(1)} %collective-permute-done.18.refs_3_, ...), custom_call_target="tpu_custom_call" | custom-call | flops 12000000000 | bytes 12000000 | tf_op jit(solution)/shard_map/pallas_call | solution.py:100
  108.2 2.8 copy-done.28
  111.0 2.4 collective-permute-done.14.refs_1_
  116.4 5.2 %shard_map.296.refs_6_ = bf16[832,16,128]{2,1,0:T(8,128)(2,1)S(1)} custom-call(s32[4]{0:T(128)S(1)} %pad_add_fusion.5.refs_0_, bf16[416,768]{1,0:T(8,128)(2,1)S(1)} %collective-permute-done.14.refs_1_, bf16[416,768]{1,0:T(8,128)(2,1)S(1)} %collective-permute-done.22.refs_2_, bf16[416,768]{1,0:T(8,128)(2,1)S(1)} %collective-permute-done.17.refs_3_, ...), custom_call_target="tpu_custom_call" | custom-call | flops 6000000000 | bytes 6000000 | tf_op jit(solution)/shard_map/pallas_call | solution.py:100
  123.3 108.5 %shard_map.297 = (bf16[832,768]{1,0:T(8,128)(2,1)}, bf16[832,768]{1,0:T(8,128)(2,1)}, bf16[832,768]{1,0:T(8,128)(2,1)}, bf16[832,768]{1,0:T(8,128)(2,1)}, bf16[8...) custom-call(s32[14592]{0:T(1024)} %broadcast_and_fusion.refs_0_, ...), custom_call_target="tpu_custom_call" | custom-call | flops 20000000000 | bytes 60000000 | tf_op jit(solution)/shard_map/pallas_call | solution.py:289
  233.3 3.4 collective-permute-done.25
  240.0 5.9 %collective-permute-done.29 = bf16[192,128]{1,0:T(8,128)(2,1)S(1)} collective-permute-done((bf16[192,128]{1,0:T(8,128)(2,1)S(1)}, bf16[192,128]{1,0:T(8,128)(2,1)S(1)}, u32[]{:S(2)}, u32[]{:S(2)}) %collective-permute-start.29) | collective-permute-done | bytes 49184 | tf_op jit(solution)/shard_map/ppermute | solution.py:933
  247.7 2.2 collective-permute-done.27
  251.8 2.7 add_convert_fusion.6
  254.4 4.4 %collective-permute-done.26 = bf16[832,896]{1,0:T(8,128)(2,1)} collective-permute-done((bf16[832,896]{1,0:T(8,128)(2,1)S(1)}, bf16[832,896]{1,0:T(8,128)(2,1)}, u32[]{:S(2)}, u32[]{:S(2)}) %collective-permute-start.26) | collective-permute-done | bytes 1490976 | tf_op jit(solution)/shard_map/ppermute | solution.py:898
  258.8 2.6 add_convert_fusion.3
  262.9 3.6 collective-permute-start.35
  268.6 4.5 %collective-permute-done.32.refs_12_ = bf16[416,896]{1,0:T(8,128)(2,1)} collective-permute-done((bf16[416,896]{1,0:T(8,128)(2,1)S(1)}, bf16[416,896]{1,0:T(8,128)(2,1)}, u32[]{:S(2)}, u32[]{:S(2)}) %collective-permute-start.32) | collective-permute-done | bytes 745504 | tf_op jit(solution)/shard_map/ppermute | solution.py:898
  276.6 9.3 %shard_map.298 = (f32[416,768]{1,0:T(8,128)}, bf16[416,768]{1,0:T(8,128)(2,1)}, f32[416,768]{1,0:T(8,128)}, bf16[2560,128]{1,0:T(8,128)(2,1)}, bf16[2,4,96,128]{...) custom-call(s32[16]{0:T(128)} %copy-done.7, s32[2]{0:T(128)} %copy-done.22, bf16[1456,384]{1,0:T(8,128)(2,1)} %copy-done.54, ...), custom_call_target="tpu_custom_call" | custom-call | flops 6000000000 | bytes 15000000 | tf_op jit(solution)/shard_map/pallas_call | solution.py:779
  285.8 15.3 %shard_map.299 = (bf16[416,768]{1,0:T(8,128)(2,1)}, bf16[2,4,288,128]{3,2,1,0:T(8,128)(2,1)}, bf16[2,4,288,128]{3,2,1,0:T(8,128)(2,1)}) custom-call(s32[16]{0:T(128)} %copy-done.7, s32[2]{0:T(128)} %copy-done.22, bf16[944,384]{1,0:T(8,128)(2,1)} %maximum_maximum_fusion.2.refs_0_, bf16[944,384]{1,0:T(8,128)(2,1)} %copy-done, bf16[944,384]{1,0:T(8,128)(2,1)} %copy-done.1, ...), custom_call_target="tpu_custom_call" | custom-call | flops 8999999488 | bytes 15000000 | tf_op jit(solution)/shard_map/pallas_call | solution.py:847
  302.6 2.0 bitcast_dynamic-update-slice_fusion.5
  307.9 3.1 collective-permute-done.39
  317.3 7.2 %collective-permute-done.42 = bf16[1088,128]{1,0:T(8,128)(2,1)S(1)} collective-permute-done((bf16[1088,128]{1,0:T(8,128)(2,1)}, bf16[1088,128]{1,0:T(8,128)(2,1)S(1)}, u32[]{:S(2)}, u32[]{:S(2)}) %collective-permute-start.42) | collective-permute-done | bytes 278560 | tf_op jit(solution)/shard_map/ppermute | solution.py:883
  324.5 5.2 %collective-permute-done.41 = bf16[1088,128]{1,0:T(8,128)(2,1)} collective-permute-done((bf16[1088,128]{1,0:T(8,128)(2,1)}, bf16[1088,128]{1,0:T(8,128)(2,1)}, u32[]{:S(2)}, u32[]{:S(2)}) %collective-permute-start.41) | collective-permute-done | bytes 278560 | tf_op jit(solution)/shard_map/ppermute | solution.py:883
  332.1 3.6 collective-permute-start.43
  343.0 2.0 collective-permute-start.47
  351.9 6.6 %collective-permute-done.49.one = bf16[704,128]{1,0:T(8,128)(2,1)S(1)} collective-permute-done((bf16[704,128]{1,0:T(8,128)(2,1)S(1)}, bf16[704,128]{1,0:T(8,128)(2,1)S(1)}, u32[]{:S(2)}, u32[]{:S(2)}) %collective-permute-start.49) | collective-permute-done | bytes 180256 | tf_op jit(solution)/shard_map/ppermute | solution.py:883
  361.8 3.1 collective-permute-done.51.three
  370.2 2.4 shard_map.301
  (327 shorter events, 103.3 us)
Async XLA Ops:
  6.1 25.7 %collective-permute-start = (bf16[944,384]{1,0:T(8,128)(2,1)}, bf16[944,384]{1,0:T(8,128)(2,1)S(1)}, u32[]{:S(2)}, u32[]{:S(2)}) collective-permute-start(bf16[944,384]{1,0:T(8,128)(2,1)} %maximum_maximum_fusion.2.refs_0_), channel_id=1, source_target_pairs={{0,1},{1,0},{2,3},{3,2},{4,5},{5,4},{6,7},{7,6},{8,9},{9,8},{10,11... | collective-permute-start | bytes 2174984 | tf_op jit(solution)/shard_map/ppermute | solution.py:883
  9.1 22.7 %collective-permute-start.1 = (bf16[944,384]{1,0:T(8,128)(2,1)}, bf16[944,384]{1,0:T(8,128)(2,1)S(1)}, u32[]{:S(2)}, u32[]{:S(2)}) collective-permute-start(bf16[944,384]{1,0:T(8,128)(2,1)} %maximum_maximum_fusion.2.refs_0_), channel_id=1, source_target_pairs={{0,2},{1,3},{2,0},{3,1},{4,6},{5,7},{6,4},{7,5},{8,10},{9,11},{10,... | collective-permute-start | bytes 2174984 | tf_op jit(solution)/shard_map/ppermute | solution.py:883
  32.1 11.4 %collective-permute-start.7 = (bf16[416,384]{1,0:T(8,128)(2,1)S(1)}, bf16[416,384]{1,0:T(8,128)(2,1)S(1)}, u32[]{:S(2)}, u32[]{:S(2)}) collective-permute-start(bf16[416,384]{1,0:T(8,128)(2,1)S(1)} %copy-done.18), channel_id=1, source_target_pairs={{0,3},{1,2},{2,1},{3,0},{4,7},{5,6},{6,5},{7,4},{8,11},{9,10},{10,... | collective-permute-start | bytes 958472 | tf_op jit(solution)/shard_map/ppermute | solution.py:883
  32.2 15.6 %collective-permute-start.8 = (bf16[416,384]{1,0:T(8,128)(2,1)S(1)}, bf16[416,384]{1,0:T(8,128)(2,1)S(1)}, u32[]{:S(2)}, u32[]{:S(2)}) collective-permute-start(bf16[416,384]{1,0:T(8,128)(2,1)S(1)} %copy-done.16), channel_id=1, source_target_pairs={{0,2},{1,3},{2,0},{3,1},{4,6},{5,7},{6,4},{7,5},{8,10},{9,11},{10,... | collective-permute-start | bytes 958472 | tf_op jit(solution)/shard_map/ppermute | solution.py:883
  34.1 15.3 %collective-permute-start.9 = (bf16[416,384]{1,0:T(8,128)(2,1)S(1)}, bf16[416,384]{1,0:T(8,128)(2,1)S(1)}, u32[]{:S(2)}, u32[]{:S(2)}) collective-permute-start(bf16[416,384]{1,0:T(8,128)(2,1)S(1)} %copy-done.14), channel_id=1, source_target_pairs={{0,1},{1,0},{2,3},{3,2},{4,5},{5,4},{6,7},{7,6},{8,9},{9,8},{10,11... | collective-permute-start | bytes 958472 | tf_op jit(solution)/shard_map/ppermute | solution.py:883
  37.7 17.9 %collective-permute-start.2 = (bf16[944,384]{1,0:T(8,128)(2,1)S(1)}, bf16[944,384]{1,0:T(8,128)(2,1)S(1)}, u32[]{:S(2)}, u32[]{:S(2)}) collective-permute-start(bf16[944,384]{1,0:T(8,128)(2,1)S(1)} %broadcast_select_fusion), channel_id=1, source_target_pairs={{0,2},{1,3},{2,0},{3,1},{4,5},{5,4},{6,7},{7,6},{8,10},{9,11},{10,... | collective-permute-start | bytes 2174984 | tf_op jit(solution)/shard_map/ppermute | solution.py:898
  38.2 20.6 %collective-permute-start.4 = (bf16[944,384]{1,0:T(8,128)(2,1)S(1)}, bf16[944,384]{1,0:T(8,128)(2,1)S(1)}, u32[]{:S(2)}, u32[]{:S(2)}) collective-permute-start(bf16[944,384]{1,0:T(8,128)(2,1)S(1)} %collective-permute-done.refs_1_), channel_id=1, source_target_pairs={{0,4},{4,0},{1,5},{5,1},{2,6},{6,2},{3,7},{7,3},{8,12},{12,8},{9,1... | collective-permute-start | bytes 2174984 | tf_op jit(solution)/shard_map/ppermute | solution.py:879
  43.5 16.6 %collective-permute-start.5 = (bf16[944,384]{1,0:T(8,128)(2,1)S(1)}, bf16[944,384]{1,0:T(8,128)(2,1)S(1)}, u32[]{:S(2)}, u32[]{:S(2)}) collective-permute-start(bf16[944,384]{1,0:T(8,128)(2,1)S(1)} %collective-permute-done.1.refs_2_), channel_id=1, source_target_pairs={{0,4},{4,0},{1,5},{5,1},{2,6},{6,2},{3,7},{7,3},{8,12},{12,8},{9,1... | collective-permute-start | bytes 2174984 | tf_op jit(solution)/shard_map/ppermute | solution.py:879
  57.3 21.7 %collective-permute-start.13 = (bf16[416,768]{1,0:T(8,128)(2,1)S(1)}, bf16[416,768]{1,0:T(8,128)(2,1)S(1)}, u32[]{:S(2)}, u32[]{:S(2)}) collective-permute-start(bf16[416,768]{1,0:T(8,128)(2,1)S(1)} %pad_maximum_fusion.1.refs_3_.refs_10_), channel_id=1, source_target_pairs={{0,4},{4,0},{1,5},{5,1},{2,6},{6,2},{3,7},{7,3},{8,12},{12,8},{9,1... | collective-permute-start | bytes 1916936 | tf_op jit(solution)/shard_map/ppermute | solution.py:879
  58.8 20.9 %collective-permute-start.15 = (bf16[416,768]{1,0:T(8,128)(2,1)S(1)}, bf16[416,768]{1,0:T(8,128)(2,1)S(1)}, u32[]{:S(2)}, u32[]{:S(2)}) collective-permute-start(bf16[416,768]{1,0:T(8,128)(2,1)S(1)} %pad_maximum_fusion.1.refs_3_.refs_10_), channel_id=1, source_target_pairs={{0,1},{1,0},{2,3},{3,2},{4,5},{5,4},{6,7},{7,6},{8,9},{9,8},{10,11... | collective-permute-start | bytes 1916936 | tf_op jit(solution)/shard_map/ppermute | solution.py:883
  60.1 19.5 %collective-permute-start.16 = (bf16[416,768]{1,0:T(8,128)(2,1)S(1)}, bf16[416,768]{1,0:T(8,128)(2,1)S(1)}, u32[]{:S(2)}, u32[]{:S(2)}) collective-permute-start(bf16[416,768]{1,0:T(8,128)(2,1)S(1)} %pad_maximum_fusion.1.refs_3_.refs_10_), channel_id=1, source_target_pairs={{0,2},{1,3},{2,0},{3,1},{4,6},{5,7},{6,4},{7,5},{8,10},{9,11},{10,... | collective-permute-start | bytes 1916936 | tf_op jit(solution)/shard_map/ppermute | solution.py:883
  77.2 16.8 %collective-permute-start.10 = (bf16[416,768]{1,0:T(8,128)(2,1)S(1)}, bf16[416,768]{1,0:T(8,128)(2,1)S(1)}, u32[]{:S(2)}, u32[]{:S(2)}) collective-permute-start(bf16[416,768]{1,0:T(8,128)(2,1)S(1)} %get-tuple-element.122.refs_1_.refs_6_), channel_id=1, source_target_pairs={{0,1},{1,0},{2,3},{3,2},{4,5},{5,4},{6,7},{7,6},{8,9},{9,8},{10,11... | collective-permute-start | bytes 1916936 | tf_op jit(solution)/shard_map/ppermute | solution.py:883
  78.9 16.5 %collective-permute-start.11 = (bf16[416,768]{1,0:T(8,128)(2,1)S(1)}, bf16[416,768]{1,0:T(8,128)(2,1)S(1)}, u32[]{:S(2)}, u32[]{:S(2)}) collective-permute-start(bf16[416,768]{1,0:T(8,128)(2,1)S(1)} %get-tuple-element.122.refs_1_.refs_6_), channel_id=1, source_target_pairs={{0,2},{1,3},{2,0},{3,1},{4,6},{5,7},{6,4},{7,5},{8,10},{9,11},{10,... | collective-permute-start | bytes 1916936 | tf_op jit(solution)/shard_map/ppermute | solution.py:883
  79.6 17.2 %collective-permute-start.20 = (bf16[416,768]{1,0:T(8,128)(2,1)S(1)}, bf16[416,768]{1,0:T(8,128)(2,1)S(1)}, u32[]{:S(2)}, u32[]{:S(2)}) collective-permute-start(bf16[416,768]{1,0:T(8,128)(2,1)S(1)} %collective-permute-done.15.refs_5_), channel_id=1, source_target_pairs={{0,4},{4,0},{1,5},{5,1},{2,6},{6,2},{3,7},{7,3},{8,12},{12,8},{9,1... | collective-permute-start | bytes 1916936 | tf_op jit(solution)/shard_map/ppermute | solution.py:879
  79.7 18.7 %collective-permute-start.21 = (bf16[416,768]{1,0:T(8,128)(2,1)S(1)}, bf16[416,768]{1,0:T(8,128)(2,1)S(1)}, u32[]{:S(2)}, u32[]{:S(2)}) collective-permute-start(bf16[416,768]{1,0:T(8,128)(2,1)S(1)} %collective-permute-done.16.refs_6_), channel_id=1, source_target_pairs={{0,4},{4,0},{1,5},{5,1},{2,6},{6,2},{3,7},{7,3},{8,12},{12,8},{9,1... | collective-permute-start | bytes 1916936 | tf_op jit(solution)/shard_map/ppermute | solution.py:879
  96.1 14.9 %collective-permute-start.17 = (bf16[416,768]{1,0:T(8,128)(2,1)S(1)}, bf16[416,768]{1,0:T(8,128)(2,1)S(1)}, u32[]{:S(2)}, u32[]{:S(2)}) collective-permute-start(bf16[416,768]{1,0:T(8,128)(2,1)S(1)} %broadcast_select_fusion.1), channel_id=1, source_target_pairs={{0,2},{1,3},{2,0},{3,1},{4,5},{5,4},{6,7},{7,6},{8,10},{9,11},{10,... | collective-permute-start | bytes 1916936 | tf_op jit(solution)/shard_map/ppermute | solution.py:898
  96.9 16.5 %collective-permute-start.14 = (bf16[416,768]{1,0:T(8,128)(2,1)S(1)}, bf16[416,768]{1,0:T(8,128)(2,1)S(1)}, u32[]{:S(2)}, u32[]{:S(2)}) collective-permute-start(bf16[416,768]{1,0:T(8,128)(2,1)S(1)} %broadcast_select_fusion.2), channel_id=1, source_target_pairs={{0,2},{1,3},{2,0},{3,1},{4,5},{5,4},{6,7},{7,6},{8,10},{9,11},{10,... | collective-permute-start | bytes 1916936 | tf_op jit(solution)/shard_map/ppermute | solution.py:898
  238.6 11.4 %collective-permute-start.30 = (bf16[832,768]{1,0:T(8,128)(2,1)}, bf16[832,768]{1,0:T(8,128)(2,1)}, u32[]{:S(2)}, u32[]{:S(2)}) collective-permute-start(bf16[832,768]{1,0:T(8,128)(2,1)} %get-tuple-element.150), channel_id=1, source_target_pairs={{0,4},{4,0},{1,5},{5,1},{2,6},{6,2},{3,7},{7,3},{8,12},{12,8},{9,1... | collective-permute-start | bytes 3833864 | tf_op jit(solution)/shard_map/ppermute | solution.py:879
  238.8 12.9 %collective-permute-start.31 = (bf16[832,768]{1,0:T(8,128)(2,1)}, bf16[832,768]{1,0:T(8,128)(2,1)}, u32[]{:S(2)}, u32[]{:S(2)}) collective-permute-start(bf16[832,768]{1,0:T(8,128)(2,1)} %get-tuple-element.152), channel_id=1, source_target_pairs={{0,4},{4,0},{1,5},{5,1},{2,6},{6,2},{3,7},{7,3},{8,12},{12,8},{9,1... | collective-permute-start | bytes 3833864 | tf_op jit(solution)/shard_map/ppermute | solution.py:879
  239.2 19.6 %collective-permute-start.26 = (bf16[832,896]{1,0:T(8,128)(2,1)S(1)}, bf16[832,896]{1,0:T(8,128)(2,1)}, u32[]{:S(2)}, u32[]{:S(2)}) collective-permute-start(bf16[832,896]{1,0:T(8,128)(2,1)S(1)} %add_convert_fusion), channel_id=1, source_target_pairs={{0,1},{1,0},{2,3},{3,2},{4,6},{5,7},{6,4},{7,5},{8,9},{9,8},{10,11... | collective-permute-start | bytes 4472840 | tf_op jit(solution)/shard_map/ppermute | solution.py:898
  261.4 11.7 %collective-permute-start.32 = (bf16[416,896]{1,0:T(8,128)(2,1)S(1)}, bf16[416,896]{1,0:T(8,128)(2,1)}, u32[]{:S(2)}, u32[]{:S(2)}) collective-permute-start(bf16[416,896]{1,0:T(8,128)(2,1)S(1)} %get-tuple-element.245), channel_id=1, source_target_pairs={{0,2},{1,3},{2,0},{3,1},{4,5},{5,4},{6,7},{7,6},{8,10},{9,11},{10,... | collective-permute-start | bytes 2236424 | tf_op jit(solution)/shard_map/ppermute | solution.py:898
  273.1 28.7 %collective-permute-start.36 = (bf16[416,768]{1,0:T(8,128)(2,1)S(1)}, bf16[416,768]{1,0:T(8,128)(2,1)S(1)}, u32[]{:S(2)}, u32[]{:S(2)}) collective-permute-start(bf16[416,768]{1,0:T(8,128)(2,1)S(1)} %get-tuple-element.168), channel_id=1, source_target_pairs={{0,2},{1,3},{2,0},{3,1},{4,5},{5,4},{6,7},{7,6},{8,10},{9,11},{10,... | collective-permute-start | bytes 1916936 | tf_op jit(solution)/shard_map/ppermute | solution.py:898
  273.8 28.0 %collective-permute-start.37 = (bf16[416,768]{1,0:T(8,128)(2,1)}, bf16[416,768]{1,0:T(8,128)(2,1)S(1)}, u32[]{:S(2)}, u32[]{:S(2)}) collective-permute-start(bf16[416,768]{1,0:T(8,128)(2,1)} %get-tuple-element.169), channel_id=1, source_target_pairs={{0,1},{1,0},{2,3},{3,2},{4,6},{5,7},{6,4},{7,5},{8,9},{9,8},{10,11... | collective-permute-start | bytes 1916936 | tf_op jit(solution)/shard_map/ppermute | solution.py:898
  275.1 26.6 %collective-permute-start.38 = (bf16[416,768]{1,0:T(8,128)(2,1)}, bf16[416,768]{1,0:T(8,128)(2,1)S(1)}, u32[]{:S(2)}, u32[]{:S(2)}) collective-permute-start(bf16[416,768]{1,0:T(8,128)(2,1)} %get-tuple-element.170), channel_id=1, source_target_pairs={{0,3},{1,2},{2,1},{3,0},{4,7},{5,6},{6,5},{7,4},{8,11},{9,10},{10,... | collective-permute-start | bytes 1916936 | tf_op jit(solution)/shard_map/ppermute | solution.py:898
  313.8 10.7 %collective-permute-start.42 = (bf16[1088,128]{1,0:T(8,128)(2,1)}, bf16[1088,128]{1,0:T(8,128)(2,1)S(1)}, u32[]{:S(2)}, u32[]{:S(2)}) collective-permute-start(bf16[1088,128]{1,0:T(8,128)(2,1)} %get-tuple-element.263), channel_id=1, source_target_pairs={{0,3},{1,2},{2,1},{3,0},{4,7},{5,6},{6,5},{7,4},{8,11},{9,10},{10,... | collective-permute-start | bytes 835592 | tf_op jit(solution)/shard_map/ppermute | solution.py:883
  315.6 14.1 %collective-permute-start.41 = (bf16[1088,128]{1,0:T(8,128)(2,1)}, bf16[1088,128]{1,0:T(8,128)(2,1)}, u32[]{:S(2)}, u32[]{:S(2)}) collective-permute-start(bf16[1088,128]{1,0:T(8,128)(2,1)} %get-tuple-element.264), channel_id=1, source_target_pairs={{0,2},{1,3},{2,0},{3,1},{4,6},{5,7},{6,4},{7,5},{8,10},{9,11},{10,... | collective-permute-start | bytes 835592 | tf_op jit(solution)/shard_map/ppermute | solution.py:883
  317.0 13.0 %collective-permute-start.40 = (bf16[1088,128]{1,0:T(8,128)(2,1)}, bf16[1088,128]{1,0:T(8,128)(2,1)}, u32[]{:S(2)}, u32[]{:S(2)}) collective-permute-start(bf16[1088,128]{1,0:T(8,128)(2,1)} %get-tuple-element.262), channel_id=1, source_target_pairs={{0,1},{1,0},{2,3},{3,2},{4,5},{5,4},{6,7},{7,6},{8,9},{9,8},{10,11... | collective-permute-start | bytes 835592 | tf_op jit(solution)/shard_map/ppermute | solution.py:883
  331.3 10.2 %collective-permute-start.45 = (bf16[272,128]{1,0:T(8,128)(2,1)S(1)}, bf16[272,128]{1,0:T(8,128)(2,1)S(1)}, u32[]{:S(2)}, u32[]{:S(2)}) collective-permute-start(bf16[272,128]{1,0:T(8,128)(2,1)S(1)} %get-tuple-element.292), channel_id=1, source_target_pairs={{0,24},{8,16},{16,8},{24,0},{1,25},{9,17},{17,9},{25,1},{2,26},{10... | collective-permute-start | bytes 208904 | tf_op jit(solution)/shard_map/ppermute | solution.py:933
  339.3 25.7 %collective-permute-start.53 = (bf16[416,384]{1,0:T(8,128)(2,1)S(1)}, bf16[416,384]{1,0:T(8,128)(2,1)S(1)}, u32[]{:S(2)}, u32[]{:S(2)}) collective-permute-start(bf16[416,384]{1,0:T(8,128)(2,1)S(1)} %get-tuple-element.257), channel_id=1, source_target_pairs={{0,1},{1,0},{2,3},{3,2},{4,5},{5,4},{6,7},{7,6},{8,9},{9,8},{10,11... | collective-permute-start | bytes 958472 | tf_op jit(solution)/shard_map/ppermute | solution.py:883
  340.8 24.2 %collective-permute-start.54 = (bf16[416,384]{1,0:T(8,128)(2,1)S(1)}, bf16[416,384]{1,0:T(8,128)(2,1)S(1)}, u32[]{:S(2)}, u32[]{:S(2)}) collective-permute-start(bf16[416,384]{1,0:T(8,128)(2,1)S(1)} %get-tuple-element.256), channel_id=1, source_target_pairs={{0,2},{1,3},{2,0},{3,1},{4,6},{5,7},{6,4},{7,5},{8,10},{9,11},{10,... | collective-permute-start | bytes 958472 | tf_op jit(solution)/shard_map/ppermute | solution.py:883
  346.9 18.1 %collective-permute-start.55 = (bf16[416,384]{1,0:T(8,128)(2,1)S(1)}, bf16[416,384]{1,0:T(8,128)(2,1)S(1)}, u32[]{:S(2)}, u32[]{:S(2)}) collective-permute-start(bf16[416,384]{1,0:T(8,128)(2,1)S(1)} %get-tuple-element.254), channel_id=1, source_target_pairs={{0,3},{1,2},{2,1},{3,0},{4,7},{5,6},{6,5},{7,4},{8,11},{9,10},{10,... | collective-permute-start | bytes 958472 | tf_op jit(solution)/shard_map/ppermute | solution.py:883
  351.5 10.3 %collective-permute-start.50 = (bf16[704,128]{1,0:T(8,128)(2,1)S(1)}, bf16[704,128]{1,0:T(8,128)(2,1)S(1)}, u32[]{:S(2)}, u32[]{:S(2)}) collective-permute-start(bf16[704,128]{1,0:T(8,128)(2,1)S(1)} %pad_maximum_fusion.13), channel_id=1, source_target_pairs={{0,2},{1,3},{2,0},{3,1},{4,6},{5,7},{6,4},{7,5},{8,10},{9,11},{10,... | collective-permute-start | bytes 540680 | tf_op jit(solution)/shard_map/ppermute | solution.py:883
  (83 other events, 632.2 us)

commit v6 on v5

--- a/solution.py
+++ b/solution.py
@@ -984,7 +984,7 @@
     )
     pairs = split_call(place, tokens, cotangent)
     from_x, from_y = across_col(packed, 1), across_col(packed, 2)
-    chosen, *pairs = lax.optimization_barrier((jnp.where(row == 0, from_x, from_y), *pairs))
+    chosen, routes, *pairs = lax.optimization_barrier((jnp.where(row == 0, from_x, from_y), routes, *pairs))
     near = [packed, from_x, from_y, across_chip(chosen, 2, 1)]
     pairs = by_place([pairs[0]] + [across_col(pairs[s], s) for s in range(1, 4)], col)
     x = jnp.concatenate([pair[:, :width] for pair in pairs], axis=1)

time: 378 us -> 381 us (level)
  starting transfers between devices: 45.6 us -> 67.6 us
  waiting for transfers between devices: 82.2 us -> 61.3 us
  Pallas kernels: 172 us -> 162 us
  other arithmetic: 40.1 us -> 46.4 us
  local copies, waits for them, and re-layouts: 32.2 us -> 36.4 us
    ppermute x12, starting transfers between devices: 12.8 us -> 31 us  [across_dp(): return lax.ppermute(value, 'dp', [(i, i ^ step) for i in range(4)])]
    ppermute x8, waiting for transfers between devices: 16.7 us -> 2.99 us  [across_chip(): return lax.ppermute(value, ('row', 'col'), pairs)]
    pallas_call x1, Pallas kernels: 108 us -> 98.8 us  [moe_call(): pl.pallas_call(lambda *refs: moe_kernel(places, *refs), grid_spec=pltpu.P...]
    unnamed x137 -> x145, local copies, waits for them, and re-layouts: 27.4 us -> 29.6 us
  transfers between devices with their start and end apart: 56 -> 56, of which waited for: 28 -> 25; matrix products, arithmetic and copies ran while one was open for 10% -> 12% of each run, Pallas kernels for 15% -> 15%
where the time goes in v6:
time: 381 us; the launch traced here: 376 us
  Pallas kernels  162 us (43%)
  starting transfers between devices  67.6 us (18%)
  waiting for transfers between devices  61.3 us (16%)
  other arithmetic  46.4 us (12%)
  local copies, waits for them, and re-layouts  36.4 us (10%)
    pallas_call x1, Pallas kernels, moe_call(): pl.pallas_call(lambda *refs: moe_kernel(places, *refs), grid_spec=pltpu.P...  98.8 us
    ppermute x18, waiting for transfers between devices, across_col(): return lax.ppermute(value, 'col', [(i, i ^ step) for i in range(4)])  39.9 us
    ppermute x12, starting transfers between devices, across_dp(): return lax.ppermute(value, 'dp', [(i, i ^ step) for i in range(4)])  31 us
    unnamed x145, local copies, waits for them, and re-layouts  29.6 us
    ppermute x18, starting transfers between devices, across_col(): return lax.ppermute(value, 'col', [(i, i ^ step) for i in range(4)])  22.9 us
    pallas_call x3, Pallas kernels, table_call(): pl.pallas_call(lambda *refs: table_kernel(n, *refs), grid_spec=pltpu.Pref...  20.1 us
    pallas_call x1, Pallas kernels, qkv_back_call(): pl.pallas_call(qkv_back_kernel, grid_spec=pltpu.PrefetchScalarGridSpec(nu...  15.3 us
    pallas_call x1, Pallas kernels, attend_call(): pl.pallas_call(attend_kernel, grid_spec=pltpu.PrefetchScalarGridSpec(num_...  13.2 us
  transfers between devices with their start and end apart: 56, of which 25 were waited for; matrix products, arithmetic and copies ran while one was open for 12% of the time, Pallas kernels for 15%

profile of v6, /device:TPU:0, one launch (start us, length us, event | category | flops | bytes accessed | tf_op | source)
XLA Modules:
  0.0 376.0 jit_solution(3235955474595656047)
XLA Ops:
  6.2 2.9 collective-permute-start
  22.1 3.4 collective-permute-done.refs_1_
  38.4 8.8 %sort.14 = (s32[14592]{0:T(1024)}, s32[14592]{0:T(1024)}) sort(s32[14592]{0:T(1024)} %pad_add_fusion, s32[14592]{0:T(1024)} %iota.71), dimensions={0}, to_apply=%region_1.2 | sort | flops 204288 | bytes 233472 | tf_op jit(solution)/shard_map/sort | solution.py:355
  50.3 4.6 %collective-permute-done.8 = bf16[416,384]{1,0:T(8,128)(2,1)S(1)} collective-permute-done((bf16[416,384]{1,0:T(8,128)(2,1)S(1)}, bf16[416,384]{1,0:T(8,128)(2,1)S(1)}, u32[]{:S(2)}, u32[]{:S(2)}) %collective-permute-start.8) | collective-permute-done | bytes 319520 | tf_op jit(solution)/shard_map/ppermute | solution.py:883
  67.9 13.2 %shard_map.293 = (bf16[416,768]{1,0:T(8,128)(2,1)S(1)}, f32[416,768]{1,0:T(8,128)}, bf16[416,768]{1,0:T(8,128)(2,1)S(1)}, bf16[3,416,768]{2,1,0:T(8,128)(2,1)}, ...) custom-call(s32[16]{0:T(128)S(1)} %and_select_fusion.5.picks_ref, ...), custom_call_target="tpu_custom_call" | custom-call | flops 4000000000 | bytes 15000000 | tf_op jit(solution)/shard_map/pallas_call | solution.py:684
  85.6 5.1 %shard_map.294.refs_4_ = bf16[832,16,128]{2,1,0:T(8,128)(2,1)S(1)} custom-call(s32[4]{0:T(128)S(1)} %pad_add_fusion.3.refs_0_, bf16[416,768]{1,0:T(8,128)(2,1)S(1)} %get-tuple-element.124.refs_1_.refs_6_, bf16[416,768]{1,0:T(8,128)(2,1)S(1)} %collective-permute-done.12.refs_2_, bf16[416,768]{1,0:T(8,128)(2,1)S(1)} %pad_maximum_fusion.1.refs_3_.refs_10_, ...), custom_call_target="tpu_custom_call" | custom-call | flops 6000000000 | bytes 6000000 | tf_op jit(solution)/shard_map/pallas_call | solution.py:100
  92.5 6.4 %collective-permute-done.10.refs_1_ = bf16[416,768]{1,0:T(8,128)(2,1)S(1)} collective-permute-done((bf16[416,768]{1,0:T(8,128)(2,1)S(1)}, bf16[416,768]{1,0:T(8,128)(2,1)S(1)}, u32[]{:S(2)}, u32[]{:S(2)}) %collective-permute-start.10) | collective-permute-done | bytes 639008 | tf_op jit(solution)/shard_map/ppermute | solution.py:883
  103.0 9.8 %shard_map.295.refs_5_ = bf16[1664,16,128]{2,1,0:T(8,128)(2,1)S(1)} custom-call(s32[8]{0:T(128)S(1)} %pad_add_fusion.4.refs_0_, bf16[416,768]{1,0:T(8,128)(2,1)S(1)} %collective-permute-done.10.refs_1_, bf16[416,768]{1,0:T(8,128)(2,1)S(1)} %collective-permute-done.11.refs_2_, bf16[416,768]{1,0:T(8,128)(2,1)S(1)} %collective-permute-done.18.refs_3_, ...), custom_call_target="tpu_custom_call" | custom-call | flops 12000000000 | bytes 12000000 | tf_op jit(solution)/shard_map/pallas_call | solution.py:100
  112.7 2.8 copy-done.29
  115.6 2.4 collective-permute-done.14.refs_1_
  121.0 5.2 %shard_map.296.refs_6_ = bf16[832,16,128]{2,1,0:T(8,128)(2,1)S(1)} custom-call(s32[4]{0:T(128)S(1)} %pad_add_fusion.5.refs_0_, bf16[416,768]{1,0:T(8,128)(2,1)S(1)} %collective-permute-done.14.refs_1_, bf16[416,768]{1,0:T(8,128)(2,1)S(1)} %collective-permute-done.22.refs_2_, bf16[416,768]{1,0:T(8,128)(2,1)S(1)} %collective-permute-done.17.refs_3_, ...), custom_call_target="tpu_custom_call" | custom-call | flops 6000000000 | bytes 6000000 | tf_op jit(solution)/shard_map/pallas_call | solution.py:100
  127.8 98.8 %shard_map.297 = (bf16[832,768]{1,0:T(8,128)(2,1)}, bf16[832,768]{1,0:T(8,128)(2,1)}, bf16[832,768]{1,0:T(8,128)(2,1)}, bf16[832,768]{1,0:T(8,128)(2,1)}, bf16[8...) custom-call(s32[14592]{0:T(1024)} %broadcast_and_fusion.refs_0_, ...), custom_call_target="tpu_custom_call" | custom-call | flops 20000000000 | bytes 60000000 | tf_op jit(solution)/shard_map/pallas_call | solution.py:289
  228.2 3.4 collective-permute-done.25
  234.3 9.6 %collective-permute-start.29 = (bf16[192,128]{1,0:T(8,128)(2,1)S(1)}, bf16[192,128]{1,0:T(8,128)(2,1)S(1)}, u32[]{:S(2)}, u32[]{:S(2)}) collective-permute-start(bf16[192,128]{1,0:T(8,128)(2,1)S(1)} %get-tuple-element.323), channel_id=1, source_target_pairs={{0,24},{8,16},{16,8},{24,0},{1,25},{9,17},{17,9},{25,1},{2,26},{10... | collective-permute-start | bytes 147464 | tf_op jit(solution)/shard_map/ppermute | solution.py:933
  252.8 2.7 add_convert_fusion.6
  255.5 2.6 add_convert_fusion.3
  258.0 2.1 collective-permute-start.32
  260.2 6.8 %collective-permute-start.33 = (bf16[192,128]{1,0:T(8,128)(2,1)S(1)}, bf16[192,128]{1,0:T(8,128)(2,1)S(1)}, u32[]{:S(2)}, u32[]{:S(2)}) collective-permute-start(bf16[192,128]{1,0:T(8,128)(2,1)S(1)} %fusion.9), channel_id=1, source_target_pairs={{0,24},{8,16},{16,8},{24,0},{1,25},{9,17},{17,9},{25,1},{2,26},{10... | collective-permute-start | bytes 147464 | tf_op jit(solution)/shard_map/ppermute | solution.py:933
  269.1 3.2 collective-permute-done.34
  274.3 2.3 collective-permute-start.38
  276.6 9.3 %shard_map.298 = (f32[416,768]{1,0:T(8,128)}, bf16[416,768]{1,0:T(8,128)(2,1)}, f32[416,768]{1,0:T(8,128)}, bf16[2560,128]{1,0:T(8,128)(2,1)}, bf16[2,4,96,128]{...) custom-call(s32[16]{0:T(128)} %copy-done.8, s32[2]{0:T(128)} %copy-done.23, bf16[1456,384]{1,0:T(8,128)(2,1)} %copy-done.58, ...), custom_call_target="tpu_custom_call" | custom-call | flops 6000000000 | bytes 15000000 | tf_op jit(solution)/shard_map/pallas_call | solution.py:779
  285.8 15.3 %shard_map.299 = (bf16[416,768]{1,0:T(8,128)(2,1)}, bf16[2,4,288,128]{3,2,1,0:T(8,128)(2,1)}, bf16[2,4,288,128]{3,2,1,0:T(8,128)(2,1)}) custom-call(s32[16]{0:T(128)} %copy-done.8, s32[2]{0:T(128)} %copy-done.23, bf16[944,384]{1,0:T(8,128)(2,1)} %maximum_maximum_fusion.2.refs_0_, bf16[944,384]{1,0:T(8,128)(2,1)} %copy-done, bf16[944,384]{1,0:T(8,128)(2,1)} %copy-done.1, ...), custom_call_target="tpu_custom_call" | custom-call | flops 8999999488 | bytes 15000000 | tf_op jit(solution)/shard_map/pallas_call | solution.py:847
  302.6 2.0 bitcast_dynamic-update-slice_fusion.5
  307.9 3.1 collective-permute-done.39
  317.3 7.2 %collective-permute-done.42 = bf16[1088,128]{1,0:T(8,128)(2,1)S(1)} collective-permute-done((bf16[1088,128]{1,0:T(8,128)(2,1)}, bf16[1088,128]{1,0:T(8,128)(2,1)S(1)}, u32[]{:S(2)}, u32[]{:S(2)}) %collective-permute-start.42) | collective-permute-done | bytes 278560 | tf_op jit(solution)/shard_map/ppermute | solution.py:883
  324.4 5.2 %collective-permute-done.41 = bf16[1088,128]{1,0:T(8,128)(2,1)} collective-permute-done((bf16[1088,128]{1,0:T(8,128)(2,1)}, bf16[1088,128]{1,0:T(8,128)(2,1)}, u32[]{:S(2)}, u32[]{:S(2)}) %collective-permute-start.41) | collective-permute-done | bytes 278560 | tf_op jit(solution)/shard_map/ppermute | solution.py:883
  331.3 5.0 %collective-permute-start.45 = (bf16[272,128]{1,0:T(8,128)(2,1)S(1)}, bf16[272,128]{1,0:T(8,128)(2,1)S(1)}, u32[]{:S(2)}, u32[]{:S(2)}) collective-permute-start(bf16[272,128]{1,0:T(8,128)(2,1)S(1)} %get-tuple-element.294), channel_id=1, source_target_pairs={{0,24},{8,16},{16,8},{24,0},{1,25},{9,17},{17,9},{25,1},{2,26},{10... | collective-permute-start | bytes 208904 | tf_op jit(solution)/shard_map/ppermute | solution.py:933
  343.1 2.1 collective-permute-start.48
  349.2 2.2 collective-permute-done.46
  355.1 5.3 %collective-permute-done.49.one = bf16[704,128]{1,0:T(8,128)(2,1)S(1)} collective-permute-done((bf16[704,128]{1,0:T(8,128)(2,1)S(1)}, bf16[704,128]{1,0:T(8,128)(2,1)S(1)}, u32[]{:S(2)}, u32[]{:S(2)}) %collective-permute-start.49) | collective-permute-done | bytes 180256 | tf_op jit(solution)/shard_map/ppermute | solution.py:883
  361.7 5.1 %collective-permute-done.51.three = bf16[704,128]{1,0:T(8,128)(2,1)S(1)} collective-permute-done((bf16[704,128]{1,0:T(8,128)(2,1)S(1)}, bf16[704,128]{1,0:T(8,128)(2,1)S(1)}, u32[]{:S(2)}, u32[]{:S(2)}) %collective-permute-start.51) | collective-permute-done | bytes 180256 | tf_op jit(solution)/shard_map/ppermute | solution.py:883
  372.0 2.4 shard_map.301
  (335 shorter events, 114.1 us)
Async XLA Ops:
  6.2 19.4 %collective-permute-start = (bf16[944,384]{1,0:T(8,128)(2,1)}, bf16[944,384]{1,0:T(8,128)(2,1)S(1)}, u32[]{:S(2)}, u32[]{:S(2)}) collective-permute-start(bf16[944,384]{1,0:T(8,128)(2,1)} %maximum_maximum_fusion.2.refs_0_), channel_id=1, source_target_pairs={{0,1},{1,0},{2,3},{3,2},{4,5},{5,4},{6,7},{7,6},{8,9},{9,8},{10,11... | collective-permute-start | bytes 2174984 | tf_op jit(solution)/shard_map/ppermute | solution.py:883
  9.1 17.9 %collective-permute-start.1 = (bf16[944,384]{1,0:T(8,128)(2,1)}, bf16[944,384]{1,0:T(8,128)(2,1)S(1)}, u32[]{:S(2)}, u32[]{:S(2)}) collective-permute-start(bf16[944,384]{1,0:T(8,128)(2,1)} %maximum_maximum_fusion.2.refs_0_), channel_id=1, source_target_pairs={{0,2},{1,3},{2,0},{3,1},{4,6},{5,7},{6,4},{7,5},{8,10},{9,11},{10,... | collective-permute-start | bytes 2174984 | tf_op jit(solution)/shard_map/ppermute | solution.py:883
  29.7 28.3 %collective-permute-start.2 = (bf16[944,384]{1,0:T(8,128)(2,1)}, bf16[944,384]{1,0:T(8,128)(2,1)}, u32[]{:S(2)}, u32[]{:S(2)}) collective-permute-start(bf16[944,384]{1,0:T(8,128)(2,1)} %broadcast_select_fusion), channel_id=1, source_target_pairs={{0,2},{1,3},{2,0},{3,1},{4,5},{5,4},{6,7},{7,6},{8,10},{9,11},{10,... | collective-permute-start | bytes 2174984 | tf_op jit(solution)/shard_map/ppermute | solution.py:898
  31.3 18.5 %collective-permute-start.7 = (bf16[416,384]{1,0:T(8,128)(2,1)S(1)}, bf16[416,384]{1,0:T(8,128)(2,1)S(1)}, u32[]{:S(2)}, u32[]{:S(2)}) collective-permute-start(bf16[416,384]{1,0:T(8,128)(2,1)S(1)} %copy-done.19), channel_id=1, source_target_pairs={{0,3},{1,2},{2,1},{3,0},{4,7},{5,6},{6,5},{7,4},{8,11},{9,10},{10,... | collective-permute-start | bytes 958472 | tf_op jit(solution)/shard_map/ppermute | solution.py:883
  31.6 23.3 %collective-permute-start.8 = (bf16[416,384]{1,0:T(8,128)(2,1)S(1)}, bf16[416,384]{1,0:T(8,128)(2,1)S(1)}, u32[]{:S(2)}, u32[]{:S(2)}) collective-permute-start(bf16[416,384]{1,0:T(8,128)(2,1)S(1)} %copy-done.17), channel_id=1, source_target_pairs={{0,2},{1,3},{2,0},{3,1},{4,6},{5,7},{6,4},{7,5},{8,10},{9,11},{10,... | collective-permute-start | bytes 958472 | tf_op jit(solution)/shard_map/ppermute | solution.py:883
  33.3 22.3 %collective-permute-start.9 = (bf16[416,384]{1,0:T(8,128)(2,1)S(1)}, bf16[416,384]{1,0:T(8,128)(2,1)}, u32[]{:S(2)}, u32[]{:S(2)}) collective-permute-start(bf16[416,384]{1,0:T(8,128)(2,1)S(1)} %copy-done.15), channel_id=1, source_target_pairs={{0,1},{1,0},{2,3},{3,2},{4,5},{5,4},{6,7},{7,6},{8,9},{9,8},{10,11... | collective-permute-start | bytes 958472 | tf_op jit(solution)/shard_map/ppermute | solution.py:883
  48.4 15.9 %collective-permute-start.4 = (bf16[944,384]{1,0:T(8,128)(2,1)S(1)}, bf16[944,384]{1,0:T(8,128)(2,1)S(1)}, u32[]{:S(2)}, u32[]{:S(2)}) collective-permute-start(bf16[944,384]{1,0:T(8,128)(2,1)S(1)} %collective-permute-done.refs_1_), channel_id=1, source_target_pairs={{0,4},{4,0},{1,5},{5,1},{2,6},{6,2},{3,7},{7,3},{8,12},{12,8},{9,1... | collective-permute-start | bytes 2174984 | tf_op jit(solution)/shard_map/ppermute | solution.py:879
  49.8 14.9 %collective-permute-start.5 = (bf16[944,384]{1,0:T(8,128)(2,1)S(1)}, bf16[944,384]{1,0:T(8,128)(2,1)S(1)}, u32[]{:S(2)}, u32[]{:S(2)}) collective-permute-start(bf16[944,384]{1,0:T(8,128)(2,1)S(1)} %collective-permute-done.1.refs_2_), channel_id=1, source_target_pairs={{0,4},{4,0},{1,5},{5,1},{2,6},{6,2},{3,7},{7,3},{8,12},{12,8},{9,1... | collective-permute-start | bytes 2174984 | tf_op jit(solution)/shard_map/ppermute | solution.py:879
  62.7 20.7 %collective-permute-start.13 = (bf16[416,768]{1,0:T(8,128)(2,1)S(1)}, bf16[416,768]{1,0:T(8,128)(2,1)S(1)}, u32[]{:S(2)}, u32[]{:S(2)}) collective-permute-start(bf16[416,768]{1,0:T(8,128)(2,1)S(1)} %pad_maximum_fusion.1.refs_3_.refs_10_), channel_id=1, source_target_pairs={{0,4},{4,0},{1,5},{5,1},{2,6},{6,2},{3,7},{7,3},{8,12},{12,8},{9,1... | collective-permute-start | bytes 1916936 | tf_op jit(solution)/shard_map/ppermute | solution.py:879
  64.2 20.8 %collective-permute-start.15 = (bf16[416,768]{1,0:T(8,128)(2,1)S(1)}, bf16[416,768]{1,0:T(8,128)(2,1)S(1)}, u32[]{:S(2)}, u32[]{:S(2)}) collective-permute-start(bf16[416,768]{1,0:T(8,128)(2,1)S(1)} %pad_maximum_fusion.1.refs_3_.refs_10_), channel_id=1, source_target_pairs={{0,1},{1,0},{2,3},{3,2},{4,5},{5,4},{6,7},{7,6},{8,9},{9,8},{10,11... | collective-permute-start | bytes 1916936 | tf_op jit(solution)/shard_map/ppermute | solution.py:883
  64.7 20.3 %collective-permute-start.16 = (bf16[416,768]{1,0:T(8,128)(2,1)S(1)}, bf16[416,768]{1,0:T(8,128)(2,1)S(1)}, u32[]{:S(2)}, u32[]{:S(2)}) collective-permute-start(bf16[416,768]{1,0:T(8,128)(2,1)S(1)} %pad_maximum_fusion.1.refs_3_.refs_10_), channel_id=1, source_target_pairs={{0,2},{1,3},{2,0},{3,1},{4,6},{5,7},{6,4},{7,5},{8,10},{9,11},{10,... | collective-permute-start | bytes 1916936 | tf_op jit(solution)/shard_map/ppermute | solution.py:883
  82.1 16.8 %collective-permute-start.10 = (bf16[416,768]{1,0:T(8,128)(2,1)S(1)}, bf16[416,768]{1,0:T(8,128)(2,1)S(1)}, u32[]{:S(2)}, u32[]{:S(2)}) collective-permute-start(bf16[416,768]{1,0:T(8,128)(2,1)S(1)} %get-tuple-element.124.refs_1_.refs_6_), channel_id=1, source_target_pairs={{0,1},{1,0},{2,3},{3,2},{4,5},{5,4},{6,7},{7,6},{8,9},{9,8},{10,11... | collective-permute-start | bytes 1916936 | tf_op jit(solution)/shard_map/ppermute | solution.py:883
  83.5 16.5 %collective-permute-start.11 = (bf16[416,768]{1,0:T(8,128)(2,1)S(1)}, bf16[416,768]{1,0:T(8,128)(2,1)S(1)}, u32[]{:S(2)}, u32[]{:S(2)}) collective-permute-start(bf16[416,768]{1,0:T(8,128)(2,1)S(1)} %get-tuple-element.124.refs_1_.refs_6_), channel_id=1, source_target_pairs={{0,2},{1,3},{2,0},{3,1},{4,6},{5,7},{6,4},{7,5},{8,10},{9,11},{10,... | collective-permute-start | bytes 1916936 | tf_op jit(solution)/shard_map/ppermute | solution.py:883
  85.1 17.2 %collective-permute-start.20 = (bf16[416,768]{1,0:T(8,128)(2,1)S(1)}, bf16[416,768]{1,0:T(8,128)(2,1)S(1)}, u32[]{:S(2)}, u32[]{:S(2)}) collective-permute-start(bf16[416,768]{1,0:T(8,128)(2,1)S(1)} %collective-permute-done.15.refs_5_), channel_id=1, source_target_pairs={{0,4},{4,0},{1,5},{5,1},{2,6},{6,2},{3,7},{7,3},{8,12},{12,8},{9,1... | collective-permute-start | bytes 1916936 | tf_op jit(solution)/shard_map/ppermute | solution.py:879
  85.1 17.8 %collective-permute-start.21 = (bf16[416,768]{1,0:T(8,128)(2,1)S(1)}, bf16[416,768]{1,0:T(8,128)(2,1)S(1)}, u32[]{:S(2)}, u32[]{:S(2)}) collective-permute-start(bf16[416,768]{1,0:T(8,128)(2,1)S(1)} %collective-permute-done.16.refs_6_), channel_id=1, source_target_pairs={{0,4},{4,0},{1,5},{5,1},{2,6},{6,2},{3,7},{7,3},{8,12},{12,8},{9,1... | collective-permute-start | bytes 1916936 | tf_op jit(solution)/shard_map/ppermute | solution.py:879
  100.6 14.9 %collective-permute-start.17 = (bf16[416,768]{1,0:T(8,128)(2,1)S(1)}, bf16[416,768]{1,0:T(8,128)(2,1)S(1)}, u32[]{:S(2)}, u32[]{:S(2)}) collective-permute-start(bf16[416,768]{1,0:T(8,128)(2,1)S(1)} %broadcast_select_fusion.1), channel_id=1, source_target_pairs={{0,2},{1,3},{2,0},{3,1},{4,5},{5,4},{6,7},{7,6},{8,10},{9,11},{10,... | collective-permute-start | bytes 1916936 | tf_op jit(solution)/shard_map/ppermute | solution.py:898
  102.3 15.6 %collective-permute-start.14 = (bf16[416,768]{1,0:T(8,128)(2,1)S(1)}, bf16[416,768]{1,0:T(8,128)(2,1)S(1)}, u32[]{:S(2)}, u32[]{:S(2)}) collective-permute-start(bf16[416,768]{1,0:T(8,128)(2,1)S(1)} %broadcast_select_fusion.2), channel_id=1, source_target_pairs={{0,2},{1,3},{2,0},{3,1},{4,5},{5,4},{6,7},{7,6},{8,10},{9,11},{10,... | collective-permute-start | bytes 1916936 | tf_op jit(solution)/shard_map/ppermute | solution.py:898
  226.8 17.1 %collective-permute-start.24 = (bf16[832,896]{1,0:T(8,128)(2,1)}, bf16[832,896]{1,0:T(8,128)(2,1)}, u32[]{:S(2)}, u32[]{:S(2)}) collective-permute-start(bf16[832,896]{1,0:T(8,128)(2,1)} %get-tuple-element.140), channel_id=1, source_target_pairs={{0,4},{4,0},{1,5},{5,1},{2,6},{6,2},{3,7},{7,3},{8,12},{12,8},{9,1... | collective-permute-start | bytes 4472840 | tf_op jit(solution)/shard_map/ppermute | solution.py:879
  233.4 17.6 %collective-permute-start.30 = (bf16[832,768]{1,0:T(8,128)(2,1)}, bf16[832,768]{1,0:T(8,128)(2,1)}, u32[]{:S(2)}, u32[]{:S(2)}) collective-permute-start(bf16[832,768]{1,0:T(8,128)(2,1)} %get-tuple-element.152), channel_id=1, source_target_pairs={{0,4},{4,0},{1,5},{5,1},{2,6},{6,2},{3,7},{7,3},{8,12},{12,8},{9,1... | collective-permute-start | bytes 3833864 | tf_op jit(solution)/shard_map/ppermute | solution.py:879
  233.6 19.2 %collective-permute-start.31 = (bf16[832,768]{1,0:T(8,128)(2,1)}, bf16[832,768]{1,0:T(8,128)(2,1)}, u32[]{:S(2)}, u32[]{:S(2)}) collective-permute-start(bf16[832,768]{1,0:T(8,128)(2,1)} %get-tuple-element.154), channel_id=1, source_target_pairs={{0,4},{4,0},{1,5},{5,1},{2,6},{6,2},{3,7},{7,3},{8,12},{12,8},{9,1... | collective-permute-start | bytes 3833864 | tf_op jit(solution)/shard_map/ppermute | solution.py:879
  234.0 21.5 %collective-permute-start.26 = (bf16[832,896]{1,0:T(8,128)(2,1)S(1)}, bf16[832,896]{1,0:T(8,128)(2,1)}, u32[]{:S(2)}, u32[]{:S(2)}) collective-permute-start(bf16[832,896]{1,0:T(8,128)(2,1)S(1)} %add_convert_fusion), channel_id=1, source_target_pairs={{0,1},{1,0},{2,3},{3,2},{4,6},{5,7},{6,4},{7,5},{8,9},{9,8},{10,11... | collective-permute-start | bytes 4472840 | tf_op jit(solution)/shard_map/ppermute | solution.py:898
  234.3 12.1 %collective-permute-start.29 = (bf16[192,128]{1,0:T(8,128)(2,1)S(1)}, bf16[192,128]{1,0:T(8,128)(2,1)S(1)}, u32[]{:S(2)}, u32[]{:S(2)}) collective-permute-start(bf16[192,128]{1,0:T(8,128)(2,1)S(1)} %get-tuple-element.323), channel_id=1, source_target_pairs={{0,24},{8,16},{16,8},{24,0},{1,25},{9,17},{17,9},{25,1},{2,26},{10... | collective-permute-start | bytes 147464 | tf_op jit(solution)/shard_map/ppermute | solution.py:933
  258.0 15.0 %collective-permute-start.32 = (bf16[416,896]{1,0:T(8,128)(2,1)S(1)}, bf16[416,896]{1,0:T(8,128)(2,1)}, u32[]{:S(2)}, u32[]{:S(2)}) collective-permute-start(bf16[416,896]{1,0:T(8,128)(2,1)S(1)} %get-tuple-element.247), channel_id=1, source_target_pairs={{0,2},{1,3},{2,0},{3,1},{4,5},{5,4},{6,7},{7,6},{8,10},{9,11},{10,... | collective-permute-start | bytes 2236424 | tf_op jit(solution)/shard_map/ppermute | solution.py:898
  273.0 28.7 %collective-permute-start.36 = (bf16[416,768]{1,0:T(8,128)(2,1)S(1)}, bf16[416,768]{1,0:T(8,128)(2,1)S(1)}, u32[]{:S(2)}, u32[]{:S(2)}) collective-permute-start(bf16[416,768]{1,0:T(8,128)(2,1)S(1)} %get-tuple-element.170), channel_id=1, source_target_pairs={{0,2},{1,3},{2,0},{3,1},{4,5},{5,4},{6,7},{7,6},{8,10},{9,11},{10,... | collective-permute-start | bytes 1916936 | tf_op jit(solution)/shard_map/ppermute | solution.py:898
  273.2 28.6 %collective-permute-start.37 = (bf16[416,768]{1,0:T(8,128)(2,1)}, bf16[416,768]{1,0:T(8,128)(2,1)S(1)}, u32[]{:S(2)}, u32[]{:S(2)}) collective-permute-start(bf16[416,768]{1,0:T(8,128)(2,1)} %get-tuple-element.171), channel_id=1, source_target_pairs={{0,1},{1,0},{2,3},{3,2},{4,6},{5,7},{6,4},{7,5},{8,9},{9,8},{10,11... | collective-permute-start | bytes 1916936 | tf_op jit(solution)/shard_map/ppermute | solution.py:898
  274.3 27.5 %collective-permute-start.38 = (bf16[416,768]{1,0:T(8,128)(2,1)}, bf16[416,768]{1,0:T(8,128)(2,1)S(1)}, u32[]{:S(2)}, u32[]{:S(2)}) collective-permute-start(bf16[416,768]{1,0:T(8,128)(2,1)} %get-tuple-element.172), channel_id=1, source_target_pairs={{0,3},{1,2},{2,1},{3,0},{4,7},{5,6},{6,5},{7,4},{8,11},{9,10},{10,... | collective-permute-start | bytes 1916936 | tf_op jit(solution)/shard_map/ppermute | solution.py:898
  315.3 14.3 %collective-permute-start.41 = (bf16[1088,128]{1,0:T(8,128)(2,1)}, bf16[1088,128]{1,0:T(8,128)(2,1)}, u32[]{:S(2)}, u32[]{:S(2)}) collective-permute-start(bf16[1088,128]{1,0:T(8,128)(2,1)} %get-tuple-element.266), channel_id=1, source_target_pairs={{0,2},{1,3},{2,0},{3,1},{4,6},{5,7},{6,4},{7,5},{8,10},{9,11},{10,... | collective-permute-start | bytes 835592 | tf_op jit(solution)/shard_map/ppermute | solution.py:883
  315.9 14.2 %collective-permute-start.40 = (bf16[1088,128]{1,0:T(8,128)(2,1)}, bf16[1088,128]{1,0:T(8,128)(2,1)}, u32[]{:S(2)}, u32[]{:S(2)}) collective-permute-start(bf16[1088,128]{1,0:T(8,128)(2,1)} %get-tuple-element.264), channel_id=1, source_target_pairs={{0,1},{1,0},{2,3},{3,2},{4,5},{5,4},{6,7},{7,6},{8,9},{9,8},{10,11... | collective-permute-start | bytes 835592 | tf_op jit(solution)/shard_map/ppermute | solution.py:883
  331.3 11.7 %collective-permute-start.45 = (bf16[272,128]{1,0:T(8,128)(2,1)S(1)}, bf16[272,128]{1,0:T(8,128)(2,1)S(1)}, u32[]{:S(2)}, u32[]{:S(2)}) collective-permute-start(bf16[272,128]{1,0:T(8,128)(2,1)S(1)} %get-tuple-element.294), channel_id=1, source_target_pairs={{0,24},{8,16},{16,8},{24,0},{1,25},{9,17},{17,9},{25,1},{2,26},{10... | collective-permute-start | bytes 208904 | tf_op jit(solution)/shard_map/ppermute | solution.py:933
  340.6 26.2 %collective-permute-start.53 = (bf16[416,384]{1,0:T(8,128)(2,1)S(1)}, bf16[416,384]{1,0:T(8,128)(2,1)S(1)}, u32[]{:S(2)}, u32[]{:S(2)}) collective-permute-start(bf16[416,384]{1,0:T(8,128)(2,1)S(1)} %get-tuple-element.259), channel_id=1, source_target_pairs={{0,1},{1,0},{2,3},{3,2},{4,5},{5,4},{6,7},{7,6},{8,9},{9,8},{10,11... | collective-permute-start | bytes 958472 | tf_op jit(solution)/shard_map/ppermute | solution.py:883
  342.5 24.4 %collective-permute-start.54 = (bf16[416,384]{1,0:T(8,128)(2,1)S(1)}, bf16[416,384]{1,0:T(8,128)(2,1)S(1)}, u32[]{:S(2)}, u32[]{:S(2)}) collective-permute-start(bf16[416,384]{1,0:T(8,128)(2,1)S(1)} %get-tuple-element.258), channel_id=1, source_target_pairs={{0,2},{1,3},{2,0},{3,1},{4,6},{5,7},{6,4},{7,5},{8,10},{9,11},{10,... | collective-permute-start | bytes 958472 | tf_op jit(solution)/shard_map/ppermute | solution.py:883
  347.6 19.3 %collective-permute-start.55 = (bf16[416,384]{1,0:T(8,128)(2,1)S(1)}, bf16[416,384]{1,0:T(8,128)(2,1)S(1)}, u32[]{:S(2)}, u32[]{:S(2)}) collective-permute-start(bf16[416,384]{1,0:T(8,128)(2,1)S(1)} %get-tuple-element.256), channel_id=1, source_target_pairs={{0,3},{1,2},{2,1},{3,0},{4,7},{5,6},{6,5},{7,4},{8,11},{9,10},{10,... | collective-permute-start | bytes 958472 | tf_op jit(solution)/shard_map/ppermute | solution.py:883
  (87 other events, 693.0 us)

commit v7 on v5

--- a/solution.py
+++ b/solution.py
@@ -15,7 +15,7 @@
 TOK = IMG_GRP * SEQP
 BLK = 2 * SEQP
 DUMMY = SEQ
-TILE = 160
+TILE = 128
 f32 = jnp.float32
 bf16 = jnp.bfloat16
 

time: 378 us -> 376 us (level)
  transfers between devices with their start and end apart: 56 -> 56, of which waited for: 28 -> 27; matrix products, arithmetic and copies ran while one was open for 10% -> 10% of each run, Pallas kernels for 15% -> 15%
where the time goes in v7:
time: 376 us; the launch traced here: 375 us
  Pallas kernels  173 us (46%)
  waiting for transfers between devices  80.5 us (21%)
  starting transfers between devices  47.3 us (13%)
  other arithmetic  40.1 us (11%)
  local copies, waits for them, and re-layouts  32.2 us (9%)
    pallas_call x1, Pallas kernels, moe_call(): pl.pallas_call(lambda *refs: moe_kernel(places, *refs), grid_spec=pltpu.P...  109 us
    ppermute x18, waiting for transfers between devices, across_col(): return lax.ppermute(value, 'col', [(i, i ^ step) for i in range(4)])  43.4 us
    unnamed x137, local copies, waits for them, and re-layouts  27.4 us
    ppermute x18, starting transfers between devices, across_col(): return lax.ppermute(value, 'col', [(i, i ^ step) for i in range(4)])  22.6 us
    pallas_call x3, Pallas kernels, table_call(): pl.pallas_call(lambda *refs: table_kernel(n, *refs), grid_spec=pltpu.Pref...  20.1 us
    ppermute x8, waiting for transfers between devices, across_chip(): return lax.ppermute(value, ('row', 'col'), pairs)  16.5 us
    pallas_call x1, Pallas kernels, qkv_back_call(): pl.pallas_call(qkv_back_kernel, grid_spec=pltpu.PrefetchScalarGridSpec(nu...  15.3 us
    ppermute x12, starting transfers between devices, across_dp(): return lax.ppermute(value, 'dp', [(i, i ^ step) for i in range(4)])  13.3 us
  transfers between devices with their start and end apart: 56, of which 27 were waited for; matrix products, arithmetic and copies ran while one was open for 10% of the time, Pallas kernels for 15%

profile of v7, /device:TPU:0, one launch (start us, length us, event | category | flops | bytes accessed | tf_op | source)
XLA Modules:
  0.0 374.9 jit_solution(3860352467042785273)
XLA Ops:
  6.1 2.9 collective-permute-start
  22.5 8.6 %sort.14 = (s32[14592]{0:T(1024)S(1)}, s32[14592]{0:T(1024)}) sort(s32[14592]{0:T(1024)} %pad_add_fusion, s32[14592]{0:T(1024)S(1)} %iota.71), dimensions={0}, to_apply=%region_1.2 | sort | flops 204288 | bytes 233472 | tf_op jit(solution)/shard_map/sort | solution.py:355
  38.2 5.3 %collective-permute-done.7 = bf16[416,384]{1,0:T(8,128)(2,1)S(1)} collective-permute-done((bf16[416,384]{1,0:T(8,128)(2,1)S(1)}, bf16[416,384]{1,0:T(8,128)(2,1)S(1)}, u32[]{:S(2)}, u32[]{:S(2)}) %collective-permute-start.7) | collective-permute-done | bytes 319520 | tf_op jit(solution)/shard_map/ppermute | solution.py:883
  43.5 4.3 %collective-permute-done.8 = bf16[416,384]{1,0:T(8,128)(2,1)S(1)} collective-permute-done((bf16[416,384]{1,0:T(8,128)(2,1)S(1)}, bf16[416,384]{1,0:T(8,128)(2,1)S(1)}, u32[]{:S(2)}, u32[]{:S(2)}) %collective-permute-start.8) | collective-permute-done | bytes 319520 | tf_op jit(solution)/shard_map/ppermute | solution.py:883
  50.7 4.8 %collective-permute-done.2.refs_3_ = bf16[944,384]{1,0:T(8,128)(2,1)S(1)} collective-permute-done((bf16[944,384]{1,0:T(8,128)(2,1)S(1)}, bf16[944,384]{1,0:T(8,128)(2,1)S(1)}, u32[]{:S(2)}, u32[]{:S(2)}) %collective-permute-start.2) | collective-permute-done | bytes 725024 | tf_op jit(solution)/shard_map/ppermute | solution.py:898
  62.9 13.2 %shard_map.293 = (bf16[416,768]{1,0:T(8,128)(2,1)S(1)}, f32[416,768]{1,0:T(8,128)}, bf16[416,768]{1,0:T(8,128)(2,1)S(1)}, bf16[3,416,768]{2,1,0:T(8,128)(2,1)}, ...) custom-call(s32[16]{0:T(128)S(1)} %and_select_fusion.5.picks_ref, ...), custom_call_target="tpu_custom_call" | custom-call | flops 4000000000 | bytes 15000000 | tf_op jit(solution)/shard_map/pallas_call | solution.py:684
  80.2 5.1 %shard_map.294.refs_4_ = bf16[832,16,128]{2,1,0:T(8,128)(2,1)S(1)} custom-call(s32[4]{0:T(128)S(1)} %pad_add_fusion.3.refs_0_, bf16[416,768]{1,0:T(8,128)(2,1)S(1)} %get-tuple-element.122.refs_1_.refs_6_, bf16[416,768]{1,0:T(8,128)(2,1)S(1)} %collective-permute-done.12.refs_2_, bf16[416,768]{1,0:T(8,128)(2,1)S(1)} %pad_maximum_fusion.1.refs_3_.refs_10_, ...), custom_call_target="tpu_custom_call" | custom-call | flops 6000000000 | bytes 6000000 | tf_op jit(solution)/shard_map/pallas_call | solution.py:100
  87.1 6.9 %collective-permute-done.10.refs_1_ = bf16[416,768]{1,0:T(8,128)(2,1)S(1)} collective-permute-done((bf16[416,768]{1,0:T(8,128)(2,1)S(1)}, bf16[416,768]{1,0:T(8,128)(2,1)S(1)}, u32[]{:S(2)}, u32[]{:S(2)}) %collective-permute-start.10) | collective-permute-done | bytes 639008 | tf_op jit(solution)/shard_map/ppermute | solution.py:883
  98.4 9.8 %shard_map.295.refs_5_ = bf16[1664,16,128]{2,1,0:T(8,128)(2,1)S(1)} custom-call(s32[8]{0:T(128)S(1)} %pad_add_fusion.4.refs_0_, bf16[416,768]{1,0:T(8,128)(2,1)S(1)} %collective-permute-done.10.refs_1_, bf16[416,768]{1,0:T(8,128)(2,1)S(1)} %collective-permute-done.11.refs_2_, bf16[416,768]{1,0:T(8,128)(2,1)S(1)} %collective-permute-done.18.refs_3_, ...), custom_call_target="tpu_custom_call" | custom-call | flops 12000000000 | bytes 12000000 | tf_op jit(solution)/shard_map/pallas_call | solution.py:100
  108.2 2.8 copy-done.28
  111.0 2.4 collective-permute-done.14.refs_1_
  116.4 5.1 %shard_map.296.refs_6_ = bf16[832,16,128]{2,1,0:T(8,128)(2,1)S(1)} custom-call(s32[4]{0:T(128)S(1)} %pad_add_fusion.5.refs_0_, bf16[416,768]{1,0:T(8,128)(2,1)S(1)} %collective-permute-done.14.refs_1_, bf16[416,768]{1,0:T(8,128)(2,1)S(1)} %collective-permute-done.22.refs_2_, bf16[416,768]{1,0:T(8,128)(2,1)S(1)} %collective-permute-done.17.refs_3_, ...), custom_call_target="tpu_custom_call" | custom-call | flops 6000000000 | bytes 6000000 | tf_op jit(solution)/shard_map/pallas_call | solution.py:100
  123.3 109.2 %shard_map.297 = (bf16[832,768]{1,0:T(8,128)(2,1)}, bf16[832,768]{1,0:T(8,128)(2,1)}, bf16[832,768]{1,0:T(8,128)(2,1)}, bf16[832,768]{1,0:T(8,128)(2,1)}, bf16[8...) custom-call(s32[14592]{0:T(1024)} %broadcast_and_fusion.refs_0_, ...), custom_call_target="tpu_custom_call" | custom-call | flops 20000000000 | bytes 60000000 | tf_op jit(solution)/shard_map/pallas_call | solution.py:289
  234.0 2.4 collective-permute-done.25
  240.2 5.6 %collective-permute-done.29 = bf16[192,128]{1,0:T(8,128)(2,1)S(1)} collective-permute-done((bf16[192,128]{1,0:T(8,128)(2,1)S(1)}, bf16[192,128]{1,0:T(8,128)(2,1)S(1)}, u32[]{:S(2)}, u32[]{:S(2)}) %collective-permute-start.29) | collective-permute-done | bytes 49184 | tf_op jit(solution)/shard_map/ppermute | solution.py:933
  247.7 2.2 collective-permute-done.27
  251.8 2.7 add_convert_fusion.6
  254.4 4.1 %collective-permute-done.26 = bf16[832,896]{1,0:T(8,128)(2,1)} collective-permute-done((bf16[832,896]{1,0:T(8,128)(2,1)S(1)}, bf16[832,896]{1,0:T(8,128)(2,1)}, u32[]{:S(2)}, u32[]{:S(2)}) %collective-permute-start.26) | collective-permute-done | bytes 1490976 | tf_op jit(solution)/shard_map/ppermute | solution.py:898
  258.5 2.6 add_convert_fusion.3
  262.8 4.1 %collective-permute-start.35 = (bf16[192,128]{1,0:T(8,128)(2,1)S(1)}, bf16[192,128]{1,0:T(8,128)(2,1)S(1)}, u32[]{:S(2)}, u32[]{:S(2)}) collective-permute-start(bf16[192,128]{1,0:T(8,128)(2,1)S(1)} %fusion.9), channel_id=1, source_target_pairs={{0,8},{8,0},{16,24},{24,16},{1,9},{9,1},{17,25},{25,17},{2,10},{10... | collective-permute-start | bytes 147464 | tf_op jit(solution)/shard_map/ppermute | solution.py:933
  269.0 3.8 %collective-permute-done.32.refs_12_ = bf16[416,896]{1,0:T(8,128)(2,1)} collective-permute-done((bf16[416,896]{1,0:T(8,128)(2,1)S(1)}, bf16[416,896]{1,0:T(8,128)(2,1)}, u32[]{:S(2)}, u32[]{:S(2)}) %collective-permute-start.32) | collective-permute-done | bytes 745504 | tf_op jit(solution)/shard_map/ppermute | solution.py:898
  276.3 9.3 %shard_map.298 = (f32[416,768]{1,0:T(8,128)}, bf16[416,768]{1,0:T(8,128)(2,1)}, f32[416,768]{1,0:T(8,128)}, bf16[2560,128]{1,0:T(8,128)(2,1)}, bf16[2,4,96,128]{...) custom-call(s32[16]{0:T(128)} %copy-done.7, s32[2]{0:T(128)} %copy-done.22, bf16[1456,384]{1,0:T(8,128)(2,1)} %copy-done.54, ...), custom_call_target="tpu_custom_call" | custom-call | flops 6000000000 | bytes 15000000 | tf_op jit(solution)/shard_map/pallas_call | solution.py:779
  285.6 15.3 %shard_map.299 = (bf16[416,768]{1,0:T(8,128)(2,1)}, bf16[2,4,288,128]{3,2,1,0:T(8,128)(2,1)}, bf16[2,4,288,128]{3,2,1,0:T(8,128)(2,1)}) custom-call(s32[16]{0:T(128)} %copy-done.7, s32[2]{0:T(128)} %copy-done.22, bf16[944,384]{1,0:T(8,128)(2,1)} %maximum_maximum_fusion.2.refs_0_, bf16[944,384]{1,0:T(8,128)(2,1)} %copy-done, bf16[944,384]{1,0:T(8,128)(2,1)} %copy-done.1, ...), custom_call_target="tpu_custom_call" | custom-call | flops 8999999488 | bytes 15000000 | tf_op jit(solution)/shard_map/pallas_call | solution.py:847
  308.4 3.1 collective-permute-done.39
  317.8 7.2 %collective-permute-done.42 = bf16[1088,128]{1,0:T(8,128)(2,1)S(1)} collective-permute-done((bf16[1088,128]{1,0:T(8,128)(2,1)}, bf16[1088,128]{1,0:T(8,128)(2,1)S(1)}, u32[]{:S(2)}, u32[]{:S(2)}) %collective-permute-start.42) | collective-permute-done | bytes 278560 | tf_op jit(solution)/shard_map/ppermute | solution.py:883
  324.9 5.2 %collective-permute-done.41 = bf16[1088,128]{1,0:T(8,128)(2,1)} collective-permute-done((bf16[1088,128]{1,0:T(8,128)(2,1)}, bf16[1088,128]{1,0:T(8,128)(2,1)}, u32[]{:S(2)}, u32[]{:S(2)}) %collective-permute-start.41) | collective-permute-done | bytes 278560 | tf_op jit(solution)/shard_map/ppermute | solution.py:883
  332.0 4.3 %collective-permute-start.43 = (bf16[272,128]{1,0:T(8,128)(2,1)S(1)}, bf16[272,128]{1,0:T(8,128)(2,1)S(1)}, u32[]{:S(2)}, u32[]{:S(2)}) collective-permute-start(bf16[272,128]{1,0:T(8,128)(2,1)S(1)} %get-tuple-element.291), channel_id=1, source_target_pairs={{0,8},{8,0},{16,24},{24,16},{1,9},{9,1},{17,25},{25,17},{2,10},{10... | collective-permute-start | bytes 208904 | tf_op jit(solution)/shard_map/ppermute | solution.py:933
  343.5 2.0 collective-permute-start.47
  352.3 6.9 %collective-permute-done.49.one = bf16[704,128]{1,0:T(8,128)(2,1)S(1)} collective-permute-done((bf16[704,128]{1,0:T(8,128)(2,1)S(1)}, bf16[704,128]{1,0:T(8,128)(2,1)S(1)}, u32[]{:S(2)}, u32[]{:S(2)}) %collective-permute-start.49) | collective-permute-done | bytes 180256 | tf_op jit(solution)/shard_map/ppermute | solution.py:883
  359.2 2.2 collective-permute-start.51
  361.5 4.1 %collective-permute-done.51.three = bf16[704,128]{1,0:T(8,128)(2,1)S(1)} collective-permute-done((bf16[704,128]{1,0:T(8,128)(2,1)S(1)}, bf16[704,128]{1,0:T(8,128)(2,1)S(1)}, u32[]{:S(2)}, u32[]{:S(2)}) %collective-permute-start.51) | collective-permute-done | bytes 180256 | tf_op jit(solution)/shard_map/ppermute | solution.py:883
  370.9 2.4 shard_map.301
  (327 shorter events, 102.9 us)
Async XLA Ops:
  6.1 25.6 %collective-permute-start = (bf16[944,384]{1,0:T(8,128)(2,1)}, bf16[944,384]{1,0:T(8,128)(2,1)S(1)}, u32[]{:S(2)}, u32[]{:S(2)}) collective-permute-start(bf16[944,384]{1,0:T(8,128)(2,1)} %maximum_maximum_fusion.2.refs_0_), channel_id=1, source_target_pairs={{0,1},{1,0},{2,3},{3,2},{4,5},{5,4},{6,7},{7,6},{8,9},{9,8},{10,11... | collective-permute-start | bytes 2174984 | tf_op jit(solution)/shard_map/ppermute | solution.py:883
  9.1 22.7 %collective-permute-start.1 = (bf16[944,384]{1,0:T(8,128)(2,1)}, bf16[944,384]{1,0:T(8,128)(2,1)S(1)}, u32[]{:S(2)}, u32[]{:S(2)}) collective-permute-start(bf16[944,384]{1,0:T(8,128)(2,1)} %maximum_maximum_fusion.2.refs_0_), channel_id=1, source_target_pairs={{0,2},{1,3},{2,0},{3,1},{4,6},{5,7},{6,4},{7,5},{8,10},{9,11},{10,... | collective-permute-start | bytes 2174984 | tf_op jit(solution)/shard_map/ppermute | solution.py:883
  32.1 11.4 %collective-permute-start.7 = (bf16[416,384]{1,0:T(8,128)(2,1)S(1)}, bf16[416,384]{1,0:T(8,128)(2,1)S(1)}, u32[]{:S(2)}, u32[]{:S(2)}) collective-permute-start(bf16[416,384]{1,0:T(8,128)(2,1)S(1)} %copy-done.18), channel_id=1, source_target_pairs={{0,3},{1,2},{2,1},{3,0},{4,7},{5,6},{6,5},{7,4},{8,11},{9,10},{10,... | collective-permute-start | bytes 958472 | tf_op jit(solution)/shard_map/ppermute | solution.py:883
  32.2 15.6 %collective-permute-start.8 = (bf16[416,384]{1,0:T(8,128)(2,1)S(1)}, bf16[416,384]{1,0:T(8,128)(2,1)S(1)}, u32[]{:S(2)}, u32[]{:S(2)}) collective-permute-start(bf16[416,384]{1,0:T(8,128)(2,1)S(1)} %copy-done.16), channel_id=1, source_target_pairs={{0,2},{1,3},{2,0},{3,1},{4,6},{5,7},{6,4},{7,5},{8,10},{9,11},{10,... | collective-permute-start | bytes 958472 | tf_op jit(solution)/shard_map/ppermute | solution.py:883
  34.1 15.3 %collective-permute-start.9 = (bf16[416,384]{1,0:T(8,128)(2,1)S(1)}, bf16[416,384]{1,0:T(8,128)(2,1)S(1)}, u32[]{:S(2)}, u32[]{:S(2)}) collective-permute-start(bf16[416,384]{1,0:T(8,128)(2,1)S(1)} %copy-done.14), channel_id=1, source_target_pairs={{0,1},{1,0},{2,3},{3,2},{4,5},{5,4},{6,7},{7,6},{8,9},{9,8},{10,11... | collective-permute-start | bytes 958472 | tf_op jit(solution)/shard_map/ppermute | solution.py:883
  37.7 17.9 %collective-permute-start.2 = (bf16[944,384]{1,0:T(8,128)(2,1)S(1)}, bf16[944,384]{1,0:T(8,128)(2,1)S(1)}, u32[]{:S(2)}, u32[]{:S(2)}) collective-permute-start(bf16[944,384]{1,0:T(8,128)(2,1)S(1)} %broadcast_select_fusion), channel_id=1, source_target_pairs={{0,2},{1,3},{2,0},{3,1},{4,5},{5,4},{6,7},{7,6},{8,10},{9,11},{10,... | collective-permute-start | bytes 2174984 | tf_op jit(solution)/shard_map/ppermute | solution.py:898
  38.2 20.6 %collective-permute-start.4 = (bf16[944,384]{1,0:T(8,128)(2,1)S(1)}, bf16[944,384]{1,0:T(8,128)(2,1)S(1)}, u32[]{:S(2)}, u32[]{:S(2)}) collective-permute-start(bf16[944,384]{1,0:T(8,128)(2,1)S(1)} %collective-permute-done.refs_1_), channel_id=1, source_target_pairs={{0,4},{4,0},{1,5},{5,1},{2,6},{6,2},{3,7},{7,3},{8,12},{12,8},{9,1... | collective-permute-start | bytes 2174984 | tf_op jit(solution)/shard_map/ppermute | solution.py:879
  43.5 16.6 %collective-permute-start.5 = (bf16[944,384]{1,0:T(8,128)(2,1)S(1)}, bf16[944,384]{1,0:T(8,128)(2,1)S(1)}, u32[]{:S(2)}, u32[]{:S(2)}) collective-permute-start(bf16[944,384]{1,0:T(8,128)(2,1)S(1)} %collective-permute-done.1.refs_2_), channel_id=1, source_target_pairs={{0,4},{4,0},{1,5},{5,1},{2,6},{6,2},{3,7},{7,3},{8,12},{12,8},{9,1... | collective-permute-start | bytes 2174984 | tf_op jit(solution)/shard_map/ppermute | solution.py:879
  57.2 21.7 %collective-permute-start.13 = (bf16[416,768]{1,0:T(8,128)(2,1)S(1)}, bf16[416,768]{1,0:T(8,128)(2,1)S(1)}, u32[]{:S(2)}, u32[]{:S(2)}) collective-permute-start(bf16[416,768]{1,0:T(8,128)(2,1)S(1)} %pad_maximum_fusion.1.refs_3_.refs_10_), channel_id=1, source_target_pairs={{0,4},{4,0},{1,5},{5,1},{2,6},{6,2},{3,7},{7,3},{8,12},{12,8},{9,1... | collective-permute-start | bytes 1916936 | tf_op jit(solution)/shard_map/ppermute | solution.py:879
  58.8 20.9 %collective-permute-start.15 = (bf16[416,768]{1,0:T(8,128)(2,1)S(1)}, bf16[416,768]{1,0:T(8,128)(2,1)S(1)}, u32[]{:S(2)}, u32[]{:S(2)}) collective-permute-start(bf16[416,768]{1,0:T(8,128)(2,1)S(1)} %pad_maximum_fusion.1.refs_3_.refs_10_), channel_id=1, source_target_pairs={{0,1},{1,0},{2,3},{3,2},{4,5},{5,4},{6,7},{7,6},{8,9},{9,8},{10,11... | collective-permute-start | bytes 1916936 | tf_op jit(solution)/shard_map/ppermute | solution.py:883
  60.1 19.5 %collective-permute-start.16 = (bf16[416,768]{1,0:T(8,128)(2,1)S(1)}, bf16[416,768]{1,0:T(8,128)(2,1)S(1)}, u32[]{:S(2)}, u32[]{:S(2)}) collective-permute-start(bf16[416,768]{1,0:T(8,128)(2,1)S(1)} %pad_maximum_fusion.1.refs_3_.refs_10_), channel_id=1, source_target_pairs={{0,2},{1,3},{2,0},{3,1},{4,6},{5,7},{6,4},{7,5},{8,10},{9,11},{10,... | collective-permute-start | bytes 1916936 | tf_op jit(solution)/shard_map/ppermute | solution.py:883
  77.2 16.8 %collective-permute-start.10 = (bf16[416,768]{1,0:T(8,128)(2,1)S(1)}, bf16[416,768]{1,0:T(8,128)(2,1)S(1)}, u32[]{:S(2)}, u32[]{:S(2)}) collective-permute-start(bf16[416,768]{1,0:T(8,128)(2,1)S(1)} %get-tuple-element.122.refs_1_.refs_6_), channel_id=1, source_target_pairs={{0,1},{1,0},{2,3},{3,2},{4,5},{5,4},{6,7},{7,6},{8,9},{9,8},{10,11... | collective-permute-start | bytes 1916936 | tf_op jit(solution)/shard_map/ppermute | solution.py:883
  78.9 16.5 %collective-permute-start.11 = (bf16[416,768]{1,0:T(8,128)(2,1)S(1)}, bf16[416,768]{1,0:T(8,128)(2,1)S(1)}, u32[]{:S(2)}, u32[]{:S(2)}) collective-permute-start(bf16[416,768]{1,0:T(8,128)(2,1)S(1)} %get-tuple-element.122.refs_1_.refs_6_), channel_id=1, source_target_pairs={{0,2},{1,3},{2,0},{3,1},{4,6},{5,7},{6,4},{7,5},{8,10},{9,11},{10,... | collective-permute-start | bytes 1916936 | tf_op jit(solution)/shard_map/ppermute | solution.py:883
  79.6 17.2 %collective-permute-start.20 = (bf16[416,768]{1,0:T(8,128)(2,1)S(1)}, bf16[416,768]{1,0:T(8,128)(2,1)S(1)}, u32[]{:S(2)}, u32[]{:S(2)}) collective-permute-start(bf16[416,768]{1,0:T(8,128)(2,1)S(1)} %collective-permute-done.15.refs_5_), channel_id=1, source_target_pairs={{0,4},{4,0},{1,5},{5,1},{2,6},{6,2},{3,7},{7,3},{8,12},{12,8},{9,1... | collective-permute-start | bytes 1916936 | tf_op jit(solution)/shard_map/ppermute | solution.py:879
  79.7 18.7 %collective-permute-start.21 = (bf16[416,768]{1,0:T(8,128)(2,1)S(1)}, bf16[416,768]{1,0:T(8,128)(2,1)S(1)}, u32[]{:S(2)}, u32[]{:S(2)}) collective-permute-start(bf16[416,768]{1,0:T(8,128)(2,1)S(1)} %collective-permute-done.16.refs_6_), channel_id=1, source_target_pairs={{0,4},{4,0},{1,5},{5,1},{2,6},{6,2},{3,7},{7,3},{8,12},{12,8},{9,1... | collective-permute-start | bytes 1916936 | tf_op jit(solution)/shard_map/ppermute | solution.py:879
  96.1 14.9 %collective-permute-start.17 = (bf16[416,768]{1,0:T(8,128)(2,1)S(1)}, bf16[416,768]{1,0:T(8,128)(2,1)S(1)}, u32[]{:S(2)}, u32[]{:S(2)}) collective-permute-start(bf16[416,768]{1,0:T(8,128)(2,1)S(1)} %broadcast_select_fusion.1), channel_id=1, source_target_pairs={{0,2},{1,3},{2,0},{3,1},{4,5},{5,4},{6,7},{7,6},{8,10},{9,11},{10,... | collective-permute-start | bytes 1916936 | tf_op jit(solution)/shard_map/ppermute | solution.py:898
  96.9 16.5 %collective-permute-start.14 = (bf16[416,768]{1,0:T(8,128)(2,1)S(1)}, bf16[416,768]{1,0:T(8,128)(2,1)S(1)}, u32[]{:S(2)}, u32[]{:S(2)}) collective-permute-start(bf16[416,768]{1,0:T(8,128)(2,1)S(1)} %broadcast_select_fusion.2), channel_id=1, source_target_pairs={{0,2},{1,3},{2,0},{3,1},{4,5},{5,4},{6,7},{7,6},{8,10},{9,11},{10,... | collective-permute-start | bytes 1916936 | tf_op jit(solution)/shard_map/ppermute | solution.py:898
  238.3 11.7 %collective-permute-start.30 = (bf16[832,768]{1,0:T(8,128)(2,1)}, bf16[832,768]{1,0:T(8,128)(2,1)}, u32[]{:S(2)}, u32[]{:S(2)}) collective-permute-start(bf16[832,768]{1,0:T(8,128)(2,1)} %get-tuple-element.150), channel_id=1, source_target_pairs={{0,4},{4,0},{1,5},{5,1},{2,6},{6,2},{3,7},{7,3},{8,12},{12,8},{9,1... | collective-permute-start | bytes 3833864 | tf_op jit(solution)/shard_map/ppermute | solution.py:879
  238.5 13.2 %collective-permute-start.31 = (bf16[832,768]{1,0:T(8,128)(2,1)}, bf16[832,768]{1,0:T(8,128)(2,1)}, u32[]{:S(2)}, u32[]{:S(2)}) collective-permute-start(bf16[832,768]{1,0:T(8,128)(2,1)} %get-tuple-element.152), channel_id=1, source_target_pairs={{0,4},{4,0},{1,5},{5,1},{2,6},{6,2},{3,7},{7,3},{8,12},{12,8},{9,1... | collective-permute-start | bytes 3833864 | tf_op jit(solution)/shard_map/ppermute | solution.py:879
  238.9 19.6 %collective-permute-start.26 = (bf16[832,896]{1,0:T(8,128)(2,1)S(1)}, bf16[832,896]{1,0:T(8,128)(2,1)}, u32[]{:S(2)}, u32[]{:S(2)}) collective-permute-start(bf16[832,896]{1,0:T(8,128)(2,1)S(1)} %add_convert_fusion), channel_id=1, source_target_pairs={{0,1},{1,0},{2,3},{3,2},{4,6},{5,7},{6,4},{7,5},{8,9},{9,8},{10,11... | collective-permute-start | bytes 4472840 | tf_op jit(solution)/shard_map/ppermute | solution.py:898
  261.1 11.7 %collective-permute-start.32 = (bf16[416,896]{1,0:T(8,128)(2,1)S(1)}, bf16[416,896]{1,0:T(8,128)(2,1)}, u32[]{:S(2)}, u32[]{:S(2)}) collective-permute-start(bf16[416,896]{1,0:T(8,128)(2,1)S(1)} %get-tuple-element.245), channel_id=1, source_target_pairs={{0,2},{1,3},{2,0},{3,1},{4,5},{5,4},{6,7},{7,6},{8,10},{9,11},{10,... | collective-permute-start | bytes 2236424 | tf_op jit(solution)/shard_map/ppermute | solution.py:898
  272.8 29.4 %collective-permute-start.36 = (bf16[416,768]{1,0:T(8,128)(2,1)S(1)}, bf16[416,768]{1,0:T(8,128)(2,1)S(1)}, u32[]{:S(2)}, u32[]{:S(2)}) collective-permute-start(bf16[416,768]{1,0:T(8,128)(2,1)S(1)} %get-tuple-element.168), channel_id=1, source_target_pairs={{0,2},{1,3},{2,0},{3,1},{4,5},{5,4},{6,7},{7,6},{8,10},{9,11},{10,... | collective-permute-start | bytes 1916936 | tf_op jit(solution)/shard_map/ppermute | solution.py:898
  274.2 28.0 %collective-permute-start.37 = (bf16[416,768]{1,0:T(8,128)(2,1)}, bf16[416,768]{1,0:T(8,128)(2,1)S(1)}, u32[]{:S(2)}, u32[]{:S(2)}) collective-permute-start(bf16[416,768]{1,0:T(8,128)(2,1)} %get-tuple-element.169), channel_id=1, source_target_pairs={{0,1},{1,0},{2,3},{3,2},{4,6},{5,7},{6,4},{7,5},{8,9},{9,8},{10,11... | collective-permute-start | bytes 1916936 | tf_op jit(solution)/shard_map/ppermute | solution.py:898
  275.6 26.6 %collective-permute-start.38 = (bf16[416,768]{1,0:T(8,128)(2,1)}, bf16[416,768]{1,0:T(8,128)(2,1)S(1)}, u32[]{:S(2)}, u32[]{:S(2)}) collective-permute-start(bf16[416,768]{1,0:T(8,128)(2,1)} %get-tuple-element.170), channel_id=1, source_target_pairs={{0,3},{1,2},{2,1},{3,0},{4,7},{5,6},{6,5},{7,4},{8,11},{9,10},{10,... | collective-permute-start | bytes 1916936 | tf_op jit(solution)/shard_map/ppermute | solution.py:898
  314.3 10.7 %collective-permute-start.42 = (bf16[1088,128]{1,0:T(8,128)(2,1)}, bf16[1088,128]{1,0:T(8,128)(2,1)S(1)}, u32[]{:S(2)}, u32[]{:S(2)}) collective-permute-start(bf16[1088,128]{1,0:T(8,128)(2,1)} %get-tuple-element.263), channel_id=1, source_target_pairs={{0,3},{1,2},{2,1},{3,0},{4,7},{5,6},{6,5},{7,4},{8,11},{9,10},{10,... | collective-permute-start | bytes 835592 | tf_op jit(solution)/shard_map/ppermute | solution.py:883
  316.0 14.1 %collective-permute-start.41 = (bf16[1088,128]{1,0:T(8,128)(2,1)}, bf16[1088,128]{1,0:T(8,128)(2,1)}, u32[]{:S(2)}, u32[]{:S(2)}) collective-permute-start(bf16[1088,128]{1,0:T(8,128)(2,1)} %get-tuple-element.264), channel_id=1, source_target_pairs={{0,2},{1,3},{2,0},{3,1},{4,6},{5,7},{6,4},{7,5},{8,10},{9,11},{10,... | collective-permute-start | bytes 835592 | tf_op jit(solution)/shard_map/ppermute | solution.py:883
  316.4 14.1 %collective-permute-start.40 = (bf16[1088,128]{1,0:T(8,128)(2,1)}, bf16[1088,128]{1,0:T(8,128)(2,1)}, u32[]{:S(2)}, u32[]{:S(2)}) collective-permute-start(bf16[1088,128]{1,0:T(8,128)(2,1)} %get-tuple-element.262), channel_id=1, source_target_pairs={{0,1},{1,0},{2,3},{3,2},{4,5},{5,4},{6,7},{7,6},{8,9},{9,8},{10,11... | collective-permute-start | bytes 835592 | tf_op jit(solution)/shard_map/ppermute | solution.py:883
  331.8 10.1 %collective-permute-start.45 = (bf16[272,128]{1,0:T(8,128)(2,1)S(1)}, bf16[272,128]{1,0:T(8,128)(2,1)S(1)}, u32[]{:S(2)}, u32[]{:S(2)}) collective-permute-start(bf16[272,128]{1,0:T(8,128)(2,1)S(1)} %get-tuple-element.292), channel_id=1, source_target_pairs={{0,24},{8,16},{16,8},{24,0},{1,25},{9,17},{17,9},{25,1},{2,26},{10... | collective-permute-start | bytes 208904 | tf_op jit(solution)/shard_map/ppermute | solution.py:933
  339.8 25.9 %collective-permute-start.53 = (bf16[416,384]{1,0:T(8,128)(2,1)S(1)}, bf16[416,384]{1,0:T(8,128)(2,1)S(1)}, u32[]{:S(2)}, u32[]{:S(2)}) collective-permute-start(bf16[416,384]{1,0:T(8,128)(2,1)S(1)} %get-tuple-element.257), channel_id=1, source_target_pairs={{0,1},{1,0},{2,3},{3,2},{4,5},{5,4},{6,7},{7,6},{8,9},{9,8},{10,11... | collective-permute-start | bytes 958472 | tf_op jit(solution)/shard_map/ppermute | solution.py:883
  340.5 25.2 %collective-permute-start.54 = (bf16[416,384]{1,0:T(8,128)(2,1)S(1)}, bf16[416,384]{1,0:T(8,128)(2,1)S(1)}, u32[]{:S(2)}, u32[]{:S(2)}) collective-permute-start(bf16[416,384]{1,0:T(8,128)(2,1)S(1)} %get-tuple-element.256), channel_id=1, source_target_pairs={{0,2},{1,3},{2,0},{3,1},{4,6},{5,7},{6,4},{7,5},{8,10},{9,11},{10,... | collective-permute-start | bytes 958472 | tf_op jit(solution)/shard_map/ppermute | solution.py:883
  347.4 18.4 %collective-permute-start.55 = (bf16[416,384]{1,0:T(8,128)(2,1)S(1)}, bf16[416,384]{1,0:T(8,128)(2,1)S(1)}, u32[]{:S(2)}, u32[]{:S(2)}) collective-permute-start(bf16[416,384]{1,0:T(8,128)(2,1)S(1)} %get-tuple-element.254), channel_id=1, source_target_pairs={{0,3},{1,2},{2,1},{3,0},{4,7},{5,6},{6,5},{7,4},{8,11},{9,10},{10,... | collective-permute-start | bytes 958472 | tf_op jit(solution)/shard_map/ppermute | solution.py:883
  350.9 10.6 %collective-permute-start.50 = (bf16[704,128]{1,0:T(8,128)(2,1)S(1)}, bf16[704,128]{1,0:T(8,128)(2,1)S(1)}, u32[]{:S(2)}, u32[]{:S(2)}) collective-permute-start(bf16[704,128]{1,0:T(8,128)(2,1)S(1)} %pad_maximum_fusion.13), channel_id=1, source_target_pairs={{0,2},{1,3},{2,0},{3,1},{4,6},{5,7},{6,4},{7,5},{8,10},{9,11},{10,... | collective-permute-start | bytes 540680 | tf_op jit(solution)/shard_map/ppermute | solution.py:883
  (83 other events, 634.1 us)
